TPU v7x, 256 devices: a whole 4x4x8 slice. The times are simulated.
256 devices in a mesh: dp: 4 (over x_lo, core), cp: 64 (over z, y, x_hi).
Axes of the slice: x: 4 (x_hi: 2, x_lo: 2; x = x_hi * 2 + x_lo), y: 4, z: 8, core: 2. Of those that a mesh axis runs over, the one named last changes fastest.
Arguments:
- q_raw: bfloat16 [32768, 4096], P(('dp', 'cp')), may hold values from -60 to 60
- k_raw: bfloat16 [32768, 512], P(('dp', 'cp')), may hold values from -60 to 60
- values: bfloat16 [32768, 512], P(('dp', 'cp')), may hold values from -6 to 6
- loss_grad: bfloat16 [32768, 4096], P(('dp', 'cp')), may hold values from -6 to 6
- send_order: int32 [256, 128], P(('dp', 'cp')), may hold values from 0 to 127, each once within a row
- doc_blocks: int32 [4, 64], P('dp', 'cp'), may hold values from 0 to 13, never falling along the last dimension, each value on 1 to 5 neighbouring positions
- gain_q: float32 [128], replicated, may hold values from 0.6 to 4.6
- gain_k: float32 [128], replicated, may hold values from 0.6 to 4.6
Outputs:
- attn_out: bfloat16 [32768, 4096], P(('dp', 'cp'))
- dq_raw: bfloat16 [32768, 4096], P(('dp', 'cp'))
- dk_raw: bfloat16 [32768, 512], P(('dp', 'cp'))
- dv_out: bfloat16 [32768, 512], P(('dp', 'cp'))
- dgain_q: float32 [128], replicated
- dgain_k: float32 [128], replicated
Inputs may be any that keep to these rules, and one draw needn't show every extreme that they name: `send_order`: each row is a permutation of 0 to 127. `doc_blocks`: within each row ids never fall, every id 0 to 13 occurs, each document covers 1 to 5 consecutive blocks, and some document covers exactly 5.
All inputs are finite; a program needn't handle non-finite values.
Results may differ from a plain program's by a relative error of at most 0.033.
The roundings to bfloat16 on the way count: a program that leaves them out, or rounds other values in their place, can miss the bound.
Values may be sent and summed in bfloat16 or wider, within the bound.
No kernel may reach another device: no remote copies, remote signals or barrier semaphores. Data moves between devices by JAX's collectives and lax.ppermute only.
A program may use at most 128 MiB of HBM per device.

v0:
```python
import math

import jax
import jax.numpy as jnp
import numpy as np
from jax import lax
from jax.experimental import pallas as pl
from jax.experimental.pallas import tpu as pltpu
from jax.sharding import PartitionSpec as P

REACH = 4
EPSILON = 1e-06
THETA = 1000000.0
NEGATIVE = -1e30
TOK = 128
DIM = 128
KV = 4
GROUP = 8
N_DP = 4
N_CP = 64
ROWS = TOK // N_DP
KEYS = (REACH + 1) * TOK
ID_ROWS = 8
TILE = 256
PAIR = 2 * DIM
WIDE = 2 * GROUP * DIM
INV_ROOT = 1.0 / math.sqrt(DIM)
LOG2E = 1.4426950408889634
BF = jnp.bfloat16
F32 = jnp.float32
VMEM = pl.BlockSpec(memory_space=pltpu.VMEM)
SMEM = pl.BlockSpec(memory_space=pltpu.SMEM)
PARAMS = pltpu.CompilerParams(vmem_limit_bytes=48 * 1024 * 1024)


def tables():
    half = DIM // 2
    frequency = (THETA ** (-(np.arange(half) * 2.0 / DIM))).astype(np.float32)
    angles = np.arange(KEYS, dtype=np.float32)[:, None] * frequency[None, :]
    cosine = np.cos(angles.astype(np.float64)).astype(np.float32)
    sine = np.sin(angles.astype(np.float64)).astype(np.float32)
    return (
        np.concatenate([cosine, cosine], axis=1),
        np.concatenate([-sine, sine], axis=1),
    )


def dot(left, right, left_dim, right_dim):
    return lax.dot_general(
        left, right, (((left_dim,), (right_dim,)), ((), ())), preferred_element_type=F32
    )


def picker(order_ref):
    rows = lax.broadcasted_iota(jnp.int32, (TOK, TOK), 0)
    return jnp.where(rows == order_ref[...], 1.0, 0.0).astype(BF)


def slot_rows(slot):
    place = lax.axis_index("dp") ^ slot
    return pl.ds(pl.multiple_of(place * ROWS, ROWS), ROWS)


def kv_pick(order_ref, k_ref, v_ref, *rest):
    outs, rows_ref = rest[:N_DP], rest[N_DP]
    chosen = picker(order_ref)
    keys = dot(chosen, k_ref[...], 0, 0).astype(BF)
    vals = dot(chosen, v_ref[...], 0, 0).astype(BF)
    for head in range(KV):
        rows_ref[:, head * PAIR : head * PAIR + DIM] = keys[:, head * DIM : (head + 1) * DIM]
        rows_ref[:, head * PAIR + DIM : (head + 1) * PAIR] = vals[:, head * DIM : (head + 1) * DIM]
    for slot in range(N_DP):
        outs[slot][...] = rows_ref[slot_rows(slot), :]


def qg_pick(order_ref, q_ref, g_ref, *rest):
    outs, rows_ref = rest[:N_DP], rest[N_DP]
    chosen = picker(order_ref)
    half = GROUP * DIM
    rows_ref[:, :half] = dot(chosen, q_ref[...], 0, 0).astype(BF)
    rows_ref[:, half:] = dot(chosen, g_ref[...], 0, 0).astype(BF)
    for slot in range(N_DP):
        outs[slot][...] = rows_ref[slot_rows(slot), :]


def kv_join(doc_ref, *rest):
    slots, out_ref = rest[:N_DP], rest[N_DP]
    for slot in range(N_DP):
        out_ref[slot_rows(slot), :] = slots[slot][...]
    width = out_ref.shape[1]
    out_ref[TOK:, :] = jnp.full((ID_ROWS, width), doc_ref[0, 0], jnp.int32).astype(F32).astype(BF)


def same_docs(doc_ref, shards):
    own = doc_ref[0, 0].astype(F32)
    place = lax.axis_index("cp")
    flags = []
    for back in range(1, REACH + 1):
        near = jnp.max(shards[back][TOK : TOK + ID_ROWS, 0:DIM].astype(F32))
        flags.append(jnp.where((near == own) & (place >= back), 1, 0).astype(jnp.int32))
    return flags


def table_rows(block):
    return pl.ds(pl.multiple_of(block * TOK, TOK), TOK)


def turn(vectors, cosine, sine):
    return vectors * cosine + pltpu.roll(vectors, DIM // 2, 1) * sine


def turn_back(vectors, cosine, sine):
    return vectors * cosine - pltpu.roll(vectors, DIM // 2, 1) * sine


def unit_of(raw):
    inv_norm = lax.rsqrt(jnp.mean(raw * raw, axis=-1, keepdims=True) + EPSILON)
    return raw * inv_norm, inv_norm


def attend(doc_ref, *rest):
    slots = rest[:N_DP]
    shards = rest[N_DP : N_DP + REACH + 1]
    cos_ref, sin_ref, gq_ref, gk_ref = rest[N_DP + REACH + 1 : N_DP + REACH + 5]
    outs = rest[N_DP + REACH + 5 :]
    out_ref, dq_ref = outs[:2]
    own_ref = outs[2]
    part_refs = outs[3 : 3 + REACH]
    gain_ref = outs[3 + REACH]
    place_ref = outs[4 + REACH]
    rows_ref, bias_ref = outs[5 + REACH :]
    step = pl.program_id(0)
    flags = same_docs(doc_ref, shards)
    block = flags[0] + flags[1] + flags[2] + flags[3]
    place_ref[0, 0] = block

    @pl.when(step == 0)
    def start():
        gain_ref[...] = jnp.zeros_like(gain_ref)
        for back in range(REACH, 0, -1):
            first = (REACH - back) * TOK
            level = jnp.where(flags[back - 1] > 0, 0.0, NEGATIVE)
            bias_ref[first : first + TOK, :] = jnp.full((TOK, TILE), level, F32)
        key = lax.broadcasted_iota(jnp.int32, (TOK, TILE), 0)
        query = lax.broadcasted_iota(jnp.int32, (TOK, TILE), 1) & (TOK - 1)
        bias_ref[REACH * TOK :, :] = jnp.where(key <= query, 0.0, NEGATIVE)

    for slot in range(N_DP):
        rows_ref[slot_rows(slot), :] = slots[slot][...]
    gain_q = gq_ref[...]
    gain_k = gk_ref[...]
    key_cos, key_sin, key_unit, key_rot, key_val = [], [], [], [], []
    for back in range(REACH, -1, -1):
        where = table_rows(jnp.maximum(block - back, 0))
        cosine, sine = cos_ref[where, :], sin_ref[where, :]
        unit, _ = unit_of(shards[back][:TOK, :DIM].astype(F32))
        key_cos.append(cosine)
        key_sin.append(sine)
        key_unit.append(unit)
        key_rot.append(turn(unit * gain_k, cosine, sine))
        key_val.append(shards[back][:TOK, DIM:])
    rot_f = jnp.concatenate(key_rot, axis=0).astype(BF)
    val_b = jnp.concatenate(key_val, axis=0)
    rot_t = rot_f.T
    val_t = val_b.T
    bias = bias_ref[...]
    own_rows = table_rows(block)
    cosine = jnp.concatenate([cos_ref[own_rows, :]] * (TILE // TOK), axis=0)
    sine = jnp.concatenate([sin_ref[own_rows, :]] * (TILE // TOK), axis=0)
    dk_total = jnp.zeros((KEYS, DIM), F32)
    dv_total = jnp.zeros((KEYS, DIM), F32)
    gq_total = jnp.zeros((8, DIM), F32)
    heads = TILE // TOK
    for first in range(0, GROUP, heads):
        places = [(first + j) * DIM for j in range(heads)]
        raw = jnp.concatenate([rows_ref[:, at : at + DIM] for at in places], axis=0)
        grad = jnp.concatenate(
            [rows_ref[:, GROUP * DIM + at : GROUP * DIM + at + DIM] for at in places], axis=0
        )
        unit, inv_norm = unit_of(raw.astype(F32))
        query = turn(unit * gain_q, cosine, sine).astype(BF)
        scores = dot(rot_f, query, 1, 1) * (INV_ROOT * LOG2E) + bias
        top = jnp.max(scores, axis=0, keepdims=True)
        weights = jnp.exp2(scores - top)
        total = jnp.sum(weights, axis=0, keepdims=True)
        inverse = 1.0 / total
        out_t = (dot(val_t, weights.astype(BF), 1, 0) / total).astype(BF).astype(F32)
        out = out_t.T.astype(BF)
        grad_t = grad.astype(F32).T
        delta = jnp.sum(grad_t * out_t, axis=0, keepdims=True)
        probs = weights * inverse
        dscore = (probs * (dot(val_b, grad, 1, 1) - delta)).astype(BF)
        dq_rot = dot(rot_t, dscore, 1, 0).T * INV_ROOT
        dk_total = dk_total + dot(dscore, query, 1, 0)
        dv_total = dv_total + dot(probs.astype(BF), grad, 1, 0)
        dqn = turn_back(dq_rot, cosine, sine)
        scaled = dqn * gain_q
        inner = jnp.mean(scaled * unit, axis=-1, keepdims=True)
        dq = (inv_norm * (scaled - unit * inner)).astype(BF)
        gq_total = gq_total + jnp.sum((dqn * unit).reshape(TILE // 8, 8, DIM), axis=0)
        for j, at in enumerate(places):
            out_ref[:, at : at + DIM] = out[j * TOK : (j + 1) * TOK]
            dq_ref[:, at : at + DIM] = dq[j * TOK : (j + 1) * TOK]
    dk_total = dk_total * INV_ROOT
    gk_total = jnp.zeros((8, DIM), F32)
    for at, back in enumerate(range(REACH, -1, -1)):
        dk_part = dk_total[at * TOK : (at + 1) * TOK]
        dv_part = dv_total[at * TOK : (at + 1) * TOK]
        dkn = turn_back(dk_part, key_cos[at], key_sin[at])
        gk_total = gk_total + jnp.sum((dkn * key_unit[at]).reshape(TOK // 8, 8, DIM), axis=0)
        target = own_ref if back == 0 else part_refs[back - 1]
        target[:, :DIM] = dk_part.astype(target.dtype)
        target[:, DIM:] = dv_part.astype(target.dtype)
    gain_ref[:, :DIM] += gq_total
    gain_ref[:, DIM:] += gk_total


def finish(place_ref, own_ref, *rest):
    parts = rest[:REACH]
    kv_ref, cos_ref, sin_ref, gk_ref, dk_ref, dv_ref = rest[REACH:]
    where = table_rows(place_ref[0, 0])
    cosine, sine = cos_ref[where, :], sin_ref[where, :]
    gain_k = gk_ref[...]
    for head in range(KV):
        left = head * PAIR
        both = own_ref[:, left : left + PAIR]
        for part in parts:
            both = both + part[:, left : left + PAIR].astype(F32)
        unit, inv_norm = unit_of(kv_ref[:TOK, left : left + DIM].astype(F32))
        scaled = turn_back(both[:, :DIM], cosine, sine) * gain_k
        inner = jnp.mean(scaled * unit, axis=-1, keepdims=True)
        dk_ref[:, head * DIM : (head + 1) * DIM] = (inv_norm * (scaled - unit * inner)).astype(BF)
        dv_ref[:, head * DIM : (head + 1) * DIM] = both[:, DIM:].astype(BF)


def swap(array, slot):
    return lax.ppermute(array, "dp", [(j, j ^ slot) for j in range(N_DP)])


def shifted(array, by):
    return lax.ppermute(array, "cp", [(j, (j + by) % N_CP) for j in range(N_CP)])


def shape(*dims, dtype=BF):
    return jax.ShapeDtypeStruct(dims, dtype)


def body(q_raw, k_raw, values, loss_grad, send_order, doc_blocks, gain_q, gain_k):
    cos_np, sin_np = tables()
    cos_tab, sin_tab = jnp.asarray(cos_np), jnp.asarray(sin_np)
    gain_q = gain_q.reshape(1, DIM)
    gain_k = gain_k.reshape(1, DIM)
    kv_slots = pl.pallas_call(
        kv_pick,
        out_shape=[shape(ROWS, KV * PAIR)] * N_DP,
        in_specs=[VMEM] * 3,
        out_specs=[VMEM] * N_DP,
        scratch_shapes=[pltpu.VMEM((TOK, KV * PAIR), BF)],
        compiler_params=PARAMS,
        name="kv_pick",
    )(send_order, k_raw, values)
    kv_slots = [kv_slots[0]] + [swap(kv_slots[slot], slot) for slot in range(1, N_DP)]
    half = GROUP * DIM
    qg_slots = pl.pallas_call(
        qg_pick,
        grid=(KV,),
        out_shape=[shape(ROWS, KV * WIDE)] * N_DP,
        in_specs=[
            pl.BlockSpec((1, TOK), lambda h: (0, 0)),
            pl.BlockSpec((TOK, half), lambda h: (0, h)),
            pl.BlockSpec((TOK, half), lambda h: (0, h)),
        ],
        out_specs=[pl.BlockSpec((ROWS, WIDE), lambda h: (0, h))] * N_DP,
        scratch_shapes=[pltpu.VMEM((TOK, WIDE), BF)],
        compiler_params=PARAMS,
        name="qg_pick",
    )(send_order, q_raw, loss_grad)
    kv_own = pl.pallas_call(
        kv_join,
        out_shape=shape(TOK + ID_ROWS, KV * PAIR),
        in_specs=[SMEM] + [VMEM] * N_DP,
        out_specs=VMEM,
        compiler_params=PARAMS,
        name="kv_join",
    )(doc_blocks, *kv_slots)
    shards = [kv_own] + [shifted(kv_own, back) for back in range(1, REACH + 1)]
    qg_slots = [qg_slots[0]] + [swap(qg_slots[slot], slot) for slot in range(1, N_DP)]
    whole = lambda h: (0, 0)
    by_head = lambda h: (0, h)
    results = pl.pallas_call(
        attend,
        grid=(KV,),
        out_shape=[
            shape(TOK, KV * half),
            shape(TOK, KV * half),
            shape(TOK, KV * PAIR, dtype=F32),
        ]
        + [shape(TOK, KV * PAIR)] * REACH
        + [shape(8, 2 * DIM, dtype=F32), shape(1, 1, dtype=jnp.int32)],
        in_specs=[SMEM]
        + [pl.BlockSpec((ROWS, WIDE), by_head)] * N_DP
        + [pl.BlockSpec((TOK + ID_ROWS, PAIR), by_head)] * (REACH + 1)
        + [pl.BlockSpec((KEYS, DIM), whole)] * 2
        + [pl.BlockSpec((1, DIM), whole)] * 2,
        out_specs=[
            pl.BlockSpec((TOK, half), by_head),
            pl.BlockSpec((TOK, half), by_head),
            pl.BlockSpec((TOK, PAIR), by_head),
        ]
        + [pl.BlockSpec((TOK, PAIR), by_head)] * REACH
        + [pl.BlockSpec((8, 2 * DIM), whole), SMEM],
        scratch_shapes=[pltpu.VMEM((TOK, WIDE), BF), pltpu.VMEM((KEYS, TILE), F32)],
        compiler_params=PARAMS,
        name="attend",
    )(doc_blocks, *qg_slots, *shards, cos_tab, sin_tab, gain_q, gain_k)
    attn_out, dq_raw, dkv_own = results[:3]
    parts = [shifted(results[2 + back], -back) for back in range(1, REACH + 1)]
    gains, place = results[3 + REACH :]
    gain_row = jnp.sum(gains, axis=0, keepdims=True)
    everyone = lax.all_to_all(
        jnp.broadcast_to(gain_row, (N_DP * N_CP, 2 * DIM)), ("dp", "cp"), 0, 0, tiled=True
    )
    gain_sum = jnp.sum(everyone, axis=0) * (1.0 / math.sqrt(TOK * N_DP * N_CP))
    dk_raw, dv_out = pl.pallas_call(
        finish,
        out_shape=[shape(TOK, KV * DIM)] * 2,
        in_specs=[SMEM] + [VMEM] * (REACH + 5),
        out_specs=[VMEM] * 2,
        compiler_params=PARAMS,
        name="finish",
    )(place, dkv_own, *parts, kv_own, cos_tab, sin_tab, gain_k)
    return attn_out, dq_raw, dk_raw, dv_out, gain_sum[:DIM], gain_sum[DIM:]


def solution(mesh):
    rows = P(("dp", "cp"), None)
    return jax.shard_map(
        body,
        mesh=mesh,
        in_specs=(rows, rows, rows, rows, rows, P("dp", "cp"), P(), P()),
        out_specs=(rows, rows, rows, rows, P(), P()),
        check_vma=False,
    )
```

profile of v0, /device:TPU:1, one launch (start us, length us, event | category | flops | bytes accessed | tf_op | source)
XLA Modules:
  0.0 133.8 jit_solution(6903010924986558610)
XLA Ops:
  0.6 0.0 copy-start.4
  0.6 0.9 copy-done.4
  1.5 0.0 copy-start.5
  1.5 0.9 copy-done.5
  2.4 0.0 copy-start.6
  2.4 0.7 copy-done.6
  3.1 0.3 kv_pick.1
  3.4 3.3 %collective-permute-start.3 = (bf16[32,1024]{1,0:T(8,128)(2,1)S(1)}, bf16[32,1024]{1,0:T(8,128)(2,1)S(1)}, u32[]{:S(2)}, u32[]{:S(2)}) collective-permute-start(bf16[32,1024]{1,0:T(8,128)(2,1)S(1)} %get-tuple-element.30), channel_id=1, source_target_pairs={{0,64},{64,0},{128,192},{192,128},{1,65},{65,1},{129,193},{193,129... | collective-permute-start | bytes 196616 | tf_op jit(solution)/shard_map/ppermute | solution.py:237
  6.7 0.0 collective-permute-start.4
  6.7 1.7 %collective-permute-start.5 = (bf16[32,1024]{1,0:T(8,128)(2,1)S(1)}, bf16[32,1024]{1,0:T(8,128)(2,1)S(1)}, u32[]{:S(2)}, u32[]{:S(2)}) collective-permute-start(bf16[32,1024]{1,0:T(8,128)(2,1)S(1)} %get-tuple-element.32), channel_id=1, source_target_pairs={{0,192},{64,128},{128,64},{192,0},{1,193},{65,129},{129,65},{193,1... | collective-permute-start | bytes 196616 | tf_op jit(solution)/shard_map/ppermute | solution.py:237
  9.1 0.0 collective-permute-done.3.rest_1_
  9.1 1.3 collective-permute-done.4.rest_2_
  10.4 1.6 %collective-permute-done.5.rest_3_ = bf16[32,1024]{1,0:T(8,128)(2,1)S(1)} collective-permute-done((bf16[32,1024]{1,0:T(8,128)(2,1)S(1)}, bf16[32,1024]{1,0:T(8,128)(2,1)S(1)}, u32[]{:S(2)}, u32[]{:S(2)}) %collective-permute-start.5) | collective-permute-done | bytes 65568 | tf_op jit(solution)/shard_map/ppermute | solution.py:237
  11.9 0.0 copy-start.7
  12.0 0.0 copy-start
  12.0 0.0 copy-start.1
  12.0 1.3 collective-permute-start.9
  13.3 2.8 %collective-permute-start.8 = (bf16[136,1024]{1,0:T(8,128)(2,1)S(1)}, bf16[136,1024]{1,0:T(8,128)(2,1)S(1)}, u32[]{:S(2)}, u32[]{:S(2)}) collective-permute-start(bf16[136,1024]{1,0:T(8,128)(2,1)S(1)} %kv_join.1.rest_4_), channel_id=1, source_target_pairs={{0,3},{1,4},{2,5},{3,6},{4,7},{5,8},{6,9},{7,10},{8,11},{9,12},{10... | collective-permute-start | bytes 835592 | tf_op jit(solution)/shard_map/ppermute | solution.py:241
  16.1 0.0 copy-done.7
  16.1 0.0 copy-start.2
  16.1 1.2 copy-done.2
  17.3 0.0 copy-start.3
  17.4 1.2 copy-done.3
  18.6 1.8 %qg_pick.1 = (bf16[32,8192]{1,0:T(8,128)(2,1)S(1)}, bf16[32,8192]{1,0:T(8,128)(2,1)S(1)}, bf16[32,8192]{1,0:T(8,128)(2,1)S(1)}, bf16[32,8192]{1,0:T(8,128)(2,1)S(1)}) custom-call(s32[1,128]{1,0:T(1,128)S(1)} %copy-done.7, bf16[128,4096]{1,0:T(8,128)(2,1)S(1)} %copy-done.2, bf16[128,4096]{1,0:T(8,128)(2,1)S(1)} %copy-done.3), custom_call_target="tpu_custom_call" | custom-call | tf_op jit(solution)/shard_map/qg_pick/pallas_call | solution.py:264
  20.4 1.0 collective-permute-start
  21.4 0.2 collective-permute-start.1
  21.6 1.6 %collective-permute-start.2 = (bf16[32,8192]{1,0:T(8,128)(2,1)S(1)}, bf16[32,8192]{1,0:T(8,128)(2,1)S(1)}, u32[]{:S(2)}, u32[]{:S(2)}) collective-permute-start(bf16[32,8192]{1,0:T(8,128)(2,1)S(1)} %get-tuple-element.28), channel_id=1, source_target_pairs={{0,192},{64,128},{128,64},{192,0},{1,193},{65,129},{129,65},{193,1... | collective-permute-start | bytes 1572872 | tf_op jit(solution)/shard_map/ppermute | solution.py:237
  23.1 2.2 %collective-permute-done.9.rest_8_ = bf16[136,1024]{1,0:T(8,128)(2,1)S(1)} collective-permute-done((bf16[136,1024]{1,0:T(8,128)(2,1)S(1)}, bf16[136,1024]{1,0:T(8,128)(2,1)S(1)}, u32[]{:S(2)}, u32[]{:S(2)}) %collective-permute-start.9) | collective-permute-done | bytes 278560 | tf_op jit(solution)/shard_map/ppermute | solution.py:241
  25.3 0.4 collective-permute-start.7
  25.7 11.4 %collective-permute-done.8.rest_7_ = bf16[136,1024]{1,0:T(8,128)(2,1)S(1)} collective-permute-done((bf16[136,1024]{1,0:T(8,128)(2,1)S(1)}, bf16[136,1024]{1,0:T(8,128)(2,1)S(1)}, u32[]{:S(2)}, u32[]{:S(2)}) %collective-permute-start.8) | collective-permute-done | bytes 278560 | tf_op jit(solution)/shard_map/ppermute | solution.py:241
  37.1 0.0 collective-permute-start.6
  37.1 4.1 %collective-permute-done.7.rest_6_ = bf16[136,1024]{1,0:T(8,128)(2,1)S(1)} collective-permute-done((bf16[136,1024]{1,0:T(8,128)(2,1)S(1)}, bf16[136,1024]{1,0:T(8,128)(2,1)S(1)}, u32[]{:S(2)}, u32[]{:S(2)}) %collective-permute-start.7) | collective-permute-done | bytes 278560 | tf_op jit(solution)/shard_map/ppermute | solution.py:241
  41.2 9.3 %collective-permute-done.6.rest_5_ = bf16[136,1024]{1,0:T(8,128)(2,1)S(1)} collective-permute-done((bf16[136,1024]{1,0:T(8,128)(2,1)S(1)}, bf16[136,1024]{1,0:T(8,128)(2,1)S(1)}, u32[]{:S(2)}, u32[]{:S(2)}) %collective-permute-start.6) | collective-permute-done | bytes 278560 | tf_op jit(solution)/shard_map/ppermute | solution.py:241
  50.6 0.0 collective-permute-done.rest_1_
  50.6 0.0 collective-permute-done.1.rest_2_
  50.6 0.0 collective-permute-done.2.rest_3_
  50.6 0.0 copy-start.8
  50.6 0.0 copy-start.9
  50.6 0.0 copy-done
  50.6 0.0 copy-done.1
  50.6 0.6 copy-done.8
  51.2 0.0 copy-done.9
  51.3 23.5 %attend.1 = (bf16[128,4096]{1,0:T(8,128)(2,1)}, bf16[128,4096]{1,0:T(8,128)(2,1)}, f32[128,1024]{1,0:T(8,128)S(1)}, bf16[128,1024]{1,0:T(8,128)(2,1)S(1)}, bf16[...) custom-call(s32[1,1]{1,0:T(1,128)S(6)} %copy.18.doc_ref, ...), custom_call_target="tpu_custom_call" | custom-call | tf_op jit(solution)/shard_map/attend/pallas_call | solution.py:290
  74.8 0.8 broadcast_in_dim.2
  75.6 19.7 %all-to-all-start = ((f32[256,1,256]{2,1,0:T(1,128)}), f32[256,1,256]{2,1,0:T(1,128)S(1)}, u32[]{:S(2)}, u32[]{:S(2)}) async-start(f32[256,1,256]{2,1,0:T(1,128)} %broadcast_in_dim.2), calls=%async_computation | async-start | bytes 524288 | tf_op jit(solution)/shard_map/all_to_all | solution.py:320
  95.3 9.2 %collective-permute-start.10 = (bf16[128,1024]{1,0:T(8,128)(2,1)S(1)}, bf16[128,1024]{1,0:T(8,128)(2,1)S(1)}, u32[]{:S(2)}, u32[]{:S(2)}) collective-permute-start(bf16[128,1024]{1,0:T(8,128)(2,1)S(1)} %get-tuple-element.37), channel_id=1, source_target_pairs={{0,63},{1,0},{2,1},{3,2},{4,3},{5,4},{6,5},{7,6},{8,7},{9,8},{10,9... | collective-permute-start | bytes 786440 | tf_op jit(solution)/shard_map/ppermute | solution.py:241
  104.5 0.5 collective-permute-start.11
  105.0 0.2 collective-permute-start.12
  105.2 3.2 %collective-permute-start.13 = (bf16[128,1024]{1,0:T(8,128)(2,1)S(1)}, bf16[128,1024]{1,0:T(8,128)(2,1)S(1)}, u32[]{:S(2)}, u32[]{:S(2)}) collective-permute-start(bf16[128,1024]{1,0:T(8,128)(2,1)S(1)} %get-tuple-element.40), channel_id=1, source_target_pairs={{0,60},{1,61},{2,62},{3,63},{4,0},{5,1},{6,2},{7,3},{8,4},{9,5},{1... | collective-permute-start | bytes 786440 | tf_op jit(solution)/shard_map/ppermute | solution.py:241
  108.3 2.1 %collective-permute-done.10.rest_0_ = bf16[128,1024]{1,0:T(8,128)(2,1)S(1)} collective-permute-done((bf16[128,1024]{1,0:T(8,128)(2,1)S(1)}, bf16[128,1024]{1,0:T(8,128)(2,1)S(1)}, u32[]{:S(2)}, u32[]{:S(2)}) %collective-permute-start.10) | collective-permute-done | bytes 262176 | tf_op jit(solution)/shard_map/ppermute | solution.py:241
  110.5 10.2 %collective-permute-done.11.rest_1_ = bf16[128,1024]{1,0:T(8,128)(2,1)S(1)} collective-permute-done((bf16[128,1024]{1,0:T(8,128)(2,1)S(1)}, bf16[128,1024]{1,0:T(8,128)(2,1)S(1)}, u32[]{:S(2)}, u32[]{:S(2)}) %collective-permute-start.11) | collective-permute-done | bytes 262176 | tf_op jit(solution)/shard_map/ppermute | solution.py:241
  120.6 4.9 %collective-permute-done.12.rest_2_ = bf16[128,1024]{1,0:T(8,128)(2,1)S(1)} collective-permute-done((bf16[128,1024]{1,0:T(8,128)(2,1)S(1)}, bf16[128,1024]{1,0:T(8,128)(2,1)S(1)}, u32[]{:S(2)}, u32[]{:S(2)}) %collective-permute-start.12) | collective-permute-done | bytes 262176 | tf_op jit(solution)/shard_map/ppermute | solution.py:241
  125.6 5.6 %collective-permute-done.13.rest_3_ = bf16[128,1024]{1,0:T(8,128)(2,1)S(1)} collective-permute-done((bf16[128,1024]{1,0:T(8,128)(2,1)S(1)}, bf16[128,1024]{1,0:T(8,128)(2,1)S(1)}, u32[]{:S(2)}, u32[]{:S(2)}) %collective-permute-start.13) | collective-permute-done | bytes 262176 | tf_op jit(solution)/shard_map/ppermute | solution.py:241
  131.2 1.8 %finish.1 = (bf16[128,512]{1,0:T(8,128)(2,1)}, bf16[128,512]{1,0:T(8,128)(2,1)}) custom-call(s32[1,1]{1,0:T(1,128)} %get-tuple-element.35.place_ref, f32[128,1024]{1,0:T(8,128)S(1)} %get-tuple-element.36.own_ref, bf16[128,1024]{1,0:T(8,128)(2,1)S(1)} %collective-permute-done.10.rest_0_, bf16[128,1024]{1,0:T(8,128)(2,1)S(1)} %collective-permute-done.11.rest_1_, ...), custom_call_target="tpu_custom_call" | custom-call | tf_op jit(solution)/shard_map/finish/pallas_call | solution.py:324
  133.0 0.0 all-to-all-done
  133.0 0.3 reduce_sum.19
  133.3 0.5 fusion
  (3 shorter events, 0.1 us)
Async XLA Ops:
  0.6 0.9 copy-start.4
  1.5 0.9 copy-start.5
  2.4 0.7 copy-start.6
  3.4 5.7 %collective-permute-start.3 = (bf16[32,1024]{1,0:T(8,128)(2,1)S(1)}, bf16[32,1024]{1,0:T(8,128)(2,1)S(1)}, u32[]{:S(2)}, u32[]{:S(2)}) collective-permute-start(bf16[32,1024]{1,0:T(8,128)(2,1)S(1)} %get-tuple-element.30), channel_id=1, source_target_pairs={{0,64},{64,0},{128,192},{192,128},{1,65},{65,1},{129,193},{193,129... | collective-permute-start | bytes 196616 | tf_op jit(solution)/shard_map/ppermute | solution.py:237
  6.7 3.7 %collective-permute-start.4 = (bf16[32,1024]{1,0:T(8,128)(2,1)S(1)}, bf16[32,1024]{1,0:T(8,128)(2,1)S(1)}, u32[]{:S(2)}, u32[]{:S(2)}) collective-permute-start(bf16[32,1024]{1,0:T(8,128)(2,1)S(1)} %get-tuple-element.31), channel_id=1, source_target_pairs={{0,128},{64,192},{128,0},{192,64},{1,129},{65,193},{129,1},{193,65... | collective-permute-start | bytes 196616 | tf_op jit(solution)/shard_map/ppermute | solution.py:237
  6.7 5.2 %collective-permute-start.5 = (bf16[32,1024]{1,0:T(8,128)(2,1)S(1)}, bf16[32,1024]{1,0:T(8,128)(2,1)S(1)}, u32[]{:S(2)}, u32[]{:S(2)}) collective-permute-start(bf16[32,1024]{1,0:T(8,128)(2,1)S(1)} %get-tuple-element.32), channel_id=1, source_target_pairs={{0,192},{64,128},{128,64},{192,0},{1,193},{65,129},{129,65},{193,1... | collective-permute-start | bytes 196616 | tf_op jit(solution)/shard_map/ppermute | solution.py:237
  11.9 4.2 %copy-start.7 = (s32[1,128]{1,0:T(1,128)S(1)}, s32[1,128]{1,0:T(1,128)}, u32[]{:S(2)}) copy-start(s32[1,128]{1,0:T(1,128)} %order_ref.3) | copy-start | bytes 1540
  12.0 38.6 %copy-start = (f32[640,128]{1,0:T(8,128)S(1)}, f32[640,128]{1,0:T(8,128)}, u32[]{:S(2)}) copy-start(f32[640,128]{1,0:T(8,128)} %constant.9.clone.rest_10_.rest_6_) | copy-start | bytes 983044
  12.0 38.6 %copy-start.1 = (f32[640,128]{1,0:T(8,128)S(1)}, f32[640,128]{1,0:T(8,128)}, u32[]{:S(2)}) copy-start(f32[640,128]{1,0:T(8,128)} %constant.8.clone.rest_9_.rest_5_) | copy-start | bytes 983044
  12.0 13.3 %collective-permute-start.9 = (bf16[136,1024]{1,0:T(8,128)(2,1)S(1)}, bf16[136,1024]{1,0:T(8,128)(2,1)S(1)}, u32[]{:S(2)}, u32[]{:S(2)}) collective-permute-start(bf16[136,1024]{1,0:T(8,128)(2,1)S(1)} %kv_join.1.rest_4_), channel_id=1, source_target_pairs={{0,4},{1,5},{2,6},{3,7},{4,8},{5,9},{6,10},{7,11},{8,12},{9,13},{1... | collective-permute-start | bytes 835592 | tf_op jit(solution)/shard_map/ppermute | solution.py:241
  13.3 23.8 %collective-permute-start.8 = (bf16[136,1024]{1,0:T(8,128)(2,1)S(1)}, bf16[136,1024]{1,0:T(8,128)(2,1)S(1)}, u32[]{:S(2)}, u32[]{:S(2)}) collective-permute-start(bf16[136,1024]{1,0:T(8,128)(2,1)S(1)} %kv_join.1.rest_4_), channel_id=1, source_target_pairs={{0,3},{1,4},{2,5},{3,6},{4,7},{5,8},{6,9},{7,10},{8,11},{9,12},{10... | collective-permute-start | bytes 835592 | tf_op jit(solution)/shard_map/ppermute | solution.py:241
  16.1 1.2 copy-start.2
  17.3 1.2 copy-start.3
  20.4 30.2 %collective-permute-start = (bf16[32,8192]{1,0:T(8,128)(2,1)S(1)}, bf16[32,8192]{1,0:T(8,128)(2,1)S(1)}, u32[]{:S(2)}, u32[]{:S(2)}) collective-permute-start(bf16[32,8192]{1,0:T(8,128)(2,1)S(1)} %get-tuple-element.26), channel_id=1, source_target_pairs={{0,64},{64,0},{128,192},{192,128},{1,65},{65,1},{129,193},{193,129... | collective-permute-start | bytes 1572872 | tf_op jit(solution)/shard_map/ppermute | solution.py:237
  21.4 29.2 %collective-permute-start.1 = (bf16[32,8192]{1,0:T(8,128)(2,1)S(1)}, bf16[32,8192]{1,0:T(8,128)(2,1)S(1)}, u32[]{:S(2)}, u32[]{:S(2)}) collective-permute-start(bf16[32,8192]{1,0:T(8,128)(2,1)S(1)} %get-tuple-element.27), channel_id=1, source_target_pairs={{0,128},{64,192},{128,0},{192,64},{1,129},{65,193},{129,1},{193,65... | collective-permute-start | bytes 1572872 | tf_op jit(solution)/shard_map/ppermute | solution.py:237
  21.6 29.0 %collective-permute-start.2 = (bf16[32,8192]{1,0:T(8,128)(2,1)S(1)}, bf16[32,8192]{1,0:T(8,128)(2,1)S(1)}, u32[]{:S(2)}, u32[]{:S(2)}) collective-permute-start(bf16[32,8192]{1,0:T(8,128)(2,1)S(1)} %get-tuple-element.28), channel_id=1, source_target_pairs={{0,192},{64,128},{128,64},{192,0},{1,193},{65,129},{129,65},{193,1... | collective-permute-start | bytes 1572872 | tf_op jit(solution)/shard_map/ppermute | solution.py:237
  25.3 15.9 %collective-permute-start.7 = (bf16[136,1024]{1,0:T(8,128)(2,1)S(1)}, bf16[136,1024]{1,0:T(8,128)(2,1)S(1)}, u32[]{:S(2)}, u32[]{:S(2)}) collective-permute-start(bf16[136,1024]{1,0:T(8,128)(2,1)S(1)} %kv_join.1.rest_4_), channel_id=1, source_target_pairs={{0,2},{1,3},{2,4},{3,5},{4,6},{5,7},{6,8},{7,9},{8,10},{9,11},{10,... | collective-permute-start | bytes 835592 | tf_op jit(solution)/shard_map/ppermute | solution.py:241
  37.1 13.4 %collective-permute-start.6 = (bf16[136,1024]{1,0:T(8,128)(2,1)S(1)}, bf16[136,1024]{1,0:T(8,128)(2,1)S(1)}, u32[]{:S(2)}, u32[]{:S(2)}) collective-permute-start(bf16[136,1024]{1,0:T(8,128)(2,1)S(1)} %kv_join.1.rest_4_), channel_id=1, source_target_pairs={{0,1},{1,2},{2,3},{3,4},{4,5},{5,6},{6,7},{7,8},{8,9},{9,10},{10,1... | collective-permute-start | bytes 835592 | tf_op jit(solution)/shard_map/ppermute | solution.py:241
  50.6 0.7 copy-start.8
  50.6 0.7 copy-start.9
  75.6 57.4 %all-to-all-start = ((f32[256,1,256]{2,1,0:T(1,128)}), f32[256,1,256]{2,1,0:T(1,128)S(1)}, u32[]{:S(2)}, u32[]{:S(2)}) async-start(f32[256,1,256]{2,1,0:T(1,128)} %broadcast_in_dim.2), calls=%async_computation | async-start | bytes 524288 | tf_op jit(solution)/shard_map/all_to_all | solution.py:320
  95.3 15.2 %collective-permute-start.10 = (bf16[128,1024]{1,0:T(8,128)(2,1)S(1)}, bf16[128,1024]{1,0:T(8,128)(2,1)S(1)}, u32[]{:S(2)}, u32[]{:S(2)}) collective-permute-start(bf16[128,1024]{1,0:T(8,128)(2,1)S(1)} %get-tuple-element.37), channel_id=1, source_target_pairs={{0,63},{1,0},{2,1},{3,2},{4,3},{5,4},{6,5},{7,6},{8,7},{9,8},{10,9... | collective-permute-start | bytes 786440 | tf_op jit(solution)/shard_map/ppermute | solution.py:241
  104.5 16.2 %collective-permute-start.11 = (bf16[128,1024]{1,0:T(8,128)(2,1)S(1)}, bf16[128,1024]{1,0:T(8,128)(2,1)S(1)}, u32[]{:S(2)}, u32[]{:S(2)}) collective-permute-start(bf16[128,1024]{1,0:T(8,128)(2,1)S(1)} %get-tuple-element.38), channel_id=1, source_target_pairs={{0,62},{1,63},{2,0},{3,1},{4,2},{5,3},{6,4},{7,5},{8,6},{9,7},{10,... | collective-permute-start | bytes 786440 | tf_op jit(solution)/shard_map/ppermute | solution.py:241
  105.0 20.6 %collective-permute-start.12 = (bf16[128,1024]{1,0:T(8,128)(2,1)S(1)}, bf16[128,1024]{1,0:T(8,128)(2,1)S(1)}, u32[]{:S(2)}, u32[]{:S(2)}) collective-permute-start(bf16[128,1024]{1,0:T(8,128)(2,1)S(1)} %get-tuple-element.39), channel_id=1, source_target_pairs={{0,61},{1,62},{2,63},{3,0},{4,1},{5,2},{6,3},{7,4},{8,5},{9,6},{10... | collective-permute-start | bytes 786440 | tf_op jit(solution)/shard_map/ppermute | solution.py:241
  105.2 26.0 %collective-permute-start.13 = (bf16[128,1024]{1,0:T(8,128)(2,1)S(1)}, bf16[128,1024]{1,0:T(8,128)(2,1)S(1)}, u32[]{:S(2)}, u32[]{:S(2)}) collective-permute-start(bf16[128,1024]{1,0:T(8,128)(2,1)S(1)} %get-tuple-element.40), channel_id=1, source_target_pairs={{0,60},{1,61},{2,62},{3,63},{4,0},{5,1},{6,2},{7,3},{8,4},{9,5},{1... | collective-permute-start | bytes 786440 | tf_op jit(solution)/shard_map/ppermute | solution.py:241
where the time goes:
time: 135 us; the launch traced here: 134 us
  waiting for transfers between devices  52.7 us (39%)
  starting transfers between devices  45 us (33%)
  Pallas kernels  27.4 us (20%)
  local copies, waits for them, and re-layouts  6.92 us (5%)
  between operations  1.4 us (1%)
    ppermute x8, waiting for transfers between devices, shifted(): lax.ppermute(array, 'cp', [(j, (j + by) % N_CP) for j in range(N_CP)])  49.9 us
    pallas_call x1, Pallas kernels, body(): pl.pallas_call(attend, grid=(KV,), out_shape=[shape(TOK, KV * half), shap...  23.5 us
    all_to_all x1, starting transfers between devices, body(): lax.all_to_all(jnp.broadcast_to(gain_row, (N_DP * N_CP, 2 * DIM)), ('dp',...  19.7 us
    ppermute x8, starting transfers between devices, shifted(): lax.ppermute(array, 'cp', [(j, (j + by) % N_CP) for j in range(N_CP)])  17.5 us
    ppermute x6, starting transfers between devices, swap(): return lax.ppermute(array, 'dp', [(j, j ^ slot) for j in range(N_DP)])  7.82 us
    unnamed x20, local copies, waits for them, and re-layouts  5.56 us
    ppermute x6, waiting for transfers between devices, swap(): return lax.ppermute(array, 'dp', [(j, j ^ slot) for j in range(N_DP)])  2.86 us
  transfers between devices with their start and end apart: 15, of which 10 were waited for; matrix products, arithmetic and copies ran while one was open for 0% of the time, Pallas kernels for 3%

commit v1 on v0

v1 whole, which is shorter than its diff:
```python
import math

import jax
import jax.numpy as jnp
import numpy as np
from jax import lax
from jax.experimental import pallas as pl
from jax.experimental.pallas import tpu as pltpu
from jax.sharding import PartitionSpec as P

REACH = 4
EPSILON = 1e-06
THETA = 1000000.0
NEGATIVE = -1e30
TOK = 128
DIM = 128
KV = 4
GROUP = 8
N_DP = 4
N_CP = 64
ROWS = TOK // N_DP
KEYS = (REACH + 1) * TOK
ID_ROWS = 8
TILE = 256
LAG = 1
PAIR = 2 * DIM
WIDE = 2 * GROUP * DIM
INV_ROOT = 1.0 / math.sqrt(DIM)
LOG2E = 1.4426950408889634
BF = jnp.bfloat16
F32 = jnp.float32
blocks = [slice(at * TOK, (at + 1) * TOK) for at in range(REACH + 1)]
VMEM = pl.BlockSpec(memory_space=pltpu.VMEM)
SMEM = pl.BlockSpec(memory_space=pltpu.SMEM)
VLIM = 24
PARAMS = pltpu.CompilerParams(vmem_limit_bytes=VLIM * 1024 * 1024)


def tables():
    half = DIM // 2
    frequency = (THETA ** (-(np.arange(half) * 2.0 / DIM))).astype(np.float32)
    angles = np.arange(KEYS, dtype=np.float32)[:, None] * frequency[None, :]
    cosine = np.cos(angles.astype(np.float64)).astype(np.float32)
    sine = np.sin(angles.astype(np.float64)).astype(np.float32)
    return np.concatenate([cosine, cosine, -sine, sine], axis=1)


def dot(left, right, left_dim, right_dim):
    return lax.dot_general(
        left, right, (((left_dim,), (right_dim,)), ((), ())), preferred_element_type=F32
    )


def picker(order_ref):
    rows = lax.broadcasted_iota(jnp.int32, (TOK, TOK), 0)
    return jnp.where(rows == order_ref[...], 1.0, 0.0).astype(BF)


def slot_rows(slot):
    place = lax.axis_index("dp") ^ slot
    return pl.ds(pl.multiple_of(place * ROWS, ROWS), ROWS)


def kv_pick(order_ref, k_ref, v_ref, *rest):
    outs, rows_ref = rest[:N_DP], rest[N_DP]
    chosen = picker(order_ref)
    keys = dot(chosen, k_ref[...], 0, 0).astype(BF)
    vals = dot(chosen, v_ref[...], 0, 0).astype(BF)
    for head in range(KV):
        rows_ref[:, head * PAIR : head * PAIR + DIM] = keys[:, head * DIM : (head + 1) * DIM]
        rows_ref[:, head * PAIR + DIM : (head + 1) * PAIR] = vals[:, head * DIM : (head + 1) * DIM]
    for slot in range(N_DP):
        outs[slot][...] = rows_ref[slot_rows(slot), :]


def qg_pick(order_ref, q_ref, g_ref, *rest):
    q_outs, g_outs, rows_ref = rest[:N_DP], rest[N_DP : 2 * N_DP], rest[2 * N_DP]
    chosen = picker(order_ref)
    half = GROUP * DIM
    rows_ref[:, :half] = dot(chosen, q_ref[...], 0, 0).astype(BF)
    rows_ref[:, half:] = dot(chosen, g_ref[...], 0, 0).astype(BF)
    for slot in range(N_DP):
        q_outs[slot][...] = rows_ref[slot_rows(slot), :half]
        g_outs[slot][...] = rows_ref[slot_rows(slot), half:]


def kv_join(doc_ref, *rest):
    slots, out_ref = rest[:N_DP], rest[N_DP]
    for slot in range(N_DP):
        out_ref[slot_rows(slot), :] = slots[slot][...]
    width = out_ref.shape[1]
    out_ref[TOK:, :] = jnp.full((ID_ROWS, width), doc_ref[0, 0], jnp.int32).astype(F32).astype(BF)


def same_docs(doc_ref, shards):
    own = doc_ref[0, 0].astype(F32)
    place = lax.axis_index("cp")
    flags = []
    for back in range(1, REACH + 1):
        near = jnp.max(shards[back][TOK : TOK + ID_ROWS, 0:DIM].astype(F32))
        flags.append(jnp.where((near == own) & (place >= back), 1, 0).astype(jnp.int32))
    return flags


def flip_angles(table_ref, block):
    first = pl.multiple_of(block * TOK, TOK)
    second = pl.multiple_of(block * TOK + KEYS, TOK)
    return table_ref[:, pl.ds(first, TOK)], table_ref[:, pl.ds(second, TOK)]


def half_swap(array):
    return jnp.concatenate([array[DIM // 2 :], array[: DIM // 2]], axis=0)


def angles_of(table_ref, block):
    rows = table_ref[pl.ds(pl.multiple_of(block * TOK, TOK), TOK), :]
    return rows[:, :DIM], rows[:, DIM:]


def turn(vectors, cosine, sine):
    return vectors * cosine + pltpu.roll(vectors, DIM // 2, 1) * sine


def turn_back(vectors, cosine, sine):
    return vectors * cosine - pltpu.roll(vectors, DIM // 2, 1) * sine


def unit_of(raw):
    inv_norm = lax.rsqrt(jnp.mean(raw * raw, axis=-1, keepdims=True) + EPSILON)
    return raw * inv_norm, inv_norm


def query_unit(*refs):
    slots = refs[:N_DP]
    table_ref, flip_ref, unit_ref, norm_ref, table_out, flip_out, rows_ref = refs[N_DP:]
    table_out[...] = table_ref[...]
    flip_out[...] = flip_ref[...]
    for slot in range(N_DP):
        rows_ref[slot_rows(slot), :] = slots[slot][...]
    for at in range(0, GROUP * DIM, DIM):
        raw = rows_ref[:, at : at + DIM].astype(F32).T
        inv_norm = lax.rsqrt(jnp.mean(raw * raw, axis=0, keepdims=True) + EPSILON)
        unit_ref[:, at : at + DIM] = raw * inv_norm
        norm_ref[:, at : at + DIM] = jnp.broadcast_to(inv_norm, (8, DIM))


def forward(doc_ref, *rest):
    unitq_ref = rest[0]
    shards = rest[1 : REACH + 2]
    table_ref, flip_ref, gq_ref, gk_ref = rest[REACH + 2 : REACH + 6]
    out_ref, again_ref, prob_ref, query_ref, rot_ref, unit_ref, place_ref = rest[REACH + 6 :]
    flags = same_docs(doc_ref, shards)
    block = flags[0] + flags[1] + flags[2] + flags[3]
    place_ref[0, 0] = block
    gain_q = jnp.broadcast_to(gq_ref[...], (TOK, DIM)).T
    gain_k = gk_ref[...]
    own_cos, own_sin = flip_angles(flip_ref, block)
    key_rot, key_val = [], []
    for at, back in enumerate(range(REACH, -1, -1)):
        cosine, sine = angles_of(table_ref, jnp.maximum(block - back, 0))
        unit, _ = unit_of(shards[back][:TOK, :DIM].astype(F32))
        turned = turn(unit * gain_k, cosine, sine).astype(BF)
        unit_ref[blocks[at], :] = unit
        rot_ref[blocks[at], :] = turned
        key_rot.append(turned)
        key_val.append(shards[back][:TOK, DIM:])
    rot_f = jnp.concatenate(key_rot, axis=0)
    val_t = jnp.concatenate(key_val, axis=0).T
    levels = [jnp.where(flags[back - 1] > 0, 0.0, NEGATIVE) for back in range(REACH, 0, -1)]
    key = lax.broadcasted_iota(jnp.int32, (TOK, TILE), 0)
    query = lax.broadcasted_iota(jnp.int32, (TOK, TILE), 1) & (TOK - 1)
    causal = key <= query
    heads = TILE // TOK

    def ready(first):
        places = [(first + j) * DIM for j in range(heads)]
        turned = []
        for at in places:
            scaled = unitq_ref[:, at : at + DIM] * gain_q
            query_t = scaled * own_cos + half_swap(scaled) * own_sin
            turned.append(query_t.astype(BF))
            query_ref[:, at : at + DIM] = query_t.T.astype(BF)
        return places, dot(rot_f, jnp.concatenate(turned, axis=1), 1, 0)

    def soft(state):
        places, scores = state
        last = jnp.where(causal, scores[blocks[REACH]], NEGATIVE)
        parts = [scores[blocks[at]] for at in range(REACH)] + [last]
        tops = [jnp.max(part, axis=0, keepdims=True) for part in parts]
        top = tops[REACH]
        for at in range(REACH):
            top = jnp.maximum(top, tops[at] + levels[at])
        top = top * (INV_ROOT * LOG2E)
        weights, total = [], 0.0
        for at in range(REACH + 1):
            shift = top if at == REACH else top - levels[at]
            weight = jnp.exp2(parts[at] * (INV_ROOT * LOG2E) - shift)
            total = total + jnp.sum(weight, axis=0, keepdims=True)
            weights.append(weight)
        inverse = 1.0 / total
        for at in range(REACH + 1):
            prob_ref[blocks[at], places[0] : places[0] + TILE] = weights[at] * inverse
        weights = jnp.concatenate(weights, axis=0).astype(BF)
        out_t = dot(val_t, weights, 1, 0) / total
        for j, at in enumerate(places):
            out = out_t[:, j * TOK : (j + 1) * TOK].T.astype(BF)
            out_ref[:, at : at + DIM] = out
            again_ref[:, at : at + DIM] = out

    count = GROUP // heads
    states = {}
    for turn_at in range(count + LAG):
        if turn_at < count:
            states[turn_at] = ready(turn_at * heads)
        if turn_at >= LAG:
            soft(states.pop(turn_at - LAG))


def backward(place_ref, *rest):
    slots = rest[:N_DP]
    shards = rest[N_DP : N_DP + REACH + 1]
    out_ref, prob_ref, query_ref, unit_ref, table_ref = rest[N_DP + REACH + 1 : N_DP + REACH + 6]
    outs = rest[N_DP + REACH + 6 :]
    ds_ref, own_ref = outs[:2]
    part_refs = outs[2 : 2 + REACH]
    gain_ref, rows_ref = outs[2 + REACH :]
    block = place_ref[0, 0]

    @pl.when(pl.program_id(0) == 0)
    def start():
        gain_ref[...] = jnp.zeros_like(gain_ref)

    for slot in range(N_DP):
        rows_ref[slot_rows(slot), :] = slots[slot][...]
    val_b = jnp.concatenate([shards[back][:TOK, DIM:] for back in range(REACH, -1, -1)], axis=0)
    heads = TILE // TOK

    def ready(first):
        places = [(first + j) * DIM for j in range(heads)]
        grads = [rows_ref[:, at : at + DIM] for at in places]
        grad = jnp.concatenate(grads, axis=0)
        deltas = []
        for at, own in zip(places, grads):
            both = own.astype(F32) * out_ref[:, at : at + DIM].astype(F32)
            deltas.append(jnp.sum(both.T, axis=0, keepdims=True))
        return places, grad, jnp.concatenate(deltas, axis=1), dot(val_b, grad, 1, 1)

    def back(state, sums):
        places, grad, delta, dprob = state
        span = slice(places[0], places[0] + TILE)
        probs = prob_ref[:, span]
        dscore = (probs * (dprob - delta)).astype(BF)
        ds_ref[:, span] = dscore
        query = jnp.concatenate([query_ref[:, at : at + DIM] for at in places], axis=0)
        dk = dot(dscore, query, 1, 0)
        dv = dot(probs.astype(BF), grad, 1, 0)
        return (dk, dv) if sums is None else (sums[0] + dk, sums[1] + dv)

    count = GROUP // heads
    states, sums = {}, None
    for turn_at in range(count + LAG):
        if turn_at < count:
            states[turn_at] = ready(turn_at * heads)
        if turn_at >= LAG:
            sums = back(states.pop(turn_at - LAG), sums)
    dk_total, dv_total = sums
    gk_total = jnp.zeros((8, DIM), F32)
    for at, back_by in enumerate(range(REACH, -1, -1)):
        cosine, sine = angles_of(table_ref, jnp.maximum(block - back_by, 0))
        dk_part = dk_total[blocks[at]] * INV_ROOT
        dkn = turn_back(dk_part, cosine, sine)
        gk_total = gk_total + jnp.sum((dkn * unit_ref[blocks[at], :]).reshape(TOK // 8, 8, DIM), axis=0)
        target = own_ref if back_by == 0 else part_refs[back_by - 1]
        target[:, :DIM] = dk_part.astype(target.dtype)
        target[:, DIM:] = dv_total[blocks[at]].astype(target.dtype)
    gain_ref[...] += gk_total


def query_back(place_ref, unit_ref, norm_ref, ds_ref, rot_ref, flip_ref, gq_ref, gk_ref, dq_ref, gain_ref, sum_ref):
    step = pl.program_id(0)

    @pl.when(step == 0)
    def start():
        sum_ref[...] = jnp.zeros_like(sum_ref)

    gain_q = jnp.broadcast_to(gq_ref[...], (TOK, DIM)).T
    cosine, sine = flip_angles(flip_ref, place_ref[0, 0])
    rot_t = rot_ref[...].T
    total = jnp.zeros((DIM, TOK), F32)
    for first in range(0, GROUP * DIM, TILE):
        both = dot(rot_t, ds_ref[:, first : first + TILE], 1, 0) * INV_ROOT
        for at in range(first, first + TILE, TOK):
            dq_t = both[:, at - first : at - first + TOK]
            unit = unit_ref[:, at : at + DIM]
            dqn = dq_t * cosine - half_swap(dq_t) * sine
            total = total + dqn * unit
            scaled = dqn * gain_q
            inner = jnp.mean(scaled * unit, axis=0, keepdims=True)
            back = norm_ref[0:1, at : at + DIM] * (scaled - unit * inner)
            dq_ref[:, at : at + DIM] = back.T.astype(BF)
    sum_ref[...] += total

    @pl.when(step == KV - 1)
    def end():
        spread = (N_DP * N_CP, DIM)
        by_query = jnp.sum(sum_ref[...].T, axis=0, keepdims=True)
        by_key = jnp.sum(gk_ref[...], axis=0, keepdims=True)
        gain_ref[:, :DIM] = jnp.broadcast_to(by_query, spread)
        gain_ref[:, DIM:] = jnp.broadcast_to(by_key, spread)


def finish(place_ref, own_ref, *rest):
    parts = rest[:REACH]
    kv_ref, table_ref, gk_ref, every_ref, dk_ref, dv_ref, gq_out, gk_out = rest[REACH:]
    sums = jnp.sum(every_ref[...], axis=0, keepdims=True) * (1.0 / math.sqrt(TOK * N_DP * N_CP))
    gq_out[...] = sums[:, :DIM]
    gk_out[...] = sums[:, DIM:]
    cosine, sine = angles_of(table_ref, place_ref[0, 0])
    gain_k = gk_ref[...]
    for head in range(KV):
        left = head * PAIR
        both = own_ref[:, left : left + PAIR]
        for part in parts:
            both = both + part[:, left : left + PAIR].astype(F32)
        unit, inv_norm = unit_of(kv_ref[:TOK, left : left + DIM].astype(F32))
        scaled = turn_back(both[:, :DIM], cosine, sine) * gain_k
        inner = jnp.mean(scaled * unit, axis=-1, keepdims=True)
        dk_ref[:, head * DIM : (head + 1) * DIM] = (inv_norm * (scaled - unit * inner)).astype(BF)
        dv_ref[:, head * DIM : (head + 1) * DIM] = both[:, DIM:].astype(BF)


def swap(array, slot):
    return lax.ppermute(array, "dp", [(j, j ^ slot) for j in range(N_DP)])


def shifted(array, by):
    return lax.ppermute(array, "cp", [(j, (j + by) % N_CP) for j in range(N_CP)])


def shape(*dims, dtype=BF):
    return jax.ShapeDtypeStruct(dims, dtype)


def body(q_raw, k_raw, values, loss_grad, send_order, doc_blocks, gain_q, gain_k):
    table_np = tables()
    table = jnp.asarray(table_np)
    flipped = jnp.asarray(np.concatenate([table_np[:, :DIM].T, table_np[:, DIM:].T], axis=1))
    gain_q = gain_q.reshape(1, DIM)
    gain_k = gain_k.reshape(1, DIM)
    kv_slots = pl.pallas_call(
        kv_pick,
        out_shape=[shape(ROWS, KV * PAIR)] * N_DP,
        in_specs=[VMEM] * 3,
        out_specs=[VMEM] * N_DP,
        scratch_shapes=[pltpu.VMEM((TOK, KV * PAIR), BF)],
        compiler_params=pltpu.CompilerParams(vmem_limit_bytes=62 * 1024 * 1024),
        name="kv_pick",
    )(send_order, k_raw, values)
    kv_slots = [kv_slots[0]] + [swap(kv_slots[slot], slot) for slot in range(1, N_DP)]
    half = GROUP * DIM
    picked = pl.pallas_call(
        qg_pick,
        grid=(KV,),
        out_shape=[shape(ROWS, KV * half)] * (2 * N_DP),
        in_specs=[
            pl.BlockSpec((1, TOK), lambda h: (0, 0)),
            pl.BlockSpec((TOK, half), lambda h: (0, h)),
            pl.BlockSpec((TOK, half), lambda h: (0, h)),
        ],
        out_specs=[pl.BlockSpec((ROWS, half), lambda h: (0, h))] * (2 * N_DP),
        scratch_shapes=[pltpu.VMEM((TOK, WIDE), BF)],
        compiler_params=PARAMS,
        name="qg_pick",
    )(send_order, q_raw, loss_grad)
    kv_own = pl.pallas_call(
        kv_join,
        out_shape=shape(TOK + ID_ROWS, KV * PAIR),
        in_specs=[SMEM] + [VMEM] * N_DP,
        out_specs=VMEM,
        compiler_params=PARAMS,
        name="kv_join",
    )(doc_blocks, *kv_slots)
    one = shifted(kv_own, 1)
    two = shifted(kv_own, 2)
    shards = [kv_own, one, two, shifted(one, 2), shifted(two, 2)]
    q_slots = [picked[0]] + [swap(picked[slot], slot) for slot in range(1, N_DP)]
    g_slots = [picked[N_DP]] + [swap(picked[N_DP + slot], slot) for slot in range(1, N_DP)]
    whole = lambda h: (0, 0)
    by_head = lambda h: (0, h)
    slot_specs = [pl.BlockSpec((ROWS, half), by_head)] * N_DP
    shard_specs = [pl.BlockSpec((TOK + ID_ROWS, PAIR), by_head)] * (REACH + 1)
    table_specs = [pl.BlockSpec((KEYS, 2 * DIM), whole)]
    rows_spec = pl.BlockSpec((TOK, half), by_head)
    keys_spec = pl.BlockSpec((KEYS, DIM), by_head)
    square_spec = pl.BlockSpec((KEYS, half), by_head)
    flip_specs = [pl.BlockSpec((DIM, 2 * KEYS), whole)]
    gain_spec = pl.BlockSpec((1, DIM), whole)
    norm_spec = pl.BlockSpec((8, half), by_head)
    part = KEYS // KV
    table_part = pl.BlockSpec((part, 2 * DIM), lambda h: (h, 0))
    flip_part = pl.BlockSpec((DIM // KV, 2 * KEYS), lambda h: (h, 0))
    units, norms, table, flipped = pl.pallas_call(
        query_unit,
        grid=(KV,),
        out_shape=[
            shape(DIM, KV * half, dtype=F32),
            shape(8, KV * half, dtype=F32),
            shape(KEYS, 2 * DIM, dtype=F32),
            shape(DIM, 2 * KEYS, dtype=F32),
        ],
        in_specs=slot_specs + [table_part, flip_part],
        out_specs=[rows_spec, norm_spec, table_part, flip_part],
        scratch_shapes=[pltpu.VMEM((TOK, half), BF)],
        compiler_params=PARAMS,
        name="query_unit",
    )(*q_slots, table, flipped)
    attn_out, out_again, probs, queries, keys_rot, keys_unit, place = pl.pallas_call(
        forward,
        grid=(KV,),
        out_shape=[
            shape(TOK, KV * half),
            shape(TOK, KV * half),
            shape(KEYS, KV * half, dtype=F32),
            shape(TOK, KV * half),
            shape(KEYS, KV * DIM),
            shape(KEYS, KV * DIM, dtype=F32),
            shape(1, 1, dtype=jnp.int32),
        ],
        in_specs=[SMEM, rows_spec] + shard_specs + table_specs + flip_specs + [gain_spec] * 2,
        out_specs=[rows_spec, rows_spec, square_spec, rows_spec, keys_spec, keys_spec, SMEM],
        compiler_params=PARAMS,
        name="forward",
    )(doc_blocks, units, *shards, table, flipped, gain_q, gain_k)
    results = pl.pallas_call(
        backward,
        grid=(KV,),
        out_shape=[shape(KEYS, KV * half), shape(TOK, KV * PAIR, dtype=F32)]
        + [shape(TOK, KV * PAIR)] * REACH
        + [shape(8, DIM, dtype=F32)],
        in_specs=[SMEM]
        + slot_specs
        + shard_specs
        + [rows_spec, square_spec, rows_spec, keys_spec]
        + table_specs,
        out_specs=[square_spec, pl.BlockSpec((TOK, PAIR), by_head)]
        + [pl.BlockSpec((TOK, PAIR), by_head)] * REACH
        + [pl.BlockSpec((8, DIM), whole)],
        scratch_shapes=[pltpu.VMEM((TOK, half), BF)],
        compiler_params=PARAMS,
        name="backward",
    )(place, *g_slots, *shards, out_again, probs, queries, keys_unit, table)
    dscores, dkv_own = results[:2]
    gk_rows = results[2 + REACH]
    parts = [shifted(results[1 + back], -back) for back in range(1, REACH + 1)]

    def query_side(operands):
        place, units, norms, dscores, keys_rot, gk_rows = operands
        dq_raw, gains = pl.pallas_call(
            query_back,
            grid=(KV,),
            out_shape=[shape(TOK, KV * half), shape(N_DP * N_CP, 2 * DIM, dtype=F32)],
            in_specs=[SMEM, rows_spec, norm_spec, square_spec, keys_spec]
            + flip_specs
            + [gain_spec, pl.BlockSpec((8, DIM), whole)],
            out_specs=[rows_spec, pl.BlockSpec((N_DP * N_CP, 2 * DIM), whole)],
            scratch_shapes=[pltpu.VMEM((DIM, TOK), F32)],
            compiler_params=PARAMS,
            name="query_back",
        )(place, units, norms, dscores, keys_rot, flipped, gain_q, gk_rows)
        return dq_raw, lax.all_to_all(gains, ("dp", "cp"), 0, 0, tiled=True)

    def nothing(operands):
        return jnp.zeros((TOK, KV * half), BF), jnp.zeros((N_DP * N_CP, 2 * DIM), F32)

    dq_raw, everyone = lax.cond(
        place[0, 0] >= 0, query_side, nothing, (place, units, norms, dscores, keys_rot, gk_rows)
    )
    dk_raw, dv_out, dgain_q, dgain_k = pl.pallas_call(
        finish,
        out_shape=[shape(TOK, KV * DIM)] * 2 + [shape(1, DIM, dtype=F32)] * 2,
        in_specs=[SMEM] + [VMEM] * (REACH + 5),
        out_specs=[VMEM] * 4,
        compiler_params=PARAMS,
        name="finish",
    )(place, dkv_own, *parts, kv_own, table, gain_k, everyone)
    return attn_out, dq_raw, dk_raw, dv_out, dgain_q.reshape(DIM), dgain_k.reshape(DIM)


def solution(mesh):
    rows = P(("dp", "cp"), None)
    return jax.shard_map(
        body,
        mesh=mesh,
        in_specs=(rows, rows, rows, rows, rows, P("dp", "cp"), P(), P()),
        out_specs=(rows, rows, rows, rows, P(), P()),
        check_vma=False,
    )
```

time: 135 us -> 108 us (0.80)
  waiting for transfers between devices: 52.7 us -> 22.3 us
  blocking collectives: 0 us -> 26.6 us
  starting transfers between devices: 45 us -> 18.7 us
  Pallas kernels: 27.4 us -> 31.8 us
    ppermute x8, waiting for transfers between devices: 49.9 us -> 19.2 us  [shifted(): lax.ppermute(array, 'cp', [(j, (j + by) % N_CP) for j in range(N_CP)])]
    all_to_all x0 -> x1, blocking collectives: none -> 26.6 us  [query_side(): return (dq_raw, lax.all_to_all(gains, ('dp', 'cp'), 0, 0, tiled=True))]
    all_to_all x1 -> x0, starting transfers between devices: 19.7 us -> none  [body(): lax.all_to_all(jnp.broadcast_to(gain_row, (N_DP * N_CP, 2 * DIM)), ('dp',...]
    ppermute x8, starting transfers between devices: 17.5 us -> 7.96 us  [shifted(): lax.ppermute(array, 'cp', [(j, (j + by) % N_CP) for j in range(N_CP)])]
    ppermute x6 -> x9, starting transfers between devices: 7.82 us -> 10.7 us  [swap(): return lax.ppermute(array, 'dp', [(j, j ^ slot) for j in range(N_DP)])]
    pallas_call x3 -> x6, Pallas kernels: 27.1 us -> 29.8 us  [the longest x1 11.9 us: body(): pl.pallas_call(forward, grid=(KV,), out_shape=[shape(TOK, KV * half), sha...]
    pallas_call x1, Pallas kernels: 0.27 us -> 1.96 us  [body(): pl.pallas_call(kv_pick, out_shape=[shape(ROWS, KV * PAIR)] * N_DP, in_spe...]
    unnamed x20 -> x16, local copies, waits for them, and re-layouts: 5.56 us -> 6.12 us
  transfers between devices with their start and end apart: 15 -> 17, of which waited for: 10 -> 6; matrix products, arithmetic and copies ran while one was open for 0% -> 0% of each run, Pallas kernels for 3% -> 18%
where the time goes in v1:
time: 108 us
  Pallas kernels  31.8 us (29%)
  blocking collectives  26.6 us (25%)
  waiting for transfers between devices  22.3 us (21%)
  starting transfers between devices  18.7 us (17%)
  local copies, waits for them, and re-layouts  6.41 us (6%)
  between operations  2.06 us (2%)
    all_to_all x1, blocking collectives, query_side(): return (dq_raw, lax.all_to_all(gains, ('dp', 'cp'), 0, 0, tiled=True))  26.6 us
    ppermute x8, waiting for transfers between devices, shifted(): lax.ppermute(array, 'cp', [(j, (j + by) % N_CP) for j in range(N_CP)])  19.2 us
    pallas_call x1, Pallas kernels, body(): pl.pallas_call(forward, grid=(KV,), out_shape=[shape(TOK, KV * half), sha...  11.9 us
    ppermute x9, starting transfers between devices, swap(): return lax.ppermute(array, 'dp', [(j, j ^ slot) for j in range(N_DP)])  10.7 us
    pallas_call x1, Pallas kernels, body(): pl.pallas_call(backward, grid=(KV,), out_shape=[shape(KEYS, KV * half), s...  8.56 us
    ppermute x8, starting transfers between devices, shifted(): lax.ppermute(array, 'cp', [(j, (j + by) % N_CP) for j in range(N_CP)])  7.96 us
    unnamed x16, local copies, waits for them, and re-layouts  6.12 us
    pallas_call x1, Pallas kernels, query_side(): pl.pallas_call(query_back, grid=(KV,), out_shape=[shape(TOK, KV * half),...  4.57 us
  transfers between devices with their start and end apart: 17, of which 6 were waited for; matrix products, arithmetic and copies ran while one was open for 0% of the time, Pallas kernels for 18%

profile of v1, /device:TPU:1, one launch (start us, length us, event | category | flops | bytes accessed | tf_op | source)
XLA Modules:
  0.0 107.9 jit_solution(4355820851505394546)
XLA Ops:
  0.6 0.0 copy-start.7
  0.6 0.0 copy-start.6
  0.7 2.0 %kv_pick.1 = (bf16[32,1024]{1,0:T(8,128)(2,1)}, bf16[32,1024]{1,0:T(8,128)(2,1)}, bf16[32,1024]{1,0:T(8,128)(2,1)}, bf16[32,1024]{1,0:T(8,128)(2,1)}) custom-call(s32[1,128]{1,0:T(1,128)} %order_ref.3, bf16[128,512]{1,0:T(8,128)(2,1)} %k_ref.1, bf16[128,512]{1,0:T(8,128)(2,1)} %v_ref.1), custom_call_target="tpu_custom_call" | custom-call | tf_op jit(solution)/shard_map/kv_pick/pallas_call | solution.py:350
  2.6 3.2 %collective-permute-start.3 = (bf16[32,1024]{1,0:T(8,128)(2,1)}, bf16[32,1024]{1,0:T(8,128)(2,1)S(1)}, u32[]{:S(2)}, u32[]{:S(2)}) collective-permute-start(bf16[32,1024]{1,0:T(8,128)(2,1)} %get-tuple-element.74), channel_id=1, source_target_pairs={{0,64},{64,0},{128,192},{192,128},{1,65},{65,1},{129,193},{193,129... | collective-permute-start | bytes 196616 | tf_op jit(solution)/shard_map/ppermute | solution.py:333
  5.9 0.0 collective-permute-start.4
  5.9 1.6 %collective-permute-start.5 = (bf16[32,1024]{1,0:T(8,128)(2,1)}, bf16[32,1024]{1,0:T(8,128)(2,1)S(1)}, u32[]{:S(2)}, u32[]{:S(2)}) collective-permute-start(bf16[32,1024]{1,0:T(8,128)(2,1)} %get-tuple-element.76), channel_id=1, source_target_pairs={{0,192},{64,128},{128,64},{192,0},{1,193},{65,129},{129,65},{193,1... | collective-permute-start | bytes 196616 | tf_op jit(solution)/shard_map/ppermute | solution.py:333
  8.1 0.0 collective-permute-done.3.rest_1_
  8.2 1.7 %collective-permute-done.4.rest_2_ = bf16[32,1024]{1,0:T(8,128)(2,1)S(1)} collective-permute-done((bf16[32,1024]{1,0:T(8,128)(2,1)}, bf16[32,1024]{1,0:T(8,128)(2,1)S(1)}, u32[]{:S(2)}, u32[]{:S(2)}) %collective-permute-start.4) | collective-permute-done | bytes 65568 | tf_op jit(solution)/shard_map/ppermute | solution.py:333
  9.8 1.5 %collective-permute-done.5.rest_3_ = bf16[32,1024]{1,0:T(8,128)(2,1)S(1)} collective-permute-done((bf16[32,1024]{1,0:T(8,128)(2,1)}, bf16[32,1024]{1,0:T(8,128)(2,1)S(1)}, u32[]{:S(2)}, u32[]{:S(2)}) %collective-permute-start.5) | collective-permute-done | bytes 65568 | tf_op jit(solution)/shard_map/ppermute | solution.py:333
  11.3 0.0 copy-start.4
  11.3 0.8 copy-done.4
  12.2 1.1 collective-permute-start.6
  13.2 1.3 %collective-permute-start.7 = (bf16[136,1024]{1,0:T(8,128)(2,1)S(1)}, bf16[136,1024]{1,0:T(8,128)(2,1)S(1)}, u32[]{:S(2)}, u32[]{:S(2)}) collective-permute-start(bf16[136,1024]{1,0:T(8,128)(2,1)S(1)} %kv_join.1.rest_1_.rest_4_), channel_id=1, source_target_pairs={{0,2},{1,3},{2,4},{3,5},{4,6},{5,7},{6,8},{7,9},{8,10},{9,11},{10,... | collective-permute-start | bytes 835592 | tf_op jit(solution)/shard_map/ppermute | solution.py:337
  14.5 0.0 copy-start
  14.5 1.2 %copy-done = bf16[128,4096]{1,0:T(8,128)(2,1)S(1)} copy-done((bf16[128,4096]{1,0:T(8,128)(2,1)S(1)}, bf16[128,4096]{1,0:T(8,128)(2,1)}, u32[]{:S(2)}) %copy-start) | copy-done | bytes 1048600
  15.8 0.0 copy-start.1
  15.8 1.2 %copy-done.1 = bf16[128,4096]{1,0:T(8,128)(2,1)S(1)} copy-done((bf16[128,4096]{1,0:T(8,128)(2,1)S(1)}, bf16[128,4096]{1,0:T(8,128)(2,1)}, u32[]{:S(2)}) %copy-start.1) | copy-done | bytes 1048600
  17.0 0.0 copy-start.5
  17.0 0.7 copy-done.5
  17.6 1.8 %qg_pick.1 = (bf16[32,4096]{1,0:T(8,128)(2,1)S(1)}, bf16[32,4096]{1,0:T(8,128)(2,1)S(1)}, bf16[32,4096]{1,0:T(8,128)(2,1)S(1)}, bf16[32,4096]{1,0:T(8,128)(2,1)S...) custom-call(s32[1,128]{1,0:T(1,128)S(1)} %copy-done.5, ...), custom_call_target="tpu_custom_call" | custom-call | tf_op jit(solution)/shard_map/qg_pick/pallas_call | solution.py:361
  19.4 1.0 collective-permute-start
  20.4 0.3 collective-permute-start.1
  20.7 1.4 %collective-permute-start.2 = (bf16[32,4096]{1,0:T(8,128)(2,1)S(1)}, bf16[32,4096]{1,0:T(8,128)(2,1)S(1)}, u32[]{:S(2)}, u32[]{:S(2)}) collective-permute-start(bf16[32,4096]{1,0:T(8,128)(2,1)S(1)} %get-tuple-element.71), channel_id=1, source_target_pairs={{0,192},{64,128},{128,64},{192,0},{1,193},{65,129},{129,65},{193,1... | collective-permute-start | bytes 786440 | tf_op jit(solution)/shard_map/ppermute | solution.py:333
  22.1 9.8 %collective-permute-done.6.rest_2_.rest_5_ = bf16[136,1024]{1,0:T(8,128)(2,1)S(1)} collective-permute-done((bf16[136,1024]{1,0:T(8,128)(2,1)S(1)}, bf16[136,1024]{1,0:T(8,128)(2,1)S(1)}, u32[]{:S(2)}, u32[]{:S(2)}) %collective-permute-start.6) | collective-permute-done | bytes 278560 | tf_op jit(solution)/shard_map/ppermute | solution.py:337
  31.9 0.0 collective-permute-start.8
  31.9 1.2 %collective-permute-done.7.rest_3_.rest_6_ = bf16[136,1024]{1,0:T(8,128)(2,1)S(1)} collective-permute-done((bf16[136,1024]{1,0:T(8,128)(2,1)S(1)}, bf16[136,1024]{1,0:T(8,128)(2,1)S(1)}, u32[]{:S(2)}, u32[]{:S(2)}) %collective-permute-start.7) | collective-permute-done | bytes 278560 | tf_op jit(solution)/shard_map/ppermute | solution.py:337
  33.1 0.0 collective-permute-start.9
  33.1 0.0 collective-permute-done.refs_1_
  33.1 1.4 %collective-permute-start.10 = (bf16[32,4096]{1,0:T(8,128)(2,1)S(1)}, bf16[32,4096]{1,0:T(8,128)(2,1)S(1)}, u32[]{:S(2)}, u32[]{:S(2)}) collective-permute-start(bf16[32,4096]{1,0:T(8,128)(2,1)S(1)} %get-tuple-element.83), channel_id=1, source_target_pairs={{0,64},{64,0},{128,192},{192,128},{1,65},{65,1},{129,193},{193,129... | collective-permute-start | bytes 786440 | tf_op jit(solution)/shard_map/ppermute | solution.py:333
  34.6 0.0 collective-permute-done.1.refs_2_
  34.6 0.3 collective-permute-start.11
  34.9 0.0 collective-permute-done.2.refs_3_
  34.9 1.4 %collective-permute-start.12 = (bf16[32,4096]{1,0:T(8,128)(2,1)S(1)}, bf16[32,4096]{1,0:T(8,128)(2,1)S(1)}, u32[]{:S(2)}, u32[]{:S(2)}) collective-permute-start(bf16[32,4096]{1,0:T(8,128)(2,1)S(1)} %get-tuple-element.85), channel_id=1, source_target_pairs={{0,192},{64,128},{128,64},{192,0},{1,193},{65,129},{129,65},{193,1... | collective-permute-start | bytes 786440 | tf_op jit(solution)/shard_map/ppermute | solution.py:333
  36.3 0.0 copy-start.2
  36.3 1.1 %copy-done.2 = f32[640,256]{1,0:T(8,128)S(1)} copy-done((f32[640,256]{1,0:T(8,128)S(1)}, f32[640,256]{1,0:T(8,128)}, u32[]{:S(2)}) %copy-start.2) | copy-done | bytes 655384
  37.4 0.0 copy-start.3
  37.4 1.1 %copy-done.3 = f32[128,1280]{1,0:T(8,128)S(1)} copy-done((f32[128,1280]{1,0:T(8,128)S(1)}, f32[128,1280]{1,0:T(8,128)}, u32[]{:S(2)}) %copy-start.3) | copy-done | bytes 655384
  38.5 1.2 %query_unit.1 = (f32[128,4096]{1,0:T(8,128)S(1)}, f32[8,4096]{1,0:T(8,128)S(1)}, f32[640,256]{1,0:T(8,128)S(1)}, f32[128,1280]{1,0:T(8,128)S(1)}) custom-call(bf16[32,4096]{1,0:T(8,128)(2,1)S(1)} %get-tuple-element.68.refs_0_, bf16[32,4096]{1,0:T(8,128)(2,1)S(1)} %collective-permute-done.refs_1_, bf16[32,4096]{1,0:T(8,128)(2,1)S(1)} %collective-permute-done.1.refs_2_, ...), custom_call_target="tpu_custom_call" | custom-call | tf_op jit(solution)/shard_map/query_unit/pallas_call | solution.py:402
  39.7 2.2 %collective-permute-done.8.rest_4_.rest_7_ = bf16[136,1024]{1,0:T(8,128)(2,1)S(1)} collective-permute-done((bf16[136,1024]{1,0:T(8,128)(2,1)S(1)}, bf16[136,1024]{1,0:T(8,128)(2,1)S(1)}, u32[]{:S(2)}, u32[]{:S(2)}) %collective-permute-start.8) | collective-permute-done | bytes 278560 | tf_op jit(solution)/shard_map/ppermute | solution.py:337
  41.9 6.0 %collective-permute-done.9.rest_5_.rest_8_ = bf16[136,1024]{1,0:T(8,128)(2,1)S(1)} collective-permute-done((bf16[136,1024]{1,0:T(8,128)(2,1)S(1)}, bf16[136,1024]{1,0:T(8,128)(2,1)S(1)}, u32[]{:S(2)}, u32[]{:S(2)}) %collective-permute-start.9) | collective-permute-done | bytes 278560 | tf_op jit(solution)/shard_map/ppermute | solution.py:337
  47.9 0.0 copy-done.7
  47.9 0.0 copy-done.6
  47.9 11.9 %forward.1 = (bf16[128,4096]{1,0:T(8,128)(2,1)}, bf16[128,4096]{1,0:T(8,128)(2,1)S(1)}, f32[640,4096]{1,0:T(8,128)S(1)}, bf16[128,4096]{1,0:T(8,128)(2,1)S(1)}, ...) custom-call(s32[1,1]{1,0:T(1,128)S(6)} %copy.24.doc_ref, ...), custom_call_target="tpu_custom_call" | custom-call | tf_op jit(solution)/shard_map/forward/pallas_call | solution.py:417
  59.8 0.0 collective-permute-done.10.rest_1_
  59.8 0.0 collective-permute-done.11.rest_2_
  59.8 0.0 collective-permute-done.12.rest_3_
  59.9 8.6 %backward.1 = (bf16[640,4096]{1,0:T(8,128)(2,1)S(1)}, f32[128,1024]{1,0:T(8,128)S(1)}, bf16[128,1024]{1,0:T(8,128)(2,1)}, bf16[128,1024]{1,0:T(8,128)(2,1)S(1)},...) custom-call(s32[1,1]{1,0:T(1,128)} %get-tuple-element.80.place_ref, ...), custom_call_target="tpu_custom_call" | custom-call | tf_op jit(solution)/shard_map/backward/pallas_call | solution.py:434
  68.4 0.0 collective-permute-start.13
  68.4 0.0 collective-permute-start.14
  68.4 2.4 %collective-permute-start.15 = (bf16[128,1024]{1,0:T(8,128)(2,1)S(1)}, bf16[128,1024]{1,0:T(8,128)(2,1)S(1)}, u32[]{:S(2)}, u32[]{:S(2)}) collective-permute-start(bf16[128,1024]{1,0:T(8,128)(2,1)S(1)} %get-tuple-element.97), channel_id=1, source_target_pairs={{0,61},{1,62},{2,63},{3,0},{4,1},{5,2},{6,3},{7,4},{8,5},{9,6},{10... | collective-permute-start | bytes 786440 | tf_op jit(solution)/shard_map/ppermute | solution.py:337
  70.8 3.2 %collective-permute-start.16 = (bf16[128,1024]{1,0:T(8,128)(2,1)S(1)}, bf16[128,1024]{1,0:T(8,128)(2,1)S(1)}, u32[]{:S(2)}, u32[]{:S(2)}) collective-permute-start(bf16[128,1024]{1,0:T(8,128)(2,1)S(1)} %get-tuple-element.98), channel_id=1, source_target_pairs={{0,60},{1,61},{2,62},{3,63},{4,0},{5,1},{6,2},{7,3},{8,4},{9,5},{1... | collective-permute-start | bytes 786440 | tf_op jit(solution)/shard_map/ppermute | solution.py:337
  74.6 31.5 %conditional.1 = (bf16[128,4096]{1,0:T(8,128)(2,1)}, f32[256,256]{1,0:T(8,128)S(1)}) conditional(s32[]{:T(128)} %bitcast.3, () %tuple.16, (s32[1,1]{1,0:T(1,128)}, f32[128,4096]{1,0:T(8,128)S(1)}, f32[8,4096]{1,0:T(8,128)S(1)}, bf16[640,4096]{1,0:T(8,128)(2,1)S(1)}, bf16[640,512]{1,0:T(8,128)(2,1)S(1)}, /*index=5*/f32[128,1280]{1,0:T(8,128)S(1)}, ...), branch_computations={%region_0.0_spmd, %region_1.0_spmd} | conditional | bytes 1572880 | solution.py:475
  74.7 4.6 %query_back.1 = (bf16[128,4096]{1,0:T(8,128)(2,1)}, f32[256,256]{1,0:T(8,128)S(1)}) custom-call(s32[1,1]{1,0:T(1,128)} %get-tuple-element.16.place_ref, f32[128,4096]{1,0:T(8,128)S(1)} %get-tuple-element.17.unit_ref, f32[8,4096]{1,0:T(8,128)S(1)} %get-tuple-element.18.norm_ref, bf16[640,4096]{1,0:T(8,128)(2,1)S(1)} %get-tuple-element.19.ds_ref, ...), custom_call_target="tpu_custom_call" | custom-call | tf_op jit(solution)/shard_map/cond/branch_1_fun/query_back/pallas_call | solution.py:458
  79.2 0.3 copy.16
  79.5 26.6 %all_to_all.9 = f32[256,1,256]{2,1,0:T(1,128)S(1)} all-to-all(f32[256,1,256]{2,1,0:T(1,128)S(1)} %copy.16), channel_id=1, replica_groups=mesh['dp'=4,'cp'=64] {'dp','cp'}, dimensions={0} | all-to-all | bytes 524288 | tf_op jit(solution)/shard_map/cond/branch_1_fun/all_to_all | solution.py:470
  106.1 0.0 collective-permute-done.13.rest_0_
  106.1 0.0 collective-permute-done.14.rest_1_
  106.1 0.0 collective-permute-done.15.rest_2_
  106.2 0.0 collective-permute-done.16.rest_3_
  106.2 1.8 %finish.1 = (bf16[128,512]{1,0:T(8,128)(2,1)}, bf16[128,512]{1,0:T(8,128)(2,1)}, f32[1,128]{1,0:T(1,128)}, f32[1,128]{1,0:T(1,128)}) custom-call(s32[1,1]{1,0:T(1,128)} %get-tuple-element.80.place_ref, f32[128,1024]{1,0:T(8,128)S(1)} %get-tuple-element.94.own_ref, bf16[128,1024]{1,0:T(8,128)(2,1)S(1)} %collective-permute-done.13.rest_0_, ...), custom_call_target="tpu_custom_call" | custom-call | tf_op jit(solution)/shard_map/finish/pallas_call | solution.py:478
  (2 shorter events, 0.0 us)
Async XLA Ops:
  0.6 47.3 %copy-start.7 = (f32[128]{0:T(128)S(1)}, f32[128]{0:T(128)}, u32[]{:S(2)}) copy-start(f32[128]{0:T(128)} %param.18) | copy-start | bytes 1540
  0.6 47.3 %copy-start.6 = (f32[128]{0:T(128)S(1)}, f32[128]{0:T(128)}, u32[]{:S(2)}) copy-start(f32[128]{0:T(128)} %param.19) | copy-start | bytes 1540
  2.6 5.5 %collective-permute-start.3 = (bf16[32,1024]{1,0:T(8,128)(2,1)}, bf16[32,1024]{1,0:T(8,128)(2,1)S(1)}, u32[]{:S(2)}, u32[]{:S(2)}) collective-permute-start(bf16[32,1024]{1,0:T(8,128)(2,1)} %get-tuple-element.74), channel_id=1, source_target_pairs={{0,64},{64,0},{128,192},{192,128},{1,65},{65,1},{129,193},{193,129... | collective-permute-start | bytes 196616 | tf_op jit(solution)/shard_map/ppermute | solution.py:333
  5.9 4.0 %collective-permute-start.4 = (bf16[32,1024]{1,0:T(8,128)(2,1)}, bf16[32,1024]{1,0:T(8,128)(2,1)S(1)}, u32[]{:S(2)}, u32[]{:S(2)}) collective-permute-start(bf16[32,1024]{1,0:T(8,128)(2,1)} %get-tuple-element.75), channel_id=1, source_target_pairs={{0,128},{64,192},{128,0},{192,64},{1,129},{65,193},{129,1},{193,65... | collective-permute-start | bytes 196616 | tf_op jit(solution)/shard_map/ppermute | solution.py:333
  5.9 5.4 %collective-permute-start.5 = (bf16[32,1024]{1,0:T(8,128)(2,1)}, bf16[32,1024]{1,0:T(8,128)(2,1)S(1)}, u32[]{:S(2)}, u32[]{:S(2)}) collective-permute-start(bf16[32,1024]{1,0:T(8,128)(2,1)} %get-tuple-element.76), channel_id=1, source_target_pairs={{0,192},{64,128},{128,64},{192,0},{1,193},{65,129},{129,65},{193,1... | collective-permute-start | bytes 196616 | tf_op jit(solution)/shard_map/ppermute | solution.py:333
  11.3 0.8 copy-start.4
  12.2 19.7 %collective-permute-start.6 = (bf16[136,1024]{1,0:T(8,128)(2,1)S(1)}, bf16[136,1024]{1,0:T(8,128)(2,1)S(1)}, u32[]{:S(2)}, u32[]{:S(2)}) collective-permute-start(bf16[136,1024]{1,0:T(8,128)(2,1)S(1)} %kv_join.1.rest_1_.rest_4_), channel_id=1, source_target_pairs={{0,1},{1,2},{2,3},{3,4},{4,5},{5,6},{6,7},{7,8},{8,9},{9,10},{10,1... | collective-permute-start | bytes 835592 | tf_op jit(solution)/shard_map/ppermute | solution.py:337
  13.2 19.9 %collective-permute-start.7 = (bf16[136,1024]{1,0:T(8,128)(2,1)S(1)}, bf16[136,1024]{1,0:T(8,128)(2,1)S(1)}, u32[]{:S(2)}, u32[]{:S(2)}) collective-permute-start(bf16[136,1024]{1,0:T(8,128)(2,1)S(1)} %kv_join.1.rest_1_.rest_4_), channel_id=1, source_target_pairs={{0,2},{1,3},{2,4},{3,5},{4,6},{5,7},{6,8},{7,9},{8,10},{9,11},{10,... | collective-permute-start | bytes 835592 | tf_op jit(solution)/shard_map/ppermute | solution.py:337
  14.5 1.2 %copy-start = (bf16[128,4096]{1,0:T(8,128)(2,1)S(1)}, bf16[128,4096]{1,0:T(8,128)(2,1)}, u32[]{:S(2)}) copy-start(bf16[128,4096]{1,0:T(8,128)(2,1)} %q_ref.1) | copy-start | bytes 3145732
  15.8 1.2 %copy-start.1 = (bf16[128,4096]{1,0:T(8,128)(2,1)S(1)}, bf16[128,4096]{1,0:T(8,128)(2,1)}, u32[]{:S(2)}) copy-start(bf16[128,4096]{1,0:T(8,128)(2,1)} %g_ref.1) | copy-start | bytes 3145732
  17.0 0.7 copy-start.5
  19.4 13.7 %collective-permute-start = (bf16[32,4096]{1,0:T(8,128)(2,1)S(1)}, bf16[32,4096]{1,0:T(8,128)(2,1)S(1)}, u32[]{:S(2)}, u32[]{:S(2)}) collective-permute-start(bf16[32,4096]{1,0:T(8,128)(2,1)S(1)} %get-tuple-element.69), channel_id=1, source_target_pairs={{0,64},{64,0},{128,192},{192,128},{1,65},{65,1},{129,193},{193,129... | collective-permute-start | bytes 786440 | tf_op jit(solution)/shard_map/ppermute | solution.py:333
  20.4 14.2 %collective-permute-start.1 = (bf16[32,4096]{1,0:T(8,128)(2,1)S(1)}, bf16[32,4096]{1,0:T(8,128)(2,1)S(1)}, u32[]{:S(2)}, u32[]{:S(2)}) collective-permute-start(bf16[32,4096]{1,0:T(8,128)(2,1)S(1)} %get-tuple-element.70), channel_id=1, source_target_pairs={{0,128},{64,192},{128,0},{192,64},{1,129},{65,193},{129,1},{193,65... | collective-permute-start | bytes 786440 | tf_op jit(solution)/shard_map/ppermute | solution.py:333
  20.7 14.2 %collective-permute-start.2 = (bf16[32,4096]{1,0:T(8,128)(2,1)S(1)}, bf16[32,4096]{1,0:T(8,128)(2,1)S(1)}, u32[]{:S(2)}, u32[]{:S(2)}) collective-permute-start(bf16[32,4096]{1,0:T(8,128)(2,1)S(1)} %get-tuple-element.71), channel_id=1, source_target_pairs={{0,192},{64,128},{128,64},{192,0},{1,193},{65,129},{129,65},{193,1... | collective-permute-start | bytes 786440 | tf_op jit(solution)/shard_map/ppermute | solution.py:333
  31.9 10.0 %collective-permute-start.8 = (bf16[136,1024]{1,0:T(8,128)(2,1)S(1)}, bf16[136,1024]{1,0:T(8,128)(2,1)S(1)}, u32[]{:S(2)}, u32[]{:S(2)}) collective-permute-start(bf16[136,1024]{1,0:T(8,128)(2,1)S(1)} %collective-permute-done.6.rest_2_.rest_5_), channel_id=1, source_target_pairs={{0,2},{1,3},{2,4},{3,5},{4,6},{5,7},{6,8},{7,9},{8,10},{9,11},{10,... | collective-permute-start | bytes 835592 | tf_op jit(solution)/shard_map/ppermute | solution.py:337
  33.1 14.8 %collective-permute-start.9 = (bf16[136,1024]{1,0:T(8,128)(2,1)S(1)}, bf16[136,1024]{1,0:T(8,128)(2,1)S(1)}, u32[]{:S(2)}, u32[]{:S(2)}) collective-permute-start(bf16[136,1024]{1,0:T(8,128)(2,1)S(1)} %collective-permute-done.7.rest_3_.rest_6_), channel_id=1, source_target_pairs={{0,2},{1,3},{2,4},{3,5},{4,6},{5,7},{6,8},{7,9},{8,10},{9,11},{10,... | collective-permute-start | bytes 835592 | tf_op jit(solution)/shard_map/ppermute | solution.py:337
  33.1 26.7 %collective-permute-start.10 = (bf16[32,4096]{1,0:T(8,128)(2,1)S(1)}, bf16[32,4096]{1,0:T(8,128)(2,1)S(1)}, u32[]{:S(2)}, u32[]{:S(2)}) collective-permute-start(bf16[32,4096]{1,0:T(8,128)(2,1)S(1)} %get-tuple-element.83), channel_id=1, source_target_pairs={{0,64},{64,0},{128,192},{192,128},{1,65},{65,1},{129,193},{193,129... | collective-permute-start | bytes 786440 | tf_op jit(solution)/shard_map/ppermute | solution.py:333
  34.6 25.3 %collective-permute-start.11 = (bf16[32,4096]{1,0:T(8,128)(2,1)S(1)}, bf16[32,4096]{1,0:T(8,128)(2,1)S(1)}, u32[]{:S(2)}, u32[]{:S(2)}) collective-permute-start(bf16[32,4096]{1,0:T(8,128)(2,1)S(1)} %get-tuple-element.84), channel_id=1, source_target_pairs={{0,128},{64,192},{128,0},{192,64},{1,129},{65,193},{129,1},{193,65... | collective-permute-start | bytes 786440 | tf_op jit(solution)/shard_map/ppermute | solution.py:333
  34.9 24.9 %collective-permute-start.12 = (bf16[32,4096]{1,0:T(8,128)(2,1)S(1)}, bf16[32,4096]{1,0:T(8,128)(2,1)S(1)}, u32[]{:S(2)}, u32[]{:S(2)}) collective-permute-start(bf16[32,4096]{1,0:T(8,128)(2,1)S(1)} %get-tuple-element.85), channel_id=1, source_target_pairs={{0,192},{64,128},{128,64},{192,0},{1,193},{65,129},{129,65},{193,1... | collective-permute-start | bytes 786440 | tf_op jit(solution)/shard_map/ppermute | solution.py:333
  36.3 1.1 %copy-start.2 = (f32[640,256]{1,0:T(8,128)S(1)}, f32[640,256]{1,0:T(8,128)}, u32[]{:S(2)}) copy-start(f32[640,256]{1,0:T(8,128)} %constant.11.clone.refs_4_) | copy-start | bytes 1966084
  37.4 1.1 %copy-start.3 = (f32[128,1280]{1,0:T(8,128)S(1)}, f32[128,1280]{1,0:T(8,128)}, u32[]{:S(2)}) copy-start(f32[128,1280]{1,0:T(8,128)} %constant.12.clone.refs_5_) | copy-start | bytes 1966084
  68.4 37.7 %collective-permute-start.13 = (bf16[128,1024]{1,0:T(8,128)(2,1)}, bf16[128,1024]{1,0:T(8,128)(2,1)S(1)}, u32[]{:S(2)}, u32[]{:S(2)}) collective-permute-start(bf16[128,1024]{1,0:T(8,128)(2,1)} %get-tuple-element.95), channel_id=1, source_target_pairs={{0,63},{1,0},{2,1},{3,2},{4,3},{5,4},{6,5},{7,6},{8,7},{9,8},{10,9... | collective-permute-start | bytes 786440 | tf_op jit(solution)/shard_map/ppermute | solution.py:337
  68.4 37.7 %collective-permute-start.14 = (bf16[128,1024]{1,0:T(8,128)(2,1)S(1)}, bf16[128,1024]{1,0:T(8,128)(2,1)S(1)}, u32[]{:S(2)}, u32[]{:S(2)}) collective-permute-start(bf16[128,1024]{1,0:T(8,128)(2,1)S(1)} %get-tuple-element.96), channel_id=1, source_target_pairs={{0,62},{1,63},{2,0},{3,1},{4,2},{5,3},{6,4},{7,5},{8,6},{9,7},{10,... | collective-permute-start | bytes 786440 | tf_op jit(solution)/shard_map/ppermute | solution.py:337
  68.4 37.7 %collective-permute-start.15 = (bf16[128,1024]{1,0:T(8,128)(2,1)S(1)}, bf16[128,1024]{1,0:T(8,128)(2,1)S(1)}, u32[]{:S(2)}, u32[]{:S(2)}) collective-permute-start(bf16[128,1024]{1,0:T(8,128)(2,1)S(1)} %get-tuple-element.97), channel_id=1, source_target_pairs={{0,61},{1,62},{2,63},{3,0},{4,1},{5,2},{6,3},{7,4},{8,5},{9,6},{10... | collective-permute-start | bytes 786440 | tf_op jit(solution)/shard_map/ppermute | solution.py:337
  70.8 35.4 %collective-permute-start.16 = (bf16[128,1024]{1,0:T(8,128)(2,1)S(1)}, bf16[128,1024]{1,0:T(8,128)(2,1)S(1)}, u32[]{:S(2)}, u32[]{:S(2)}) collective-permute-start(bf16[128,1024]{1,0:T(8,128)(2,1)S(1)} %get-tuple-element.98), channel_id=1, source_target_pairs={{0,60},{1,61},{2,62},{3,63},{4,0},{5,1},{6,2},{7,3},{8,4},{9,5},{1... | collective-permute-start | bytes 786440 | tf_op jit(solution)/shard_map/ppermute | solution.py:337

commit v2 on v1

--- a/solution.py
+++ b/solution.py
@@ -21,10 +21,11 @@
 ROWS = TOK // N_DP
 KEYS = (REACH + 1) * TOK
 ID_ROWS = 8
-TILE = 256
+TILE = 512
 LAG = 1
 PAIR = 2 * DIM
 WIDE = 2 * GROUP * DIM
+HALF = GROUP * DIM
 INV_ROOT = 1.0 / math.sqrt(DIM)
 LOG2E = 1.4426950408889634
 BF = jnp.bfloat16
@@ -106,6 +107,10 @@
     first = pl.multiple_of(block * TOK, TOK)
     second = pl.multiple_of(block * TOK + KEYS, TOK)
     return table_ref[:, pl.ds(first, TOK)], table_ref[:, pl.ds(second, TOK)]
+
+
+def columns(head, width, at=0, size=None):
+    return pl.ds(pl.multiple_of(head * width + at, DIM), width if size is None else size)
 
 
 def half_swap(array):
@@ -155,65 +160,68 @@
     gain_q = jnp.broadcast_to(gq_ref[...], (TOK, DIM)).T
     gain_k = gk_ref[...]
     own_cos, own_sin = flip_angles(flip_ref, block)
-    key_rot, key_val = [], []
-    for at, back in enumerate(range(REACH, -1, -1)):
-        cosine, sine = angles_of(table_ref, jnp.maximum(block - back, 0))
-        unit, _ = unit_of(shards[back][:TOK, :DIM].astype(F32))
-        turned = turn(unit * gain_k, cosine, sine).astype(BF)
-        unit_ref[blocks[at], :] = unit
-        rot_ref[blocks[at], :] = turned
-        key_rot.append(turned)
-        key_val.append(shards[back][:TOK, DIM:])
-    rot_f = jnp.concatenate(key_rot, axis=0)
-    val_t = jnp.concatenate(key_val, axis=0).T
     levels = [jnp.where(flags[back - 1] > 0, 0.0, NEGATIVE) for back in range(REACH, 0, -1)]
     key = lax.broadcasted_iota(jnp.int32, (TOK, TILE), 0)
     query = lax.broadcasted_iota(jnp.int32, (TOK, TILE), 1) & (TOK - 1)
     causal = key <= query
-    heads = TILE // TOK
-
-    def ready(first):
-        places = [(first + j) * DIM for j in range(heads)]
-        turned = []
-        for at in places:
-            scaled = unitq_ref[:, at : at + DIM] * gain_q
-            query_t = scaled * own_cos + half_swap(scaled) * own_sin
-            turned.append(query_t.astype(BF))
-            query_ref[:, at : at + DIM] = query_t.T.astype(BF)
-        return places, dot(rot_f, jnp.concatenate(turned, axis=1), 1, 0)
-
-    def soft(state):
-        places, scores = state
-        last = jnp.where(causal, scores[blocks[REACH]], NEGATIVE)
-        parts = [scores[blocks[at]] for at in range(REACH)] + [last]
-        tops = [jnp.max(part, axis=0, keepdims=True) for part in parts]
-        top = tops[REACH]
-        for at in range(REACH):
-            top = jnp.maximum(top, tops[at] + levels[at])
-        top = top * (INV_ROOT * LOG2E)
-        weights, total = [], 0.0
-        for at in range(REACH + 1):
-            shift = top if at == REACH else top - levels[at]
-            weight = jnp.exp2(parts[at] * (INV_ROOT * LOG2E) - shift)
-            total = total + jnp.sum(weight, axis=0, keepdims=True)
-            weights.append(weight)
-        inverse = 1.0 / total
-        for at in range(REACH + 1):
-            prob_ref[blocks[at], places[0] : places[0] + TILE] = weights[at] * inverse
-        weights = jnp.concatenate(weights, axis=0).astype(BF)
-        out_t = dot(val_t, weights, 1, 0) / total
-        for j, at in enumerate(places):
-            out = out_t[:, j * TOK : (j + 1) * TOK].T.astype(BF)
-            out_ref[:, at : at + DIM] = out
-            again_ref[:, at : at + DIM] = out
-
-    count = GROUP // heads
-    states = {}
-    for turn_at in range(count + LAG):
-        if turn_at < count:
-            states[turn_at] = ready(turn_at * heads)
-        if turn_at >= LAG:
-            soft(states.pop(turn_at - LAG))
+
+    @pl.loop(0, KV)
+    def each(head):
+        key_rot, key_val = [], []
+        for at, back in enumerate(range(REACH, -1, -1)):
+            cosine, sine = angles_of(table_ref, jnp.maximum(block - back, 0))
+            unit, _ = unit_of(shards[back][:TOK, columns(head, PAIR, 0, DIM)].astype(F32))
+            turned = turn(unit * gain_k, cosine, sine).astype(BF)
+            unit_ref[blocks[at], columns(head, DIM)] = unit
+            rot_ref[blocks[at], columns(head, DIM)] = turned
+            key_rot.append(turned)
+            key_val.append(shards[back][:TOK, columns(head, PAIR, DIM, DIM)])
+        rot_f = jnp.concatenate(key_rot, axis=0)
+        val_t = jnp.concatenate(key_val, axis=0).T
+        heads = TILE // TOK
+
+        def ready(first):
+            places = [(first + j) * DIM for j in range(heads)]
+            turned = []
+            for at in places:
+                scaled = unitq_ref[:, columns(head, HALF, at, DIM)] * gain_q
+                query_t = scaled * own_cos + half_swap(scaled) * own_sin
+                turned.append(query_t.astype(BF))
+                query_ref[:, columns(head, HALF, at, DIM)] = query_t.T.astype(BF)
+            return places, dot(rot_f, jnp.concatenate(turned, axis=1), 1, 0)
+
+        def soft(state):
+            places, scores = state
+            last = jnp.where(causal, scores[blocks[REACH]], NEGATIVE)
+            parts = [scores[blocks[at]] for at in range(REACH)] + [last]
+            tops = [jnp.max(part, axis=0, keepdims=True) for part in parts]
+            top = tops[REACH]
+            for at in range(REACH):
+                top = jnp.maximum(top, tops[at] + levels[at])
+            top = top * (INV_ROOT * LOG2E)
+            weights, total = [], 0.0
+            for at in range(REACH + 1):
+                shift = top if at == REACH else top - levels[at]
+                weight = jnp.exp2(parts[at] * (INV_ROOT * LOG2E) - shift)
+                total = total + jnp.sum(weight, axis=0, keepdims=True)
+                weights.append(weight)
+            inverse = 1.0 / total
+            for at in range(REACH + 1):
+                prob_ref[blocks[at], columns(head, HALF, places[0], TILE)] = weights[at] * inverse
+            weights = jnp.concatenate(weights, axis=0).astype(BF)
+            out_t = dot(val_t, weights, 1, 0) / total
+            for j, at in enumerate(places):
+                out = out_t[:, j * TOK : (j + 1) * TOK].T.astype(BF)
+                out_ref[:, columns(head, HALF, at, DIM)] = out
+                again_ref[:, columns(head, HALF, at, DIM)] = out
+
+        count = GROUP // heads
+        states = {}
+        for turn_at in range(count + LAG):
+            if turn_at < count:
+                states[turn_at] = ready(turn_at * heads)
+            if turn_at >= LAG:
+                soft(states.pop(turn_at - LAG))
 
 
 def backward(place_ref, *rest):
@@ -226,87 +234,83 @@
     gain_ref, rows_ref = outs[2 + REACH :]
     block = place_ref[0, 0]
 
-    @pl.when(pl.program_id(0) == 0)
-    def start():
-        gain_ref[...] = jnp.zeros_like(gain_ref)
-
-    for slot in range(N_DP):
-        rows_ref[slot_rows(slot), :] = slots[slot][...]
-    val_b = jnp.concatenate([shards[back][:TOK, DIM:] for back in range(REACH, -1, -1)], axis=0)
-    heads = TILE // TOK
-
-    def ready(first):
-        places = [(first + j) * DIM for j in range(heads)]
-        grads = [rows_ref[:, at : at + DIM] for at in places]
-        grad = jnp.concatenate(grads, axis=0)
-        deltas = []
-        for at, own in zip(places, grads):
-            both = own.astype(F32) * out_ref[:, at : at + DIM].astype(F32)
-            deltas.append(jnp.sum(both.T, axis=0, keepdims=True))
-        return places, grad, jnp.concatenate(deltas, axis=1), dot(val_b, grad, 1, 1)
-
-    def back(state, sums):
-        places, grad, delta, dprob = state
-        span = slice(places[0], places[0] + TILE)
-        probs = prob_ref[:, span]
-        dscore = (probs * (dprob - delta)).astype(BF)
-        ds_ref[:, span] = dscore
-        query = jnp.concatenate([query_ref[:, at : at + DIM] for at in places], axis=0)
-        dk = dot(dscore, query, 1, 0)
-        dv = dot(probs.astype(BF), grad, 1, 0)
-        return (dk, dv) if sums is None else (sums[0] + dk, sums[1] + dv)
-
-    count = GROUP // heads
-    states, sums = {}, None
-    for turn_at in range(count + LAG):
-        if turn_at < count:
-            states[turn_at] = ready(turn_at * heads)
-        if turn_at >= LAG:
-            sums = back(states.pop(turn_at - LAG), sums)
-    dk_total, dv_total = sums
-    gk_total = jnp.zeros((8, DIM), F32)
-    for at, back_by in enumerate(range(REACH, -1, -1)):
-        cosine, sine = angles_of(table_ref, jnp.maximum(block - back_by, 0))
-        dk_part = dk_total[blocks[at]] * INV_ROOT
-        dkn = turn_back(dk_part, cosine, sine)
-        gk_total = gk_total + jnp.sum((dkn * unit_ref[blocks[at], :]).reshape(TOK // 8, 8, DIM), axis=0)
-        target = own_ref if back_by == 0 else part_refs[back_by - 1]
-        target[:, :DIM] = dk_part.astype(target.dtype)
-        target[:, DIM:] = dv_total[blocks[at]].astype(target.dtype)
-    gain_ref[...] += gk_total
+    gain_ref[...] = jnp.zeros_like(gain_ref)
+
+    @pl.loop(0, KV)
+    def each(head):
+        for slot in range(N_DP):
+            rows_ref[slot_rows(slot), :] = slots[slot][:, columns(head, HALF)]
+        val_b = jnp.concatenate([shards[back][:TOK, columns(head, PAIR, DIM, DIM)] for back in range(REACH, -1, -1)], axis=0)
+        heads = TILE // TOK
+
+        def ready(first):
+            places = [(first + j) * DIM for j in range(heads)]
+            grads = [rows_ref[:, at : at + DIM] for at in places]
+            grad = jnp.concatenate(grads, axis=0)
+            deltas = []
+            for at, own in zip(places, grads):
+                both = own.astype(F32) * out_ref[:, columns(head, HALF, at, DIM)].astype(F32)
+                deltas.append(jnp.sum(both.T, axis=0, keepdims=True))
+            return places, grad, jnp.concatenate(deltas, axis=1), dot(val_b, grad, 1, 1)
+
+        def back(state, sums):
+            places, grad, delta, dprob = state
+            span = columns(head, HALF, places[0], TILE)
+            probs = prob_ref[:, span]
+            dscore = (probs * (dprob - delta)).astype(BF)
+            ds_ref[:, span] = dscore
+            query = jnp.concatenate([query_ref[:, columns(head, HALF, at, DIM)] for at in places], axis=0)
+            dk = dot(dscore, query, 1, 0)
+            dv = dot(probs.astype(BF), grad, 1, 0)
+            return (dk, dv) if sums is None else (sums[0] + dk, sums[1] + dv)
+
+        count = GROUP // heads
+        states, sums = {}, None
+        for turn_at in range(count + LAG):
+            if turn_at < count:
+                states[turn_at] = ready(turn_at * heads)
+            if turn_at >= LAG:
+                sums = back(states.pop(turn_at - LAG), sums)
+        dk_total, dv_total = sums
+        gk_total = jnp.zeros((8, DIM), F32)
+        for at, back_by in enumerate(range(REACH, -1, -1)):
+            cosine, sine = angles_of(table_ref, jnp.maximum(block - back_by, 0))
+            dk_part = dk_total[blocks[at]] * INV_ROOT
+            dkn = turn_back(dk_part, cosine, sine)
+            gk_total = gk_total + jnp.sum((dkn * unit_ref[blocks[at], columns(head, DIM)]).reshape(TOK // 8, 8, DIM), axis=0)
+            target = own_ref if back_by == 0 else part_refs[back_by - 1]
+            target[:, columns(head, PAIR, 0, DIM)] = dk_part.astype(target.dtype)
+            target[:, columns(head, PAIR, DIM, DIM)] = dv_total[blocks[at]].astype(target.dtype)
+        gain_ref[...] += gk_total
 
 
 def query_back(place_ref, unit_ref, norm_ref, ds_ref, rot_ref, flip_ref, gq_ref, gk_ref, dq_ref, gain_ref, sum_ref):
-    step = pl.program_id(0)
-
-    @pl.when(step == 0)
-    def start():
-        sum_ref[...] = jnp.zeros_like(sum_ref)
-
+    sum_ref[...] = jnp.zeros_like(sum_ref)
     gain_q = jnp.broadcast_to(gq_ref[...], (TOK, DIM)).T
     cosine, sine = flip_angles(flip_ref, place_ref[0, 0])
-    rot_t = rot_ref[...].T
-    total = jnp.zeros((DIM, TOK), F32)
-    for first in range(0, GROUP * DIM, TILE):
-        both = dot(rot_t, ds_ref[:, first : first + TILE], 1, 0) * INV_ROOT
-        for at in range(first, first + TILE, TOK):
-            dq_t = both[:, at - first : at - first + TOK]
-            unit = unit_ref[:, at : at + DIM]
-            dqn = dq_t * cosine - half_swap(dq_t) * sine
-            total = total + dqn * unit
-            scaled = dqn * gain_q
-            inner = jnp.mean(scaled * unit, axis=0, keepdims=True)
-            back = norm_ref[0:1, at : at + DIM] * (scaled - unit * inner)
-            dq_ref[:, at : at + DIM] = back.T.astype(BF)
-    sum_ref[...] += total
-
-    @pl.when(step == KV - 1)
-    def end():
-        spread = (N_DP * N_CP, DIM)
-        by_query = jnp.sum(sum_ref[...].T, axis=0, keepdims=True)
-        by_key = jnp.sum(gk_ref[...], axis=0, keepdims=True)
-        gain_ref[:, :DIM] = jnp.broadcast_to(by_query, spread)
-        gain_ref[:, DIM:] = jnp.broadcast_to(by_key, spread)
+
+    @pl.loop(0, KV)
+    def each(head):
+        rot_t = rot_ref[:, columns(head, DIM)].T
+        total = jnp.zeros((DIM, TOK), F32)
+        for first in range(0, GROUP * DIM, TILE):
+            both = dot(rot_t, ds_ref[:, columns(head, HALF, first, TILE)], 1, 0) * INV_ROOT
+            for at in range(first, first + TILE, TOK):
+                dq_t = both[:, at - first : at - first + TOK]
+                unit = unit_ref[:, columns(head, HALF, at, DIM)]
+                dqn = dq_t * cosine - half_swap(dq_t) * sine
+                total = total + dqn * unit
+                scaled = dqn * gain_q
+                inner = jnp.mean(scaled * unit, axis=0, keepdims=True)
+                back = norm_ref[0:1, columns(head, HALF, at, DIM)] * (scaled - unit * inner)
+                dq_ref[:, columns(head, HALF, at, DIM)] = back.T.astype(BF)
+        sum_ref[...] += total
+
+    spread = (8, DIM)
+    by_query = jnp.sum(sum_ref[...].T, axis=0, keepdims=True)
+    by_key = jnp.sum(gk_ref[...], axis=0, keepdims=True)
+    gain_ref[:, :DIM] = jnp.broadcast_to(by_query, spread)
+    gain_ref[:, DIM:] = jnp.broadcast_to(by_key, spread)
 
 
 def finish(place_ref, own_ref, *rest):
@@ -381,8 +385,7 @@
         name="kv_join",
     )(doc_blocks, *kv_slots)
     one = shifted(kv_own, 1)
-    two = shifted(kv_own, 2)
-    shards = [kv_own, one, two, shifted(one, 2), shifted(two, 2)]
+    shards = [kv_own, one, shifted(kv_own, 2), shifted(one, 2), shifted(kv_own, 4)]
     q_slots = [picked[0]] + [swap(picked[slot], slot) for slot in range(1, N_DP)]
     g_slots = [picked[N_DP]] + [swap(picked[N_DP + slot], slot) for slot in range(1, N_DP)]
     whole = lambda h: (0, 0)
@@ -416,7 +419,6 @@
     )(*q_slots, table, flipped)
     attn_out, out_again, probs, queries, keys_rot, keys_unit, place = pl.pallas_call(
         forward,
-        grid=(KV,),
         out_shape=[
             shape(TOK, KV * half),
             shape(TOK, KV * half),
@@ -426,25 +428,18 @@
             shape(KEYS, KV * DIM, dtype=F32),
             shape(1, 1, dtype=jnp.int32),
         ],
-        in_specs=[SMEM, rows_spec] + shard_specs + table_specs + flip_specs + [gain_spec] * 2,
-        out_specs=[rows_spec, rows_spec, square_spec, rows_spec, keys_spec, keys_spec, SMEM],
+        in_specs=[SMEM] + [VMEM] * (REACH + 6),
+        out_specs=[VMEM] * 6 + [SMEM],
         compiler_params=PARAMS,
         name="forward",
     )(doc_blocks, units, *shards, table, flipped, gain_q, gain_k)
     results = pl.pallas_call(
         backward,
-        grid=(KV,),
         out_shape=[shape(KEYS, KV * half), shape(TOK, KV * PAIR, dtype=F32)]
         + [shape(TOK, KV * PAIR)] * REACH
         + [shape(8, DIM, dtype=F32)],
-        in_specs=[SMEM]
-        + slot_specs
-        + shard_specs
-        + [rows_spec, square_spec, rows_spec, keys_spec]
-        + table_specs,
-        out_specs=[square_spec, pl.BlockSpec((TOK, PAIR), by_head)]
-        + [pl.BlockSpec((TOK, PAIR), by_head)] * REACH
-        + [pl.BlockSpec((8, DIM), whole)],
+        in_specs=[SMEM] + [VMEM] * (N_DP + REACH + 6),
+        out_specs=[VMEM] * (3 + REACH),
         scratch_shapes=[pltpu.VMEM((TOK, half), BF)],
         compiler_params=PARAMS,
         name="backward",
@@ -457,20 +452,25 @@
         place, units, norms, dscores, keys_rot, gk_rows = operands
         dq_raw, gains = pl.pallas_call(
             query_back,
-            grid=(KV,),
-            out_shape=[shape(TOK, KV * half), shape(N_DP * N_CP, 2 * DIM, dtype=F32)],
-            in_specs=[SMEM, rows_spec, norm_spec, square_spec, keys_spec]
-            + flip_specs
-            + [gain_spec, pl.BlockSpec((8, DIM), whole)],
-            out_specs=[rows_spec, pl.BlockSpec((N_DP * N_CP, 2 * DIM), whole)],
+            out_shape=[shape(TOK, KV * half), shape(8, 2 * DIM, dtype=F32)],
+            in_specs=[SMEM] + [VMEM] * 7,
+            out_specs=[VMEM] * 2,
             scratch_shapes=[pltpu.VMEM((DIM, TOK), F32)],
             compiler_params=PARAMS,
             name="query_back",
         )(place, units, norms, dscores, keys_rot, flipped, gain_q, gk_rows)
-        return dq_raw, lax.all_to_all(gains, ("dp", "cp"), 0, 0, tiled=True)
+        gains = gains[0:1] + swap(gains, 1)[0:1]
+        gains = jnp.broadcast_to(gains, (2 * N_CP, 2 * DIM))
+        groups = [
+            [(2 * chip + core) * N_CP + place for chip in range(2) for place in range(N_CP)]
+            for core in range(2)
+        ]
+        return dq_raw, lax.all_to_all(
+            gains, ("dp", "cp"), 0, 0, tiled=True, axis_index_groups=groups
+        )
 
     def nothing(operands):
-        return jnp.zeros((TOK, KV * half), BF), jnp.zeros((N_DP * N_CP, 2 * DIM), F32)
+        return jnp.zeros((TOK, KV * half), BF), jnp.zeros((2 * N_CP, 2 * DIM), F32)
 
     dq_raw, everyone = lax.cond(
         place[0, 0] >= 0, query_side, nothing, (place, units, norms, dscores, keys_rot, gk_rows)

time: 108 us -> 102 us (0.944)
  the two profiles are of different devices: /device:TPU:1 before, /device:TPU:56 now
where the time goes in v2:
time: 102 us
  Pallas kernels  28.5 us (28%)
  blocking collectives  27.5 us (27%)
  starting transfers between devices  24 us (24%)
  waiting for transfers between devices  13.3 us (13%)
  local copies, waits for them, and re-layouts  6.21 us (6%)
  between operations  2.08 us (2%)
    all_to_all x1, blocking collectives, query_side(): lax.all_to_all(gains, ('dp', 'cp'), 0, 0, tiled=True, axis_index_groups=g...  27.5 us
    ppermute x8, starting transfers between devices, shifted(): lax.ppermute(array, 'cp', [(j, (j + by) % N_CP) for j in range(N_CP)])  18.3 us
    ppermute x10, waiting for transfers between devices, swap(): return lax.ppermute(array, 'dp', [(j, j ^ slot) for j in range(N_DP)])  13.3 us
    pallas_call x1, Pallas kernels, body(): pl.pallas_call(forward, out_shape=[shape(TOK, KV * half), shape(TOK, KV *...  10.6 us
    pallas_call x1, Pallas kernels, body(): pl.pallas_call(backward, out_shape=[shape(KEYS, KV * half), shape(TOK, KV...  6.83 us
    unnamed x16, local copies, waits for them, and re-layouts  6.12 us
    ppermute x10, starting transfers between devices, swap(): return lax.ppermute(array, 'dp', [(j, j ^ slot) for j in range(N_DP)])  5.72 us
    pallas_call x1, Pallas kernels, query_side(): pl.pallas_call(query_back, out_shape=[shape(TOK, KV * half), shape(8, 2 *...  4.28 us
  transfers between devices with their start and end apart: 18, of which 5 were waited for; matrix products, arithmetic and copies ran while one was open for 0% of the time, Pallas kernels for 18%

profile of v2, /device:TPU:56, one launch (start us, length us, event | category | flops | bytes accessed | tf_op | source)
XLA Modules:
  0.0 101.6 jit_solution(12286519916521992208)
XLA Ops:
  0.6 0.0 copy-start.7
  0.6 0.0 copy-start.6
  0.7 2.0 %kv_pick.1 = (bf16[32,1024]{1,0:T(8,128)(2,1)}, bf16[32,1024]{1,0:T(8,128)(2,1)}, bf16[32,1024]{1,0:T(8,128)(2,1)}, bf16[32,1024]{1,0:T(8,128)(2,1)}) custom-call(s32[1,128]{1,0:T(1,128)} %order_ref.3, bf16[128,512]{1,0:T(8,128)(2,1)} %k_ref.1, bf16[128,512]{1,0:T(8,128)(2,1)} %v_ref.1), custom_call_target="tpu_custom_call" | custom-call | tf_op jit(solution)/shard_map/kv_pick/pallas_call | solution.py:354
  2.6 0.0 collective-permute-start.4
  2.6 1.5 %collective-permute-start.5 = (bf16[32,1024]{1,0:T(8,128)(2,1)}, bf16[32,1024]{1,0:T(8,128)(2,1)S(1)}, u32[]{:S(2)}, u32[]{:S(2)}) collective-permute-start(bf16[32,1024]{1,0:T(8,128)(2,1)} %get-tuple-element.75), channel_id=1, source_target_pairs={{0,128},{64,192},{128,0},{192,64},{1,129},{65,193},{129,1},{193,65... | collective-permute-start | bytes 196616 | tf_op jit(solution)/shard_map/ppermute | solution.py:337
  4.1 0.4 collective-permute-start.6
  5.1 0.0 collective-permute-done.4.rest_1_
  5.1 2.2 %collective-permute-done.5.rest_2_ = bf16[32,1024]{1,0:T(8,128)(2,1)S(1)} collective-permute-done((bf16[32,1024]{1,0:T(8,128)(2,1)}, bf16[32,1024]{1,0:T(8,128)(2,1)S(1)}, u32[]{:S(2)}, u32[]{:S(2)}) %collective-permute-start.5) | collective-permute-done | bytes 65568 | tf_op jit(solution)/shard_map/ppermute | solution.py:337
  7.4 1.1 %collective-permute-done.6.rest_3_ = bf16[32,1024]{1,0:T(8,128)(2,1)S(1)} collective-permute-done((bf16[32,1024]{1,0:T(8,128)(2,1)}, bf16[32,1024]{1,0:T(8,128)(2,1)S(1)}, u32[]{:S(2)}, u32[]{:S(2)}) %collective-permute-start.6) | collective-permute-done | bytes 65568 | tf_op jit(solution)/shard_map/ppermute | solution.py:337
  8.4 0.0 copy-start.4
  8.4 0.8 copy-done.4
  9.3 3.0 %collective-permute-start.7 = (bf16[136,1024]{1,0:T(8,128)(2,1)S(1)}, bf16[136,1024]{1,0:T(8,128)(2,1)S(1)}, u32[]{:S(2)}, u32[]{:S(2)}) collective-permute-start(bf16[136,1024]{1,0:T(8,128)(2,1)S(1)} %kv_join.1.rest_1_.rest_4_), channel_id=1, source_target_pairs={{0,1},{1,2},{2,3},{3,4},{4,5},{5,6},{6,7},{7,8},{8,9},{9,10},{10,1... | collective-permute-start | bytes 835592 | tf_op jit(solution)/shard_map/ppermute | solution.py:341
  12.3 0.0 copy-start
  12.3 1.2 %copy-done = bf16[128,4096]{1,0:T(8,128)(2,1)S(1)} copy-done((bf16[128,4096]{1,0:T(8,128)(2,1)S(1)}, bf16[128,4096]{1,0:T(8,128)(2,1)}, u32[]{:S(2)}) %copy-start) | copy-done | bytes 1048600
  13.6 0.0 copy-start.1
  13.6 1.2 %copy-done.1 = bf16[128,4096]{1,0:T(8,128)(2,1)S(1)} copy-done((bf16[128,4096]{1,0:T(8,128)(2,1)S(1)}, bf16[128,4096]{1,0:T(8,128)(2,1)}, u32[]{:S(2)}) %copy-start.1) | copy-done | bytes 1048600
  14.8 0.0 copy-start.5
  14.8 0.7 copy-done.5
  15.4 1.8 %qg_pick.1 = (bf16[32,4096]{1,0:T(8,128)(2,1)S(1)}, bf16[32,4096]{1,0:T(8,128)(2,1)S(1)}, bf16[32,4096]{1,0:T(8,128)(2,1)S(1)}, bf16[32,4096]{1,0:T(8,128)(2,1)S...) custom-call(s32[1,128]{1,0:T(1,128)S(1)} %copy-done.5, ...), custom_call_target="tpu_custom_call" | custom-call | tf_op jit(solution)/shard_map/qg_pick/pallas_call | solution.py:365
  17.2 0.1 collective-permute-start.1
  17.3 2.7 %collective-permute-start.10 = (bf16[136,1024]{1,0:T(8,128)(2,1)S(1)}, bf16[136,1024]{1,0:T(8,128)(2,1)S(1)}, u32[]{:S(2)}, u32[]{:S(2)}) collective-permute-start(bf16[136,1024]{1,0:T(8,128)(2,1)S(1)} %kv_join.1.rest_1_.rest_4_), channel_id=1, source_target_pairs={{0,4},{1,5},{2,6},{3,7},{4,8},{5,9},{6,10},{7,11},{8,12},{9,13},{1... | collective-permute-start | bytes 835592 | tf_op jit(solution)/shard_map/ppermute | solution.py:341
  20.0 0.6 collective-permute-start.2
  20.6 0.9 collective-permute-start.3
  21.5 0.0 collective-permute-done.1.refs_1_
  21.5 2.2 %collective-permute-start.8 = (bf16[136,1024]{1,0:T(8,128)(2,1)S(1)}, bf16[136,1024]{1,0:T(8,128)(2,1)S(1)}, u32[]{:S(2)}, u32[]{:S(2)}) collective-permute-start(bf16[136,1024]{1,0:T(8,128)(2,1)S(1)} %kv_join.1.rest_1_.rest_4_), channel_id=1, source_target_pairs={{0,2},{1,3},{2,4},{3,5},{4,6},{5,7},{6,8},{7,9},{8,10},{9,11},{10,... | collective-permute-start | bytes 835592 | tf_op jit(solution)/shard_map/ppermute | solution.py:341
  23.7 0.0 collective-permute-done.7.rest_2_.rest_5_
  23.7 0.7 collective-permute-start.9
  24.4 4.8 %collective-permute-done.2.refs_2_ = bf16[32,4096]{1,0:T(8,128)(2,1)S(1)} collective-permute-done((bf16[32,4096]{1,0:T(8,128)(2,1)S(1)}, bf16[32,4096]{1,0:T(8,128)(2,1)S(1)}, u32[]{:S(2)}, u32[]{:S(2)}) %collective-permute-start.2) | collective-permute-done | bytes 262176 | tf_op jit(solution)/shard_map/ppermute | solution.py:337
  29.1 0.0 collective-permute-start.11
  29.2 4.0 %collective-permute-done.3.refs_3_ = bf16[32,4096]{1,0:T(8,128)(2,1)S(1)} collective-permute-done((bf16[32,4096]{1,0:T(8,128)(2,1)S(1)}, bf16[32,4096]{1,0:T(8,128)(2,1)S(1)}, u32[]{:S(2)}, u32[]{:S(2)}) %collective-permute-start.3) | collective-permute-done | bytes 262176 | tf_op jit(solution)/shard_map/ppermute | solution.py:337
  33.2 0.6 collective-permute-start.12
  33.8 0.0 collective-permute-done.10.rest_5_.rest_8_
  33.8 1.7 %collective-permute-start.13 = (bf16[32,4096]{1,0:T(8,128)(2,1)S(1)}, bf16[32,4096]{1,0:T(8,128)(2,1)S(1)}, u32[]{:S(2)}, u32[]{:S(2)}) collective-permute-start(bf16[32,4096]{1,0:T(8,128)(2,1)S(1)} %get-tuple-element.85), channel_id=1, source_target_pairs={{0,192},{64,128},{128,64},{192,0},{1,193},{65,129},{129,65},{193,1... | collective-permute-start | bytes 786440 | tf_op jit(solution)/shard_map/ppermute | solution.py:337
  35.5 0.0 copy-start.2
  35.5 1.1 %copy-done.2 = f32[640,256]{1,0:T(8,128)S(1)} copy-done((f32[640,256]{1,0:T(8,128)S(1)}, f32[640,256]{1,0:T(8,128)}, u32[]{:S(2)}) %copy-start.2) | copy-done | bytes 655384
  36.5 0.0 copy-start.3
  36.5 1.1 %copy-done.3 = f32[128,1280]{1,0:T(8,128)S(1)} copy-done((f32[128,1280]{1,0:T(8,128)S(1)}, f32[128,1280]{1,0:T(8,128)}, u32[]{:S(2)}) %copy-start.3) | copy-done | bytes 655384
  37.6 1.2 %query_unit.1 = (f32[128,4096]{1,0:T(8,128)S(1)}, f32[8,4096]{1,0:T(8,128)S(1)}, f32[640,256]{1,0:T(8,128)S(1)}, f32[128,1280]{1,0:T(8,128)S(1)}) custom-call(bf16[32,4096]{1,0:T(8,128)(2,1)S(1)} %get-tuple-element.68.refs_0_, bf16[32,4096]{1,0:T(8,128)(2,1)S(1)} %collective-permute-done.1.refs_1_, bf16[32,4096]{1,0:T(8,128)(2,1)S(1)} %collective-permute-done.2.refs_2_, ...), custom_call_target="tpu_custom_call" | custom-call | tf_op jit(solution)/shard_map/query_unit/pallas_call | solution.py:405
  38.9 0.0 collective-permute-done.8.rest_3_.rest_6_
  38.9 0.0 collective-permute-done.9.rest_4_.rest_7_
  38.9 0.0 copy-done.7
  38.9 0.0 copy-done.6
  38.9 10.6 %forward.1 = (bf16[128,4096]{1,0:T(8,128)(2,1)}, bf16[128,4096]{1,0:T(8,128)(2,1)S(1)}, f32[640,4096]{1,0:T(8,128)S(1)}, bf16[128,4096]{1,0:T(8,128)(2,1)S(1)}, ...) custom-call(s32[1,1]{1,0:T(1,128)S(6)} %copy.23.doc_ref, ...), custom_call_target="tpu_custom_call" | custom-call | tf_op jit(solution)/shard_map/forward/pallas_call | solution.py:420
  49.5 0.0 collective-permute-done.11.rest_1_
  49.5 0.0 collective-permute-done.12.rest_2_
  49.5 0.0 collective-permute-done.13.rest_3_
  49.5 6.8 %backward.1 = (bf16[640,4096]{1,0:T(8,128)(2,1)S(1)}, f32[128,1024]{1,0:T(8,128)S(1)}, bf16[128,1024]{1,0:T(8,128)(2,1)}, bf16[128,1024]{1,0:T(8,128)(2,1)S(1)},...) custom-call(s32[1,1]{1,0:T(1,128)} %get-tuple-element.80.place_ref, ...), custom_call_target="tpu_custom_call" | custom-call | tf_op jit(solution)/shard_map/backward/pallas_call | solution.py:436
  56.4 2.4 %collective-permute-start.14 = (bf16[128,1024]{1,0:T(8,128)(2,1)}, bf16[128,1024]{1,0:T(8,128)(2,1)S(1)}, u32[]{:S(2)}, u32[]{:S(2)}) collective-permute-start(bf16[128,1024]{1,0:T(8,128)(2,1)} %get-tuple-element.95), channel_id=1, source_target_pairs={{0,63},{1,0},{2,1},{3,2},{4,3},{5,4},{6,5},{7,6},{8,7},{9,8},{10,9... | collective-permute-start | bytes 786440 | tf_op jit(solution)/shard_map/ppermute | solution.py:341
  58.8 0.6 collective-permute-start.15
  59.4 4.2 %collective-permute-start.16 = (bf16[128,1024]{1,0:T(8,128)(2,1)S(1)}, bf16[128,1024]{1,0:T(8,128)(2,1)S(1)}, u32[]{:S(2)}, u32[]{:S(2)}) collective-permute-start(bf16[128,1024]{1,0:T(8,128)(2,1)S(1)} %get-tuple-element.97), channel_id=1, source_target_pairs={{0,61},{1,62},{2,63},{3,0},{4,1},{5,2},{6,3},{7,4},{8,5},{9,6},{10... | collective-permute-start | bytes 786440 | tf_op jit(solution)/shard_map/ppermute | solution.py:341
  63.6 2.5 %collective-permute-start.17 = (bf16[128,1024]{1,0:T(8,128)(2,1)S(1)}, bf16[128,1024]{1,0:T(8,128)(2,1)S(1)}, u32[]{:S(2)}, u32[]{:S(2)}) collective-permute-start(bf16[128,1024]{1,0:T(8,128)(2,1)S(1)} %get-tuple-element.98), channel_id=1, source_target_pairs={{0,60},{1,61},{2,62},{3,63},{4,0},{5,1},{6,2},{7,3},{8,4},{9,5},{1... | collective-permute-start | bytes 786440 | tf_op jit(solution)/shard_map/ppermute | solution.py:341
  66.7 33.0 %conditional.1 = (bf16[128,4096]{1,0:T(8,128)(2,1)}, f32[128,256]{1,0:T(8,128)S(1)}) conditional(s32[]{:T(128)} %bitcast.3, () %tuple.16, (s32[1,1]{1,0:T(1,128)}, f32[128,4096]{1,0:T(8,128)S(1)}, f32[8,4096]{1,0:T(8,128)S(1)}, bf16[640,4096]{1,0:T(8,128)(2,1)S(1)}, bf16[640,512]{1,0:T(8,128)(2,1)S(1)}, /*index=5*/f32[128,1280]{1,0:T(8,128)S(1)}, ...), branch_computations={%region_0.0_spmd, %region_1.0_spmd} | conditional | flops 256 | bytes 1179670 | solution.py:475
  66.8 4.3 %query_back.1 = (bf16[128,4096]{1,0:T(8,128)(2,1)}, f32[8,256]{1,0:T(8,128)S(1)}) custom-call(s32[1,1]{1,0:T(1,128)} %get-tuple-element.16.place_ref, f32[128,4096]{1,0:T(8,128)S(1)} %get-tuple-element.17.unit_ref, f32[8,4096]{1,0:T(8,128)S(1)} %get-tuple-element.18.norm_ref, bf16[640,4096]{1,0:T(8,128)(2,1)S(1)} %get-tuple-element.19.ds_ref, ...), custom_call_target="tpu_custom_call" | custom-call | tf_op jit(solution)/shard_map/cond/branch_1_fun/query_back/pallas_call | solution.py:453
  71.0 0.0 collective-permute-start
  71.0 1.2 %collective-permute-done = f32[8,256]{1,0:T(8,128)S(1)} collective-permute-done((f32[8,256]{1,0:T(8,128)S(1)}, f32[8,256]{1,0:T(8,128)S(1)}, u32[]{:S(2)}, u32[]{:S(2)}) %collective-permute-start) | collective-permute-done | bytes 8224 | tf_op jit(solution)/shard_map/cond/branch_1_fun/ppermute | solution.py:337
  72.2 0.1 broadcast_in_dim.0
  72.3 27.5 %all_to_all.7 = f32[128,1,256]{2,1,0:T(1,128)S(1)} all-to-all(f32[128,1,256]{2,1,0:T(1,128)S(1)} %broadcast_in_dim.0), channel_id=1, replica_groups={{0,1,2,3,4,5,6,7,8,9,10,11,12,13,14,15,16,17,18,19,20,21,22,23,24,25,26..., dimensions={0} | all-to-all | bytes 262144 | tf_op jit(solution)/shard_map/cond/branch_1_fun/all_to_all | solution.py:468
  99.8 0.0 collective-permute-done.14.rest_0_
  99.8 0.0 collective-permute-done.15.rest_1_
  99.8 0.0 collective-permute-done.16.rest_2_
  99.8 0.0 collective-permute-done.17.rest_3_
  99.8 1.8 %finish.1 = (bf16[128,512]{1,0:T(8,128)(2,1)}, bf16[128,512]{1,0:T(8,128)(2,1)}, f32[1,128]{1,0:T(1,128)}, f32[1,128]{1,0:T(1,128)}) custom-call(s32[1,1]{1,0:T(1,128)} %get-tuple-element.80.place_ref, f32[128,1024]{1,0:T(8,128)S(1)} %get-tuple-element.94.own_ref, bf16[128,1024]{1,0:T(8,128)(2,1)S(1)} %collective-permute-done.14.rest_0_, ...), custom_call_target="tpu_custom_call" | custom-call | tf_op jit(solution)/shard_map/finish/pallas_call | solution.py:478
  (3 shorter events, 0.0 us)
Async XLA Ops:
  0.6 38.3 %copy-start.7 = (f32[128]{0:T(128)S(1)}, f32[128]{0:T(128)}, u32[]{:S(2)}) copy-start(f32[128]{0:T(128)} %param.18) | copy-start | bytes 1540
  0.6 38.3 %copy-start.6 = (f32[128]{0:T(128)S(1)}, f32[128]{0:T(128)}, u32[]{:S(2)}) copy-start(f32[128]{0:T(128)} %param.19) | copy-start | bytes 1540
  2.6 2.5 %collective-permute-start.4 = (bf16[32,1024]{1,0:T(8,128)(2,1)}, bf16[32,1024]{1,0:T(8,128)(2,1)S(1)}, u32[]{:S(2)}, u32[]{:S(2)}) collective-permute-start(bf16[32,1024]{1,0:T(8,128)(2,1)} %get-tuple-element.74), channel_id=1, source_target_pairs={{0,64},{64,0},{128,192},{192,128},{1,65},{65,1},{129,193},{193,129... | collective-permute-start | bytes 196616 | tf_op jit(solution)/shard_map/ppermute | solution.py:337
  2.6 4.8 %collective-permute-start.5 = (bf16[32,1024]{1,0:T(8,128)(2,1)}, bf16[32,1024]{1,0:T(8,128)(2,1)S(1)}, u32[]{:S(2)}, u32[]{:S(2)}) collective-permute-start(bf16[32,1024]{1,0:T(8,128)(2,1)} %get-tuple-element.75), channel_id=1, source_target_pairs={{0,128},{64,192},{128,0},{192,64},{1,129},{65,193},{129,1},{193,65... | collective-permute-start | bytes 196616 | tf_op jit(solution)/shard_map/ppermute | solution.py:337
  4.1 4.3 %collective-permute-start.6 = (bf16[32,1024]{1,0:T(8,128)(2,1)}, bf16[32,1024]{1,0:T(8,128)(2,1)S(1)}, u32[]{:S(2)}, u32[]{:S(2)}) collective-permute-start(bf16[32,1024]{1,0:T(8,128)(2,1)} %get-tuple-element.76), channel_id=1, source_target_pairs={{0,192},{64,128},{128,64},{192,0},{1,193},{65,129},{129,65},{193,1... | collective-permute-start | bytes 196616 | tf_op jit(solution)/shard_map/ppermute | solution.py:337
  8.4 0.8 copy-start.4
  9.3 14.4 %collective-permute-start.7 = (bf16[136,1024]{1,0:T(8,128)(2,1)S(1)}, bf16[136,1024]{1,0:T(8,128)(2,1)S(1)}, u32[]{:S(2)}, u32[]{:S(2)}) collective-permute-start(bf16[136,1024]{1,0:T(8,128)(2,1)S(1)} %kv_join.1.rest_1_.rest_4_), channel_id=1, source_target_pairs={{0,1},{1,2},{2,3},{3,4},{4,5},{5,6},{6,7},{7,8},{8,9},{9,10},{10,1... | collective-permute-start | bytes 835592 | tf_op jit(solution)/shard_map/ppermute | solution.py:341
  12.3 1.2 %copy-start = (bf16[128,4096]{1,0:T(8,128)(2,1)S(1)}, bf16[128,4096]{1,0:T(8,128)(2,1)}, u32[]{:S(2)}) copy-start(bf16[128,4096]{1,0:T(8,128)(2,1)} %q_ref.1) | copy-start | bytes 3145732
  13.6 1.2 %copy-start.1 = (bf16[128,4096]{1,0:T(8,128)(2,1)S(1)}, bf16[128,4096]{1,0:T(8,128)(2,1)}, u32[]{:S(2)}) copy-start(bf16[128,4096]{1,0:T(8,128)(2,1)} %g_ref.1) | copy-start | bytes 3145732
  14.8 0.7 copy-start.5
  17.2 4.3 %collective-permute-start.1 = (bf16[32,4096]{1,0:T(8,128)(2,1)S(1)}, bf16[32,4096]{1,0:T(8,128)(2,1)S(1)}, u32[]{:S(2)}, u32[]{:S(2)}) collective-permute-start(bf16[32,4096]{1,0:T(8,128)(2,1)S(1)} %get-tuple-element.69), channel_id=1, source_target_pairs={{0,64},{64,0},{128,192},{192,128},{1,65},{65,1},{129,193},{193,129... | collective-permute-start | bytes 786440 | tf_op jit(solution)/shard_map/ppermute | solution.py:337
  17.3 16.4 %collective-permute-start.10 = (bf16[136,1024]{1,0:T(8,128)(2,1)S(1)}, bf16[136,1024]{1,0:T(8,128)(2,1)S(1)}, u32[]{:S(2)}, u32[]{:S(2)}) collective-permute-start(bf16[136,1024]{1,0:T(8,128)(2,1)S(1)} %kv_join.1.rest_1_.rest_4_), channel_id=1, source_target_pairs={{0,4},{1,5},{2,6},{3,7},{4,8},{5,9},{6,10},{7,11},{8,12},{9,13},{1... | collective-permute-start | bytes 835592 | tf_op jit(solution)/shard_map/ppermute | solution.py:341
  20.0 9.1 %collective-permute-start.2 = (bf16[32,4096]{1,0:T(8,128)(2,1)S(1)}, bf16[32,4096]{1,0:T(8,128)(2,1)S(1)}, u32[]{:S(2)}, u32[]{:S(2)}) collective-permute-start(bf16[32,4096]{1,0:T(8,128)(2,1)S(1)} %get-tuple-element.70), channel_id=1, source_target_pairs={{0,128},{64,192},{128,0},{192,64},{1,129},{65,193},{129,1},{193,65... | collective-permute-start | bytes 786440 | tf_op jit(solution)/shard_map/ppermute | solution.py:337
  20.6 12.6 %collective-permute-start.3 = (bf16[32,4096]{1,0:T(8,128)(2,1)S(1)}, bf16[32,4096]{1,0:T(8,128)(2,1)S(1)}, u32[]{:S(2)}, u32[]{:S(2)}) collective-permute-start(bf16[32,4096]{1,0:T(8,128)(2,1)S(1)} %get-tuple-element.71), channel_id=1, source_target_pairs={{0,192},{64,128},{128,64},{192,0},{1,193},{65,129},{129,65},{193,1... | collective-permute-start | bytes 786440 | tf_op jit(solution)/shard_map/ppermute | solution.py:337
  21.5 17.4 %collective-permute-start.8 = (bf16[136,1024]{1,0:T(8,128)(2,1)S(1)}, bf16[136,1024]{1,0:T(8,128)(2,1)S(1)}, u32[]{:S(2)}, u32[]{:S(2)}) collective-permute-start(bf16[136,1024]{1,0:T(8,128)(2,1)S(1)} %kv_join.1.rest_1_.rest_4_), channel_id=1, source_target_pairs={{0,2},{1,3},{2,4},{3,5},{4,6},{5,7},{6,8},{7,9},{8,10},{9,11},{10,... | collective-permute-start | bytes 835592 | tf_op jit(solution)/shard_map/ppermute | solution.py:341
  23.7 15.2 %collective-permute-start.9 = (bf16[136,1024]{1,0:T(8,128)(2,1)S(1)}, bf16[136,1024]{1,0:T(8,128)(2,1)S(1)}, u32[]{:S(2)}, u32[]{:S(2)}) collective-permute-start(bf16[136,1024]{1,0:T(8,128)(2,1)S(1)} %collective-permute-done.7.rest_2_.rest_5_), channel_id=1, source_target_pairs={{0,2},{1,3},{2,4},{3,5},{4,6},{5,7},{6,8},{7,9},{8,10},{9,11},{10,... | collective-permute-start | bytes 835592 | tf_op jit(solution)/shard_map/ppermute | solution.py:341
  29.1 20.4 %collective-permute-start.11 = (bf16[32,4096]{1,0:T(8,128)(2,1)S(1)}, bf16[32,4096]{1,0:T(8,128)(2,1)S(1)}, u32[]{:S(2)}, u32[]{:S(2)}) collective-permute-start(bf16[32,4096]{1,0:T(8,128)(2,1)S(1)} %get-tuple-element.83), channel_id=1, source_target_pairs={{0,64},{64,0},{128,192},{192,128},{1,65},{65,1},{129,193},{193,129... | collective-permute-start | bytes 786440 | tf_op jit(solution)/shard_map/ppermute | solution.py:337
  33.2 16.3 %collective-permute-start.12 = (bf16[32,4096]{1,0:T(8,128)(2,1)S(1)}, bf16[32,4096]{1,0:T(8,128)(2,1)S(1)}, u32[]{:S(2)}, u32[]{:S(2)}) collective-permute-start(bf16[32,4096]{1,0:T(8,128)(2,1)S(1)} %get-tuple-element.84), channel_id=1, source_target_pairs={{0,128},{64,192},{128,0},{192,64},{1,129},{65,193},{129,1},{193,65... | collective-permute-start | bytes 786440 | tf_op jit(solution)/shard_map/ppermute | solution.py:337
  33.8 15.8 %collective-permute-start.13 = (bf16[32,4096]{1,0:T(8,128)(2,1)S(1)}, bf16[32,4096]{1,0:T(8,128)(2,1)S(1)}, u32[]{:S(2)}, u32[]{:S(2)}) collective-permute-start(bf16[32,4096]{1,0:T(8,128)(2,1)S(1)} %get-tuple-element.85), channel_id=1, source_target_pairs={{0,192},{64,128},{128,64},{192,0},{1,193},{65,129},{129,65},{193,1... | collective-permute-start | bytes 786440 | tf_op jit(solution)/shard_map/ppermute | solution.py:337
  35.5 1.1 %copy-start.2 = (f32[640,256]{1,0:T(8,128)S(1)}, f32[640,256]{1,0:T(8,128)}, u32[]{:S(2)}) copy-start(f32[640,256]{1,0:T(8,128)} %constant.11.clone.refs_4_) | copy-start | bytes 1966084
  36.5 1.1 %copy-start.3 = (f32[128,1280]{1,0:T(8,128)S(1)}, f32[128,1280]{1,0:T(8,128)}, u32[]{:S(2)}) copy-start(f32[128,1280]{1,0:T(8,128)} %constant.12.clone.refs_5_) | copy-start | bytes 1966084
  56.4 43.4 %collective-permute-start.14 = (bf16[128,1024]{1,0:T(8,128)(2,1)}, bf16[128,1024]{1,0:T(8,128)(2,1)S(1)}, u32[]{:S(2)}, u32[]{:S(2)}) collective-permute-start(bf16[128,1024]{1,0:T(8,128)(2,1)} %get-tuple-element.95), channel_id=1, source_target_pairs={{0,63},{1,0},{2,1},{3,2},{4,3},{5,4},{6,5},{7,6},{8,7},{9,8},{10,9... | collective-permute-start | bytes 786440 | tf_op jit(solution)/shard_map/ppermute | solution.py:341
  58.8 41.0 %collective-permute-start.15 = (bf16[128,1024]{1,0:T(8,128)(2,1)S(1)}, bf16[128,1024]{1,0:T(8,128)(2,1)S(1)}, u32[]{:S(2)}, u32[]{:S(2)}) collective-permute-start(bf16[128,1024]{1,0:T(8,128)(2,1)S(1)} %get-tuple-element.96), channel_id=1, source_target_pairs={{0,62},{1,63},{2,0},{3,1},{4,2},{5,3},{6,4},{7,5},{8,6},{9,7},{10,... | collective-permute-start | bytes 786440 | tf_op jit(solution)/shard_map/ppermute | solution.py:341
  59.4 40.4 %collective-permute-start.16 = (bf16[128,1024]{1,0:T(8,128)(2,1)S(1)}, bf16[128,1024]{1,0:T(8,128)(2,1)S(1)}, u32[]{:S(2)}, u32[]{:S(2)}) collective-permute-start(bf16[128,1024]{1,0:T(8,128)(2,1)S(1)} %get-tuple-element.97), channel_id=1, source_target_pairs={{0,61},{1,62},{2,63},{3,0},{4,1},{5,2},{6,3},{7,4},{8,5},{9,6},{10... | collective-permute-start | bytes 786440 | tf_op jit(solution)/shard_map/ppermute | solution.py:341
  63.6 36.2 %collective-permute-start.17 = (bf16[128,1024]{1,0:T(8,128)(2,1)S(1)}, bf16[128,1024]{1,0:T(8,128)(2,1)S(1)}, u32[]{:S(2)}, u32[]{:S(2)}) collective-permute-start(bf16[128,1024]{1,0:T(8,128)(2,1)S(1)} %get-tuple-element.98), channel_id=1, source_target_pairs={{0,60},{1,61},{2,62},{3,63},{4,0},{5,1},{6,2},{7,3},{8,4},{9,5},{1... | collective-permute-start | bytes 786440 | tf_op jit(solution)/shard_map/ppermute | solution.py:341
  71.0 1.2 %collective-permute-start = (f32[8,256]{1,0:T(8,128)S(1)}, f32[8,256]{1,0:T(8,128)S(1)}, u32[]{:S(2)}, u32[]{:S(2)}) collective-permute-start(f32[8,256]{1,0:T(8,128)S(1)} %get-tuple-element.25), channel_id=1, source_target_pairs={{0,64},{64,0},{128,192},{192,128},{1,65},{65,1},{129,193},{193,129... | collective-permute-start | bytes 24584 | tf_op jit(solution)/shard_map/cond/branch_1_fun/ppermute | solution.py:337

commit v3 on v2

--- a/solution.py
+++ b/solution.py
@@ -446,7 +446,7 @@
     )(place, *g_slots, *shards, out_again, probs, queries, keys_unit, table)
     dscores, dkv_own = results[:2]
     gk_rows = results[2 + REACH]
-    parts = [shifted(results[1 + back], -back) for back in range(1, REACH + 1)]
+    parts = [shifted(results[1 + back], -back) for back in (4, 2, 3, 1)]
 
     def query_side(operands):
         place, units, norms, dscores, keys_rot, gk_rows = operands

time: 102 us -> 99.8 us (0.978)
  the two profiles are of different devices: /device:TPU:56 before, /device:TPU:1 now
where the time goes in v3:
time: 99.8 us; the launch traced here: 99.4 us
  Pallas kernels  28.5 us (29%)
  starting transfers between devices  23.9 us (24%)
  blocking collectives  19.5 us (20%)
  waiting for transfers between devices  19.2 us (19%)
  local copies, waits for them, and re-layouts  6.21 us (6%)
  between operations  2.05 us (2%)
    all_to_all x1, blocking collectives, query_side(): lax.all_to_all(gains, ('dp', 'cp'), 0, 0, tiled=True, axis_index_groups=g...  19.5 us
    ppermute x10, starting transfers between devices, swap(): return lax.ppermute(array, 'dp', [(j, j ^ slot) for j in range(N_DP)])  12.5 us
    ppermute x8, starting transfers between devices, shifted(): lax.ppermute(array, 'cp', [(j, (j + by) % N_CP) for j in range(N_CP)])  11.4 us
    pallas_call x1, Pallas kernels, body(): pl.pallas_call(forward, out_shape=[shape(TOK, KV * half), shape(TOK, KV *...  10.6 us
    ppermute x10, waiting for transfers between devices, swap(): return lax.ppermute(array, 'dp', [(j, j ^ slot) for j in range(N_DP)])  9.95 us
    ppermute x8, waiting for transfers between devices, shifted(): lax.ppermute(array, 'cp', [(j, (j + by) % N_CP) for j in range(N_CP)])  9.27 us
    pallas_call x1, Pallas kernels, body(): pl.pallas_call(backward, out_shape=[shape(KEYS, KV * half), shape(TOK, KV...  6.83 us
    unnamed x16, local copies, waits for them, and re-layouts  6.12 us
  transfers between devices with their start and end apart: 18, of which 7 were waited for; matrix products, arithmetic and copies ran while one was open for 0% of the time, Pallas kernels for 18%

profile of v3, /device:TPU:1, one launch (start us, length us, event | category | flops | bytes accessed | tf_op | source)
XLA Modules:
  0.0 99.4 jit_solution(4957053376665751582)
XLA Ops:
  0.6 0.0 copy-start.7
  0.6 0.0 copy-start.6
  0.7 2.0 %kv_pick.1 = (bf16[32,1024]{1,0:T(8,128)(2,1)}, bf16[32,1024]{1,0:T(8,128)(2,1)}, bf16[32,1024]{1,0:T(8,128)(2,1)}, bf16[32,1024]{1,0:T(8,128)(2,1)}) custom-call(s32[1,128]{1,0:T(1,128)} %order_ref.3, bf16[128,512]{1,0:T(8,128)(2,1)} %k_ref.1, bf16[128,512]{1,0:T(8,128)(2,1)} %v_ref.1), custom_call_target="tpu_custom_call" | custom-call | tf_op jit(solution)/shard_map/kv_pick/pallas_call | solution.py:354
  2.6 3.2 %collective-permute-start.4 = (bf16[32,1024]{1,0:T(8,128)(2,1)}, bf16[32,1024]{1,0:T(8,128)(2,1)S(1)}, u32[]{:S(2)}, u32[]{:S(2)}) collective-permute-start(bf16[32,1024]{1,0:T(8,128)(2,1)} %get-tuple-element.74), channel_id=1, source_target_pairs={{0,64},{64,0},{128,192},{192,128},{1,65},{65,1},{129,193},{193,129... | collective-permute-start | bytes 196616 | tf_op jit(solution)/shard_map/ppermute | solution.py:337
  5.9 0.0 collective-permute-start.5
  5.9 1.6 %collective-permute-start.6 = (bf16[32,1024]{1,0:T(8,128)(2,1)}, bf16[32,1024]{1,0:T(8,128)(2,1)S(1)}, u32[]{:S(2)}, u32[]{:S(2)}) collective-permute-start(bf16[32,1024]{1,0:T(8,128)(2,1)} %get-tuple-element.76), channel_id=1, source_target_pairs={{0,192},{64,128},{128,64},{192,0},{1,193},{65,129},{129,65},{193,1... | collective-permute-start | bytes 196616 | tf_op jit(solution)/shard_map/ppermute | solution.py:337
  8.1 0.0 collective-permute-done.4.rest_1_
  8.2 1.7 %collective-permute-done.5.rest_2_ = bf16[32,1024]{1,0:T(8,128)(2,1)S(1)} collective-permute-done((bf16[32,1024]{1,0:T(8,128)(2,1)}, bf16[32,1024]{1,0:T(8,128)(2,1)S(1)}, u32[]{:S(2)}, u32[]{:S(2)}) %collective-permute-start.5) | collective-permute-done | bytes 65568 | tf_op jit(solution)/shard_map/ppermute | solution.py:337
  9.8 1.5 %collective-permute-done.6.rest_3_ = bf16[32,1024]{1,0:T(8,128)(2,1)S(1)} collective-permute-done((bf16[32,1024]{1,0:T(8,128)(2,1)}, bf16[32,1024]{1,0:T(8,128)(2,1)S(1)}, u32[]{:S(2)}, u32[]{:S(2)}) %collective-permute-start.6) | collective-permute-done | bytes 65568 | tf_op jit(solution)/shard_map/ppermute | solution.py:337
  11.3 0.0 copy-start.4
  11.3 0.8 copy-done.4
  12.2 1.1 %collective-permute-start.7 = (bf16[136,1024]{1,0:T(8,128)(2,1)S(1)}, bf16[136,1024]{1,0:T(8,128)(2,1)S(1)}, u32[]{:S(2)}, u32[]{:S(2)}) collective-permute-start(bf16[136,1024]{1,0:T(8,128)(2,1)S(1)} %kv_join.1.rest_1_.rest_4_), channel_id=1, source_target_pairs={{0,1},{1,2},{2,3},{3,4},{4,5},{5,6},{6,7},{7,8},{8,9},{9,10},{10,1... | collective-permute-start | bytes 835592 | tf_op jit(solution)/shard_map/ppermute | solution.py:341
  13.2 0.0 copy-start
  13.2 1.2 %copy-done = bf16[128,4096]{1,0:T(8,128)(2,1)S(1)} copy-done((bf16[128,4096]{1,0:T(8,128)(2,1)S(1)}, bf16[128,4096]{1,0:T(8,128)(2,1)}, u32[]{:S(2)}) %copy-start) | copy-done | bytes 1048600
  14.5 0.0 copy-start.1
  14.5 1.2 %copy-done.1 = bf16[128,4096]{1,0:T(8,128)(2,1)S(1)} copy-done((bf16[128,4096]{1,0:T(8,128)(2,1)S(1)}, bf16[128,4096]{1,0:T(8,128)(2,1)}, u32[]{:S(2)}) %copy-start.1) | copy-done | bytes 1048600
  15.7 0.0 copy-start.5
  15.7 0.7 copy-done.5
  16.3 1.8 %qg_pick.1 = (bf16[32,4096]{1,0:T(8,128)(2,1)S(1)}, bf16[32,4096]{1,0:T(8,128)(2,1)S(1)}, bf16[32,4096]{1,0:T(8,128)(2,1)S(1)}, bf16[32,4096]{1,0:T(8,128)(2,1)S...) custom-call(s32[1,128]{1,0:T(1,128)S(1)} %copy-done.5, ...), custom_call_target="tpu_custom_call" | custom-call | tf_op jit(solution)/shard_map/qg_pick/pallas_call | solution.py:365
  18.1 0.7 collective-permute-start.1
  18.8 2.9 %collective-permute-start.10 = (bf16[136,1024]{1,0:T(8,128)(2,1)S(1)}, bf16[136,1024]{1,0:T(8,128)(2,1)S(1)}, u32[]{:S(2)}, u32[]{:S(2)}) collective-permute-start(bf16[136,1024]{1,0:T(8,128)(2,1)S(1)} %kv_join.1.rest_1_.rest_4_), channel_id=1, source_target_pairs={{0,4},{1,5},{2,6},{3,7},{4,8},{5,9},{6,10},{7,11},{8,12},{9,13},{1... | collective-permute-start | bytes 835592 | tf_op jit(solution)/shard_map/ppermute | solution.py:341
  21.8 0.3 collective-permute-start.2
  22.1 1.7 %collective-permute-start.3 = (bf16[32,4096]{1,0:T(8,128)(2,1)S(1)}, bf16[32,4096]{1,0:T(8,128)(2,1)S(1)}, u32[]{:S(2)}, u32[]{:S(2)}) collective-permute-start(bf16[32,4096]{1,0:T(8,128)(2,1)S(1)} %get-tuple-element.71), channel_id=1, source_target_pairs={{0,192},{64,128},{128,64},{192,0},{1,193},{65,129},{129,65},{193,1... | collective-permute-start | bytes 786440 | tf_op jit(solution)/shard_map/ppermute | solution.py:337
  23.7 0.0 collective-permute-done.1.refs_1_
  23.8 0.4 collective-permute-start.8
  24.2 3.6 %collective-permute-done.7.rest_2_.rest_5_ = bf16[136,1024]{1,0:T(8,128)(2,1)S(1)} collective-permute-done((bf16[136,1024]{1,0:T(8,128)(2,1)S(1)}, bf16[136,1024]{1,0:T(8,128)(2,1)S(1)}, u32[]{:S(2)}, u32[]{:S(2)}) %collective-permute-start.7) | collective-permute-done | bytes 278560 | tf_op jit(solution)/shard_map/ppermute | solution.py:341
  27.8 0.0 collective-permute-start.9
  27.8 1.5 %collective-permute-done.2.refs_2_ = bf16[32,4096]{1,0:T(8,128)(2,1)S(1)} collective-permute-done((bf16[32,4096]{1,0:T(8,128)(2,1)S(1)}, bf16[32,4096]{1,0:T(8,128)(2,1)S(1)}, u32[]{:S(2)}, u32[]{:S(2)}) %collective-permute-start.2) | collective-permute-done | bytes 262176 | tf_op jit(solution)/shard_map/ppermute | solution.py:337
  29.3 2.0 %collective-permute-start.11 = (bf16[32,4096]{1,0:T(8,128)(2,1)S(1)}, bf16[32,4096]{1,0:T(8,128)(2,1)S(1)}, u32[]{:S(2)}, u32[]{:S(2)}) collective-permute-start(bf16[32,4096]{1,0:T(8,128)(2,1)S(1)} %get-tuple-element.83), channel_id=1, source_target_pairs={{0,64},{64,0},{128,192},{192,128},{1,65},{65,1},{129,193},{193,129... | collective-permute-start | bytes 786440 | tf_op jit(solution)/shard_map/ppermute | solution.py:337
  31.3 4.4 %collective-permute-done.3.refs_3_ = bf16[32,4096]{1,0:T(8,128)(2,1)S(1)} collective-permute-done((bf16[32,4096]{1,0:T(8,128)(2,1)S(1)}, bf16[32,4096]{1,0:T(8,128)(2,1)S(1)}, u32[]{:S(2)}, u32[]{:S(2)}) %collective-permute-start.3) | collective-permute-done | bytes 262176 | tf_op jit(solution)/shard_map/ppermute | solution.py:337
  35.7 0.3 collective-permute-start.12
  36.0 0.0 collective-permute-done.10.rest_5_.rest_8_
  36.0 0.9 collective-permute-start.13
  36.9 0.0 copy-start.2
  36.9 1.1 %copy-done.2 = f32[640,256]{1,0:T(8,128)S(1)} copy-done((f32[640,256]{1,0:T(8,128)S(1)}, f32[640,256]{1,0:T(8,128)}, u32[]{:S(2)}) %copy-start.2) | copy-done | bytes 655384
  38.0 0.0 copy-start.3
  38.0 1.1 %copy-done.3 = f32[128,1280]{1,0:T(8,128)S(1)} copy-done((f32[128,1280]{1,0:T(8,128)S(1)}, f32[128,1280]{1,0:T(8,128)}, u32[]{:S(2)}) %copy-start.3) | copy-done | bytes 655384
  39.1 1.2 %query_unit.1 = (f32[128,4096]{1,0:T(8,128)S(1)}, f32[8,4096]{1,0:T(8,128)S(1)}, f32[640,256]{1,0:T(8,128)S(1)}, f32[128,1280]{1,0:T(8,128)S(1)}) custom-call(bf16[32,4096]{1,0:T(8,128)(2,1)S(1)} %get-tuple-element.68.refs_0_, bf16[32,4096]{1,0:T(8,128)(2,1)S(1)} %collective-permute-done.1.refs_1_, bf16[32,4096]{1,0:T(8,128)(2,1)S(1)} %collective-permute-done.2.refs_2_, ...), custom_call_target="tpu_custom_call" | custom-call | tf_op jit(solution)/shard_map/query_unit/pallas_call | solution.py:405
  40.4 0.0 collective-permute-done.8.rest_3_.rest_6_
  40.4 5.6 %collective-permute-done.9.rest_4_.rest_7_ = bf16[136,1024]{1,0:T(8,128)(2,1)S(1)} collective-permute-done((bf16[136,1024]{1,0:T(8,128)(2,1)S(1)}, bf16[136,1024]{1,0:T(8,128)(2,1)S(1)}, u32[]{:S(2)}, u32[]{:S(2)}) %collective-permute-start.9) | collective-permute-done | bytes 278560 | tf_op jit(solution)/shard_map/ppermute | solution.py:341
  46.0 0.0 copy-done.7
  46.0 0.0 copy-done.6
  46.0 10.6 %forward.1 = (bf16[128,4096]{1,0:T(8,128)(2,1)}, bf16[128,4096]{1,0:T(8,128)(2,1)S(1)}, f32[640,4096]{1,0:T(8,128)S(1)}, bf16[128,4096]{1,0:T(8,128)(2,1)S(1)}, ...) custom-call(s32[1,1]{1,0:T(1,128)S(6)} %copy.23.doc_ref, ...), custom_call_target="tpu_custom_call" | custom-call | tf_op jit(solution)/shard_map/forward/pallas_call | solution.py:420
  56.6 0.0 collective-permute-done.11.rest_1_
  56.6 0.0 collective-permute-done.12.rest_2_
  56.6 0.0 collective-permute-done.13.rest_3_
  56.6 6.8 %backward.1 = (bf16[640,4096]{1,0:T(8,128)(2,1)S(1)}, f32[128,1024]{1,0:T(8,128)S(1)}, bf16[128,1024]{1,0:T(8,128)(2,1)S(1)}, bf16[128,1024]{1,0:T(8,128)(2,1)S(...) custom-call(s32[1,1]{1,0:T(1,128)} %get-tuple-element.80.place_ref, ...), custom_call_target="tpu_custom_call" | custom-call | tf_op jit(solution)/shard_map/backward/pallas_call | solution.py:436
  63.5 3.1 %collective-permute-start.14 = (bf16[128,1024]{1,0:T(8,128)(2,1)}, bf16[128,1024]{1,0:T(8,128)(2,1)S(1)}, u32[]{:S(2)}, u32[]{:S(2)}) collective-permute-start(bf16[128,1024]{1,0:T(8,128)(2,1)} %get-tuple-element.95), channel_id=1, source_target_pairs={{0,60},{1,61},{2,62},{3,63},{4,0},{5,1},{6,2},{7,3},{8,4},{9,5},{1... | collective-permute-start | bytes 786440 | tf_op jit(solution)/shard_map/ppermute | solution.py:341
  66.6 0.5 collective-permute-start.15
  67.1 1.8 %collective-permute-start.16 = (bf16[128,1024]{1,0:T(8,128)(2,1)S(1)}, bf16[128,1024]{1,0:T(8,128)(2,1)S(1)}, u32[]{:S(2)}, u32[]{:S(2)}) collective-permute-start(bf16[128,1024]{1,0:T(8,128)(2,1)S(1)} %get-tuple-element.97), channel_id=1, source_target_pairs={{0,61},{1,62},{2,63},{3,0},{4,1},{5,2},{6,3},{7,4},{8,5},{9,6},{10... | collective-permute-start | bytes 786440 | tf_op jit(solution)/shard_map/ppermute | solution.py:341
  68.8 1.7 %collective-permute-start.17 = (bf16[128,1024]{1,0:T(8,128)(2,1)S(1)}, bf16[128,1024]{1,0:T(8,128)(2,1)S(1)}, u32[]{:S(2)}, u32[]{:S(2)}) collective-permute-start(bf16[128,1024]{1,0:T(8,128)(2,1)S(1)} %get-tuple-element.98), channel_id=1, source_target_pairs={{0,63},{1,0},{2,1},{3,2},{4,3},{5,4},{6,5},{7,6},{8,7},{9,8},{10,9... | collective-permute-start | bytes 786440 | tf_op jit(solution)/shard_map/ppermute | solution.py:341
  71.1 26.4 %conditional.1 = (bf16[128,4096]{1,0:T(8,128)(2,1)}, f32[128,256]{1,0:T(8,128)S(1)}) conditional(s32[]{:T(128)} %bitcast.3, () %tuple.16, (s32[1,1]{1,0:T(1,128)}, f32[128,4096]{1,0:T(8,128)S(1)}, f32[8,4096]{1,0:T(8,128)S(1)}, bf16[640,4096]{1,0:T(8,128)(2,1)S(1)}, bf16[640,512]{1,0:T(8,128)(2,1)S(1)}, /*index=5*/f32[128,1280]{1,0:T(8,128)S(1)}, ...), branch_computations={%region_0.0_spmd, %region_1.0_spmd} | conditional | flops 256 | bytes 1179670 | solution.py:475
  71.1 4.3 %query_back.1 = (bf16[128,4096]{1,0:T(8,128)(2,1)}, f32[8,256]{1,0:T(8,128)S(1)}) custom-call(s32[1,1]{1,0:T(1,128)} %get-tuple-element.16.place_ref, f32[128,4096]{1,0:T(8,128)S(1)} %get-tuple-element.17.unit_ref, f32[8,4096]{1,0:T(8,128)S(1)} %get-tuple-element.18.norm_ref, bf16[640,4096]{1,0:T(8,128)(2,1)S(1)} %get-tuple-element.19.ds_ref, ...), custom_call_target="tpu_custom_call" | custom-call | tf_op jit(solution)/shard_map/cond/branch_1_fun/query_back/pallas_call | solution.py:453
  75.4 1.7 %collective-permute-start = (f32[8,256]{1,0:T(8,128)S(1)}, f32[8,256]{1,0:T(8,128)S(1)}, u32[]{:S(2)}, u32[]{:S(2)}) collective-permute-start(f32[8,256]{1,0:T(8,128)S(1)} %get-tuple-element.25), channel_id=1, source_target_pairs={{0,64},{64,0},{128,192},{192,128},{1,65},{65,1},{129,193},{193,129... | collective-permute-start | bytes 24584 | tf_op jit(solution)/shard_map/cond/branch_1_fun/ppermute | solution.py:337
  77.1 0.8 collective-permute-done
  78.0 0.1 broadcast_in_dim.0
  78.0 19.5 %all_to_all.7 = f32[128,1,256]{2,1,0:T(1,128)S(1)} all-to-all(f32[128,1,256]{2,1,0:T(1,128)S(1)} %broadcast_in_dim.0), channel_id=1, replica_groups={{0,1,2,3,4,5,6,7,8,9,10,11,12,13,14,15,16,17,18,19,20,21,22,23,24,25,26..., dimensions={0} | all-to-all | bytes 262144 | tf_op jit(solution)/shard_map/cond/branch_1_fun/all_to_all | solution.py:468
  97.6 0.0 collective-permute-done.14.rest_0_
  97.6 0.0 collective-permute-done.15.rest_1_
  97.6 0.0 collective-permute-done.16.rest_2_
  97.6 0.0 collective-permute-done.17.rest_3_
  97.6 1.8 %finish.1 = (bf16[128,512]{1,0:T(8,128)(2,1)}, bf16[128,512]{1,0:T(8,128)(2,1)}, f32[1,128]{1,0:T(1,128)}, f32[1,128]{1,0:T(1,128)}) custom-call(s32[1,1]{1,0:T(1,128)} %get-tuple-element.80.place_ref, f32[128,1024]{1,0:T(8,128)S(1)} %get-tuple-element.94.own_ref, bf16[128,1024]{1,0:T(8,128)(2,1)S(1)} %collective-permute-done.14.rest_0_, ...), custom_call_target="tpu_custom_call" | custom-call | tf_op jit(solution)/shard_map/finish/pallas_call | solution.py:478
  (3 shorter events, 0.0 us)
Async XLA Ops:
  0.6 45.4 %copy-start.7 = (f32[128]{0:T(128)S(1)}, f32[128]{0:T(128)}, u32[]{:S(2)}) copy-start(f32[128]{0:T(128)} %param.18) | copy-start | bytes 1540
  0.6 45.4 %copy-start.6 = (f32[128]{0:T(128)S(1)}, f32[128]{0:T(128)}, u32[]{:S(2)}) copy-start(f32[128]{0:T(128)} %param.19) | copy-start | bytes 1540
  2.6 5.5 %collective-permute-start.4 = (bf16[32,1024]{1,0:T(8,128)(2,1)}, bf16[32,1024]{1,0:T(8,128)(2,1)S(1)}, u32[]{:S(2)}, u32[]{:S(2)}) collective-permute-start(bf16[32,1024]{1,0:T(8,128)(2,1)} %get-tuple-element.74), channel_id=1, source_target_pairs={{0,64},{64,0},{128,192},{192,128},{1,65},{65,1},{129,193},{193,129... | collective-permute-start | bytes 196616 | tf_op jit(solution)/shard_map/ppermute | solution.py:337
  5.9 4.0 %collective-permute-start.5 = (bf16[32,1024]{1,0:T(8,128)(2,1)}, bf16[32,1024]{1,0:T(8,128)(2,1)S(1)}, u32[]{:S(2)}, u32[]{:S(2)}) collective-permute-start(bf16[32,1024]{1,0:T(8,128)(2,1)} %get-tuple-element.75), channel_id=1, source_target_pairs={{0,128},{64,192},{128,0},{192,64},{1,129},{65,193},{129,1},{193,65... | collective-permute-start | bytes 196616 | tf_op jit(solution)/shard_map/ppermute | solution.py:337
  5.9 5.4 %collective-permute-start.6 = (bf16[32,1024]{1,0:T(8,128)(2,1)}, bf16[32,1024]{1,0:T(8,128)(2,1)S(1)}, u32[]{:S(2)}, u32[]{:S(2)}) collective-permute-start(bf16[32,1024]{1,0:T(8,128)(2,1)} %get-tuple-element.76), channel_id=1, source_target_pairs={{0,192},{64,128},{128,64},{192,0},{1,193},{65,129},{129,65},{193,1... | collective-permute-start | bytes 196616 | tf_op jit(solution)/shard_map/ppermute | solution.py:337
  11.3 0.8 copy-start.4
  12.2 15.6 %collective-permute-start.7 = (bf16[136,1024]{1,0:T(8,128)(2,1)S(1)}, bf16[136,1024]{1,0:T(8,128)(2,1)S(1)}, u32[]{:S(2)}, u32[]{:S(2)}) collective-permute-start(bf16[136,1024]{1,0:T(8,128)(2,1)S(1)} %kv_join.1.rest_1_.rest_4_), channel_id=1, source_target_pairs={{0,1},{1,2},{2,3},{3,4},{4,5},{5,6},{6,7},{7,8},{8,9},{9,10},{10,1... | collective-permute-start | bytes 835592 | tf_op jit(solution)/shard_map/ppermute | solution.py:341
  13.2 1.2 %copy-start = (bf16[128,4096]{1,0:T(8,128)(2,1)S(1)}, bf16[128,4096]{1,0:T(8,128)(2,1)}, u32[]{:S(2)}) copy-start(bf16[128,4096]{1,0:T(8,128)(2,1)} %q_ref.1) | copy-start | bytes 3145732
  14.5 1.2 %copy-start.1 = (bf16[128,4096]{1,0:T(8,128)(2,1)S(1)}, bf16[128,4096]{1,0:T(8,128)(2,1)}, u32[]{:S(2)}) copy-start(bf16[128,4096]{1,0:T(8,128)(2,1)} %g_ref.1) | copy-start | bytes 3145732
  15.7 0.7 copy-start.5
  18.1 5.6 %collective-permute-start.1 = (bf16[32,4096]{1,0:T(8,128)(2,1)S(1)}, bf16[32,4096]{1,0:T(8,128)(2,1)S(1)}, u32[]{:S(2)}, u32[]{:S(2)}) collective-permute-start(bf16[32,4096]{1,0:T(8,128)(2,1)S(1)} %get-tuple-element.69), channel_id=1, source_target_pairs={{0,64},{64,0},{128,192},{192,128},{1,65},{65,1},{129,193},{193,129... | collective-permute-start | bytes 786440 | tf_op jit(solution)/shard_map/ppermute | solution.py:337
  18.8 17.2 %collective-permute-start.10 = (bf16[136,1024]{1,0:T(8,128)(2,1)S(1)}, bf16[136,1024]{1,0:T(8,128)(2,1)S(1)}, u32[]{:S(2)}, u32[]{:S(2)}) collective-permute-start(bf16[136,1024]{1,0:T(8,128)(2,1)S(1)} %kv_join.1.rest_1_.rest_4_), channel_id=1, source_target_pairs={{0,4},{1,5},{2,6},{3,7},{4,8},{5,9},{6,10},{7,11},{8,12},{9,13},{1... | collective-permute-start | bytes 835592 | tf_op jit(solution)/shard_map/ppermute | solution.py:341
  21.8 7.5 %collective-permute-start.2 = (bf16[32,4096]{1,0:T(8,128)(2,1)S(1)}, bf16[32,4096]{1,0:T(8,128)(2,1)S(1)}, u32[]{:S(2)}, u32[]{:S(2)}) collective-permute-start(bf16[32,4096]{1,0:T(8,128)(2,1)S(1)} %get-tuple-element.70), channel_id=1, source_target_pairs={{0,128},{64,192},{128,0},{192,64},{1,129},{65,193},{129,1},{193,65... | collective-permute-start | bytes 786440 | tf_op jit(solution)/shard_map/ppermute | solution.py:337
  22.1 13.7 %collective-permute-start.3 = (bf16[32,4096]{1,0:T(8,128)(2,1)S(1)}, bf16[32,4096]{1,0:T(8,128)(2,1)S(1)}, u32[]{:S(2)}, u32[]{:S(2)}) collective-permute-start(bf16[32,4096]{1,0:T(8,128)(2,1)S(1)} %get-tuple-element.71), channel_id=1, source_target_pairs={{0,192},{64,128},{128,64},{192,0},{1,193},{65,129},{129,65},{193,1... | collective-permute-start | bytes 786440 | tf_op jit(solution)/shard_map/ppermute | solution.py:337
  23.8 16.6 %collective-permute-start.8 = (bf16[136,1024]{1,0:T(8,128)(2,1)S(1)}, bf16[136,1024]{1,0:T(8,128)(2,1)S(1)}, u32[]{:S(2)}, u32[]{:S(2)}) collective-permute-start(bf16[136,1024]{1,0:T(8,128)(2,1)S(1)} %kv_join.1.rest_1_.rest_4_), channel_id=1, source_target_pairs={{0,2},{1,3},{2,4},{3,5},{4,6},{5,7},{6,8},{7,9},{8,10},{9,11},{10,... | collective-permute-start | bytes 835592 | tf_op jit(solution)/shard_map/ppermute | solution.py:341
  27.8 18.2 %collective-permute-start.9 = (bf16[136,1024]{1,0:T(8,128)(2,1)S(1)}, bf16[136,1024]{1,0:T(8,128)(2,1)S(1)}, u32[]{:S(2)}, u32[]{:S(2)}) collective-permute-start(bf16[136,1024]{1,0:T(8,128)(2,1)S(1)} %collective-permute-done.7.rest_2_.rest_5_), channel_id=1, source_target_pairs={{0,2},{1,3},{2,4},{3,5},{4,6},{5,7},{6,8},{7,9},{8,10},{9,11},{10,... | collective-permute-start | bytes 835592 | tf_op jit(solution)/shard_map/ppermute | solution.py:341
  29.3 27.3 %collective-permute-start.11 = (bf16[32,4096]{1,0:T(8,128)(2,1)S(1)}, bf16[32,4096]{1,0:T(8,128)(2,1)S(1)}, u32[]{:S(2)}, u32[]{:S(2)}) collective-permute-start(bf16[32,4096]{1,0:T(8,128)(2,1)S(1)} %get-tuple-element.83), channel_id=1, source_target_pairs={{0,64},{64,0},{128,192},{192,128},{1,65},{65,1},{129,193},{193,129... | collective-permute-start | bytes 786440 | tf_op jit(solution)/shard_map/ppermute | solution.py:337
  35.7 20.9 %collective-permute-start.12 = (bf16[32,4096]{1,0:T(8,128)(2,1)S(1)}, bf16[32,4096]{1,0:T(8,128)(2,1)S(1)}, u32[]{:S(2)}, u32[]{:S(2)}) collective-permute-start(bf16[32,4096]{1,0:T(8,128)(2,1)S(1)} %get-tuple-element.84), channel_id=1, source_target_pairs={{0,128},{64,192},{128,0},{192,64},{1,129},{65,193},{129,1},{193,65... | collective-permute-start | bytes 786440 | tf_op jit(solution)/shard_map/ppermute | solution.py:337
  36.0 20.6 %collective-permute-start.13 = (bf16[32,4096]{1,0:T(8,128)(2,1)S(1)}, bf16[32,4096]{1,0:T(8,128)(2,1)S(1)}, u32[]{:S(2)}, u32[]{:S(2)}) collective-permute-start(bf16[32,4096]{1,0:T(8,128)(2,1)S(1)} %get-tuple-element.85), channel_id=1, source_target_pairs={{0,192},{64,128},{128,64},{192,0},{1,193},{65,129},{129,65},{193,1... | collective-permute-start | bytes 786440 | tf_op jit(solution)/shard_map/ppermute | solution.py:337
  36.9 1.1 %copy-start.2 = (f32[640,256]{1,0:T(8,128)S(1)}, f32[640,256]{1,0:T(8,128)}, u32[]{:S(2)}) copy-start(f32[640,256]{1,0:T(8,128)} %constant.11.clone.refs_4_) | copy-start | bytes 1966084
  38.0 1.1 %copy-start.3 = (f32[128,1280]{1,0:T(8,128)S(1)}, f32[128,1280]{1,0:T(8,128)}, u32[]{:S(2)}) copy-start(f32[128,1280]{1,0:T(8,128)} %constant.12.clone.refs_5_) | copy-start | bytes 1966084
  63.5 34.1 %collective-permute-start.14 = (bf16[128,1024]{1,0:T(8,128)(2,1)}, bf16[128,1024]{1,0:T(8,128)(2,1)S(1)}, u32[]{:S(2)}, u32[]{:S(2)}) collective-permute-start(bf16[128,1024]{1,0:T(8,128)(2,1)} %get-tuple-element.95), channel_id=1, source_target_pairs={{0,60},{1,61},{2,62},{3,63},{4,0},{5,1},{6,2},{7,3},{8,4},{9,5},{1... | collective-permute-start | bytes 786440 | tf_op jit(solution)/shard_map/ppermute | solution.py:341
  66.6 31.0 %collective-permute-start.15 = (bf16[128,1024]{1,0:T(8,128)(2,1)S(1)}, bf16[128,1024]{1,0:T(8,128)(2,1)S(1)}, u32[]{:S(2)}, u32[]{:S(2)}) collective-permute-start(bf16[128,1024]{1,0:T(8,128)(2,1)S(1)} %get-tuple-element.96), channel_id=1, source_target_pairs={{0,62},{1,63},{2,0},{3,1},{4,2},{5,3},{6,4},{7,5},{8,6},{9,7},{10,... | collective-permute-start | bytes 786440 | tf_op jit(solution)/shard_map/ppermute | solution.py:341
  67.1 30.5 %collective-permute-start.16 = (bf16[128,1024]{1,0:T(8,128)(2,1)S(1)}, bf16[128,1024]{1,0:T(8,128)(2,1)S(1)}, u32[]{:S(2)}, u32[]{:S(2)}) collective-permute-start(bf16[128,1024]{1,0:T(8,128)(2,1)S(1)} %get-tuple-element.97), channel_id=1, source_target_pairs={{0,61},{1,62},{2,63},{3,0},{4,1},{5,2},{6,3},{7,4},{8,5},{9,6},{10... | collective-permute-start | bytes 786440 | tf_op jit(solution)/shard_map/ppermute | solution.py:341
  68.8 28.8 %collective-permute-start.17 = (bf16[128,1024]{1,0:T(8,128)(2,1)S(1)}, bf16[128,1024]{1,0:T(8,128)(2,1)S(1)}, u32[]{:S(2)}, u32[]{:S(2)}) collective-permute-start(bf16[128,1024]{1,0:T(8,128)(2,1)S(1)} %get-tuple-element.98), channel_id=1, source_target_pairs={{0,63},{1,0},{2,1},{3,2},{4,3},{5,4},{6,5},{7,6},{8,7},{9,8},{10,9... | collective-permute-start | bytes 786440 | tf_op jit(solution)/shard_map/ppermute | solution.py:341
  75.4 2.5 %collective-permute-start = (f32[8,256]{1,0:T(8,128)S(1)}, f32[8,256]{1,0:T(8,128)S(1)}, u32[]{:S(2)}, u32[]{:S(2)}) collective-permute-start(f32[8,256]{1,0:T(8,128)S(1)} %get-tuple-element.25), channel_id=1, source_target_pairs={{0,64},{64,0},{128,192},{192,128},{1,65},{65,1},{129,193},{193,129... | collective-permute-start | bytes 24584 | tf_op jit(solution)/shard_map/cond/branch_1_fun/ppermute | solution.py:337

commit v4 on v3

--- a/solution.py
+++ b/solution.py
@@ -74,15 +74,11 @@
         outs[slot][...] = rows_ref[slot_rows(slot), :]
 
 
-def qg_pick(order_ref, q_ref, g_ref, *rest):
-    q_outs, g_outs, rows_ref = rest[:N_DP], rest[N_DP : 2 * N_DP], rest[2 * N_DP]
-    chosen = picker(order_ref)
-    half = GROUP * DIM
-    rows_ref[:, :half] = dot(chosen, q_ref[...], 0, 0).astype(BF)
-    rows_ref[:, half:] = dot(chosen, g_ref[...], 0, 0).astype(BF)
+def one_pick(order_ref, array_ref, *rest):
+    outs, rows_ref = rest[:N_DP], rest[N_DP]
+    rows_ref[...] = dot(picker(order_ref), array_ref[...], 0, 0).astype(BF)
     for slot in range(N_DP):
-        q_outs[slot][...] = rows_ref[slot_rows(slot), :half]
-        g_outs[slot][...] = rows_ref[slot_rows(slot), half:]
+        outs[slot][...] = rows_ref[slot_rows(slot), :]
 
 
 def kv_join(doc_ref, *rest):
@@ -362,20 +358,22 @@
     )(send_order, k_raw, values)
     kv_slots = [kv_slots[0]] + [swap(kv_slots[slot], slot) for slot in range(1, N_DP)]
     half = GROUP * DIM
-    picked = pl.pallas_call(
-        qg_pick,
-        grid=(KV,),
-        out_shape=[shape(ROWS, KV * half)] * (2 * N_DP),
-        in_specs=[
-            pl.BlockSpec((1, TOK), lambda h: (0, 0)),
-            pl.BlockSpec((TOK, half), lambda h: (0, h)),
-            pl.BlockSpec((TOK, half), lambda h: (0, h)),
-        ],
-        out_specs=[pl.BlockSpec((ROWS, half), lambda h: (0, h))] * (2 * N_DP),
-        scratch_shapes=[pltpu.VMEM((TOK, WIDE), BF)],
-        compiler_params=PARAMS,
-        name="qg_pick",
-    )(send_order, q_raw, loss_grad)
+    def pick_rows(array, name):
+        return pl.pallas_call(
+            one_pick,
+            grid=(KV,),
+            out_shape=[shape(ROWS, KV * half)] * N_DP,
+            in_specs=[
+                pl.BlockSpec((1, TOK), lambda h: (0, 0)),
+                pl.BlockSpec((TOK, half), lambda h: (0, h)),
+            ],
+            out_specs=[pl.BlockSpec((ROWS, half), lambda h: (0, h))] * N_DP,
+            scratch_shapes=[pltpu.VMEM((TOK, half), BF)],
+            compiler_params=PARAMS,
+            name=name,
+        )(send_order, array)
+
+    picked = list(pick_rows(q_raw, "q_pick")) + list(pick_rows(loss_grad, "g_pick"))
     kv_own = pl.pallas_call(
         kv_join,
         out_shape=shape(TOK + ID_ROWS, KV * PAIR),

time: 99.8 us -> 98.9 us (level)
  waiting for transfers between devices: 19.2 us -> 17.6 us
    ppermute x10, waiting for transfers between devices: 9.95 us -> 5.04 us  [swap(): return lax.ppermute(array, 'dp', [(j, j ^ slot) for j in range(N_DP)])]
    ppermute x8, waiting for transfers between devices: 9.27 us -> 12.6 us  [shifted(): lax.ppermute(array, 'cp', [(j, (j + by) % N_CP) for j in range(N_CP)])]
    pallas_call x1 -> x2, Pallas kernels: 1.79 us -> 2.68 us  [pick_rows(): pl.pallas_call(one_pick, grid=(KV,), out_shape=[shape(ROWS, KV * half)] *...]
  transfers between devices with their start and end apart: 18 -> 18, of which waited for: 7 -> 7; matrix products, arithmetic and copies ran while one was open for 0% -> 0% of each run, Pallas kernels for 18% -> 19%
where the time goes in v4:
time: 98.9 us; the launch traced here: 98.4 us
  Pallas kernels  29.4 us (30%)
  starting transfers between devices  24.4 us (25%)
  blocking collectives  18.7 us (19%)
  waiting for transfers between devices  17.6 us (18%)
  local copies, waits for them, and re-layouts  6.21 us (6%)
  between operations  2.08 us (2%)
    all_to_all x1, blocking collectives, query_side(): lax.all_to_all(gains, ('dp', 'cp'), 0, 0, tiled=True, axis_index_groups=g...  18.7 us
    ppermute x10, starting transfers between devices, swap(): return lax.ppermute(array, 'dp', [(j, j ^ slot) for j in range(N_DP)])  12.8 us
    ppermute x8, waiting for transfers between devices, shifted(): lax.ppermute(array, 'cp', [(j, (j + by) % N_CP) for j in range(N_CP)])  12.6 us
    ppermute x8, starting transfers between devices, shifted(): lax.ppermute(array, 'cp', [(j, (j + by) % N_CP) for j in range(N_CP)])  11.6 us
    pallas_call x1, Pallas kernels, body(): pl.pallas_call(forward, out_shape=[shape(TOK, KV * half), shape(TOK, KV *...  10.6 us
    pallas_call x1, Pallas kernels, body(): pl.pallas_call(backward, out_shape=[shape(KEYS, KV * half), shape(TOK, KV...  6.87 us
    unnamed x16, local copies, waits for them, and re-layouts  6.13 us
    ppermute x10, waiting for transfers between devices, swap(): return lax.ppermute(array, 'dp', [(j, j ^ slot) for j in range(N_DP)])  5.04 us
  transfers between devices with their start and end apart: 18, of which 7 were waited for; matrix products, arithmetic and copies ran while one was open for 0% of the time, Pallas kernels for 19%

profile of v4, /device:TPU:1, one launch (start us, length us, event | category | flops | bytes accessed | tf_op | source)
XLA Modules:
  0.0 98.4 jit_solution(9734864362999022640)
XLA Ops:
  0.6 0.0 copy-start.7
  0.6 0.0 copy-start.6
  0.7 2.0 %kv_pick.1 = (bf16[32,1024]{1,0:T(8,128)(2,1)}, bf16[32,1024]{1,0:T(8,128)(2,1)}, bf16[32,1024]{1,0:T(8,128)(2,1)}, bf16[32,1024]{1,0:T(8,128)(2,1)}) custom-call(s32[1,128]{1,0:T(1,128)} %order_ref.5, bf16[128,512]{1,0:T(8,128)(2,1)} %k_ref.1, bf16[128,512]{1,0:T(8,128)(2,1)} %v_ref.1), custom_call_target="tpu_custom_call" | custom-call | tf_op jit(solution)/shard_map/kv_pick/pallas_call | solution.py:350
  2.6 3.2 %collective-permute-start.4 = (bf16[32,1024]{1,0:T(8,128)(2,1)}, bf16[32,1024]{1,0:T(8,128)(2,1)S(1)}, u32[]{:S(2)}, u32[]{:S(2)}) collective-permute-start(bf16[32,1024]{1,0:T(8,128)(2,1)} %get-tuple-element.74), channel_id=1, source_target_pairs={{0,64},{64,0},{128,192},{192,128},{1,65},{65,1},{129,193},{193,129... | collective-permute-start | bytes 196616 | tf_op jit(solution)/shard_map/ppermute | solution.py:333
  5.9 0.0 collective-permute-start.5
  5.9 1.6 %collective-permute-start.6 = (bf16[32,1024]{1,0:T(8,128)(2,1)}, bf16[32,1024]{1,0:T(8,128)(2,1)S(1)}, u32[]{:S(2)}, u32[]{:S(2)}) collective-permute-start(bf16[32,1024]{1,0:T(8,128)(2,1)} %get-tuple-element.76), channel_id=1, source_target_pairs={{0,192},{64,128},{128,64},{192,0},{1,193},{65,129},{129,65},{193,1... | collective-permute-start | bytes 196616 | tf_op jit(solution)/shard_map/ppermute | solution.py:333
  8.1 0.0 collective-permute-done.4.rest_1_
  8.2 1.7 %collective-permute-done.5.rest_2_ = bf16[32,1024]{1,0:T(8,128)(2,1)S(1)} collective-permute-done((bf16[32,1024]{1,0:T(8,128)(2,1)}, bf16[32,1024]{1,0:T(8,128)(2,1)S(1)}, u32[]{:S(2)}, u32[]{:S(2)}) %collective-permute-start.5) | collective-permute-done | bytes 65568 | tf_op jit(solution)/shard_map/ppermute | solution.py:333
  9.8 1.5 %collective-permute-done.6.rest_3_ = bf16[32,1024]{1,0:T(8,128)(2,1)S(1)} collective-permute-done((bf16[32,1024]{1,0:T(8,128)(2,1)}, bf16[32,1024]{1,0:T(8,128)(2,1)S(1)}, u32[]{:S(2)}, u32[]{:S(2)}) %collective-permute-start.6) | collective-permute-done | bytes 65568 | tf_op jit(solution)/shard_map/ppermute | solution.py:333
  11.3 0.0 copy-start.4
  11.3 0.8 copy-done.4
  12.2 1.1 %collective-permute-start.7 = (bf16[136,1024]{1,0:T(8,128)(2,1)S(1)}, bf16[136,1024]{1,0:T(8,128)(2,1)S(1)}, u32[]{:S(2)}, u32[]{:S(2)}) collective-permute-start(bf16[136,1024]{1,0:T(8,128)(2,1)S(1)} %kv_join.1.rest_1_.rest_4_), channel_id=1, source_target_pairs={{0,1},{1,2},{2,3},{3,4},{4,5},{5,6},{6,7},{7,8},{8,9},{9,10},{10,1... | collective-permute-start | bytes 835592 | tf_op jit(solution)/shard_map/ppermute | solution.py:337
  13.2 0.0 copy-start
  13.2 1.2 %copy-done = bf16[128,4096]{1,0:T(8,128)(2,1)S(1)} copy-done((bf16[128,4096]{1,0:T(8,128)(2,1)S(1)}, bf16[128,4096]{1,0:T(8,128)(2,1)}, u32[]{:S(2)}) %copy-start) | copy-done | bytes 1048600
  14.5 0.0 copy-start.5
  14.5 0.7 copy-done.5
  15.1 1.3 %q_pick.1 = (bf16[32,4096]{1,0:T(8,128)(2,1)S(1)}, bf16[32,4096]{1,0:T(8,128)(2,1)S(1)}, bf16[32,4096]{1,0:T(8,128)(2,1)S(1)}, bf16[32,4096]{1,0:T(8,128)(2,1)S(1)}) custom-call(s32[1,128]{1,0:T(1,128)S(1)} %copy-done.5, bf16[128,4096]{1,0:T(8,128)(2,1)S(1)} %copy-done), custom_call_target="tpu_custom_call" | custom-call | tf_op jit(solution)/shard_map/q_pick/pallas_call | solution.py:362
  16.5 0.7 collective-permute-start.1
  17.1 2.9 %collective-permute-start.10 = (bf16[136,1024]{1,0:T(8,128)(2,1)S(1)}, bf16[136,1024]{1,0:T(8,128)(2,1)S(1)}, u32[]{:S(2)}, u32[]{:S(2)}) collective-permute-start(bf16[136,1024]{1,0:T(8,128)(2,1)S(1)} %kv_join.1.rest_1_.rest_4_), channel_id=1, source_target_pairs={{0,4},{1,5},{2,6},{3,7},{4,8},{5,9},{6,10},{7,11},{8,12},{9,13},{1... | collective-permute-start | bytes 835592 | tf_op jit(solution)/shard_map/ppermute | solution.py:337
  20.1 0.3 collective-permute-start.2
  20.4 1.7 %collective-permute-start.3 = (bf16[32,4096]{1,0:T(8,128)(2,1)S(1)}, bf16[32,4096]{1,0:T(8,128)(2,1)S(1)}, u32[]{:S(2)}, u32[]{:S(2)}) collective-permute-start(bf16[32,4096]{1,0:T(8,128)(2,1)S(1)} %get-tuple-element.71), channel_id=1, source_target_pairs={{0,192},{64,128},{128,64},{192,0},{1,193},{65,129},{129,65},{193,1... | collective-permute-start | bytes 786440 | tf_op jit(solution)/shard_map/ppermute | solution.py:333
  22.1 0.0 collective-permute-done.1.refs_1_
  22.1 0.4 collective-permute-start.8
  22.5 6.2 %collective-permute-done.7.rest_2_.rest_5_ = bf16[136,1024]{1,0:T(8,128)(2,1)S(1)} collective-permute-done((bf16[136,1024]{1,0:T(8,128)(2,1)S(1)}, bf16[136,1024]{1,0:T(8,128)(2,1)S(1)}, u32[]{:S(2)}, u32[]{:S(2)}) %collective-permute-start.7) | collective-permute-done | bytes 278560 | tf_op jit(solution)/shard_map/ppermute | solution.py:337
  28.7 0.0 collective-permute-start.9
  28.7 0.0 copy-start.1
  28.7 1.2 %copy-done.1 = bf16[128,4096]{1,0:T(8,128)(2,1)S(1)} copy-done((bf16[128,4096]{1,0:T(8,128)(2,1)S(1)}, bf16[128,4096]{1,0:T(8,128)(2,1)}, u32[]{:S(2)}) %copy-start.1) | copy-done | bytes 1048600
  29.9 1.3 %g_pick.1 = (bf16[32,4096]{1,0:T(8,128)(2,1)S(1)}, bf16[32,4096]{1,0:T(8,128)(2,1)S(1)}, bf16[32,4096]{1,0:T(8,128)(2,1)S(1)}, bf16[32,4096]{1,0:T(8,128)(2,1)S(1)}) custom-call(s32[1,128]{1,0:T(1,128)S(1)} %copy-done.5, bf16[128,4096]{1,0:T(8,128)(2,1)S(1)} %copy-done.1), custom_call_target="tpu_custom_call" | custom-call | tf_op jit(solution)/shard_map/g_pick/pallas_call | solution.py:362
  31.2 0.0 collective-permute-done.2.refs_2_
  31.3 1.7 %collective-permute-start.11 = (bf16[32,4096]{1,0:T(8,128)(2,1)S(1)}, bf16[32,4096]{1,0:T(8,128)(2,1)S(1)}, u32[]{:S(2)}, u32[]{:S(2)}) collective-permute-start(bf16[32,4096]{1,0:T(8,128)(2,1)S(1)} %get-tuple-element.83), channel_id=1, source_target_pairs={{0,64},{64,0},{128,192},{192,128},{1,65},{65,1},{129,193},{193,129... | collective-permute-start | bytes 786440 | tf_op jit(solution)/shard_map/ppermute | solution.py:333
  33.0 1.0 %collective-permute-done.3.refs_3_ = bf16[32,4096]{1,0:T(8,128)(2,1)S(1)} collective-permute-done((bf16[32,4096]{1,0:T(8,128)(2,1)S(1)}, bf16[32,4096]{1,0:T(8,128)(2,1)S(1)}, u32[]{:S(2)}, u32[]{:S(2)}) %collective-permute-start.3) | collective-permute-done | bytes 262176 | tf_op jit(solution)/shard_map/ppermute | solution.py:333
  34.0 0.3 collective-permute-start.12
  34.3 1.0 %collective-permute-done.10.rest_5_.rest_8_ = bf16[136,1024]{1,0:T(8,128)(2,1)S(1)} collective-permute-done((bf16[136,1024]{1,0:T(8,128)(2,1)S(1)}, bf16[136,1024]{1,0:T(8,128)(2,1)S(1)}, u32[]{:S(2)}, u32[]{:S(2)}) %collective-permute-start.10) | collective-permute-done | bytes 278560 | tf_op jit(solution)/shard_map/ppermute | solution.py:337
  35.3 1.7 %collective-permute-start.13 = (bf16[32,4096]{1,0:T(8,128)(2,1)S(1)}, bf16[32,4096]{1,0:T(8,128)(2,1)S(1)}, u32[]{:S(2)}, u32[]{:S(2)}) collective-permute-start(bf16[32,4096]{1,0:T(8,128)(2,1)S(1)} %get-tuple-element.85), channel_id=1, source_target_pairs={{0,192},{64,128},{128,64},{192,0},{1,193},{65,129},{129,65},{193,1... | collective-permute-start | bytes 786440 | tf_op jit(solution)/shard_map/ppermute | solution.py:333
  37.0 0.0 copy-start.2
  37.0 1.1 %copy-done.2 = f32[640,256]{1,0:T(8,128)S(1)} copy-done((f32[640,256]{1,0:T(8,128)S(1)}, f32[640,256]{1,0:T(8,128)}, u32[]{:S(2)}) %copy-start.2) | copy-done | bytes 655384
  38.1 0.0 copy-start.3
  38.1 1.1 %copy-done.3 = f32[128,1280]{1,0:T(8,128)S(1)} copy-done((f32[128,1280]{1,0:T(8,128)S(1)}, f32[128,1280]{1,0:T(8,128)}, u32[]{:S(2)}) %copy-start.3) | copy-done | bytes 655384
  39.2 1.2 %query_unit.1 = (f32[128,4096]{1,0:T(8,128)S(1)}, f32[8,4096]{1,0:T(8,128)S(1)}, f32[640,256]{1,0:T(8,128)S(1)}, f32[128,1280]{1,0:T(8,128)S(1)}) custom-call(bf16[32,4096]{1,0:T(8,128)(2,1)S(1)} %get-tuple-element.68.refs_0_, bf16[32,4096]{1,0:T(8,128)(2,1)S(1)} %collective-permute-done.1.refs_1_, bf16[32,4096]{1,0:T(8,128)(2,1)S(1)} %collective-permute-done.2.refs_2_, ...), custom_call_target="tpu_custom_call" | custom-call | tf_op jit(solution)/shard_map/query_unit/pallas_call | solution.py:403
  40.5 0.0 collective-permute-done.8.rest_3_.rest_6_
  40.5 5.3 %collective-permute-done.9.rest_4_.rest_7_ = bf16[136,1024]{1,0:T(8,128)(2,1)S(1)} collective-permute-done((bf16[136,1024]{1,0:T(8,128)(2,1)S(1)}, bf16[136,1024]{1,0:T(8,128)(2,1)S(1)}, u32[]{:S(2)}, u32[]{:S(2)}) %collective-permute-start.9) | collective-permute-done | bytes 278560 | tf_op jit(solution)/shard_map/ppermute | solution.py:337
  45.8 0.0 copy-done.7
  45.8 0.0 copy-done.6
  45.8 10.6 %forward.1 = (bf16[128,4096]{1,0:T(8,128)(2,1)}, bf16[128,4096]{1,0:T(8,128)(2,1)S(1)}, f32[640,4096]{1,0:T(8,128)S(1)}, bf16[128,4096]{1,0:T(8,128)(2,1)S(1)}, ...) custom-call(s32[1,1]{1,0:T(1,128)S(6)} %copy.23.doc_ref, ...), custom_call_target="tpu_custom_call" | custom-call | tf_op jit(solution)/shard_map/forward/pallas_call | solution.py:418
  56.4 0.0 collective-permute-done.11.rest_1_
  56.4 0.0 collective-permute-done.12.rest_2_
  56.4 0.0 collective-permute-done.13.rest_3_
  56.4 6.9 %backward.1 = (bf16[640,4096]{1,0:T(8,128)(2,1)S(1)}, f32[128,1024]{1,0:T(8,128)S(1)}, bf16[128,1024]{1,0:T(8,128)(2,1)S(1)}, bf16[128,1024]{1,0:T(8,128)(2,1)S(...) custom-call(s32[1,1]{1,0:T(1,128)} %get-tuple-element.80.place_ref, ...), custom_call_target="tpu_custom_call" | custom-call | tf_op jit(solution)/shard_map/backward/pallas_call | solution.py:434
  63.3 1.9 %collective-permute-start.14 = (bf16[128,1024]{1,0:T(8,128)(2,1)}, bf16[128,1024]{1,0:T(8,128)(2,1)S(1)}, u32[]{:S(2)}, u32[]{:S(2)}) collective-permute-start(bf16[128,1024]{1,0:T(8,128)(2,1)} %get-tuple-element.95), channel_id=1, source_target_pairs={{0,60},{1,61},{2,62},{3,63},{4,0},{5,1},{6,2},{7,3},{8,4},{9,5},{1... | collective-permute-start | bytes 786440 | tf_op jit(solution)/shard_map/ppermute | solution.py:337
  65.2 0.6 collective-permute-start.15
  65.8 1.8 %collective-permute-start.16 = (bf16[128,1024]{1,0:T(8,128)(2,1)S(1)}, bf16[128,1024]{1,0:T(8,128)(2,1)S(1)}, u32[]{:S(2)}, u32[]{:S(2)}) collective-permute-start(bf16[128,1024]{1,0:T(8,128)(2,1)S(1)} %get-tuple-element.97), channel_id=1, source_target_pairs={{0,61},{1,62},{2,63},{3,0},{4,1},{5,2},{6,3},{7,4},{8,5},{9,6},{10... | collective-permute-start | bytes 786440 | tf_op jit(solution)/shard_map/ppermute | solution.py:337
  67.5 2.9 %collective-permute-start.17 = (bf16[128,1024]{1,0:T(8,128)(2,1)S(1)}, bf16[128,1024]{1,0:T(8,128)(2,1)S(1)}, u32[]{:S(2)}, u32[]{:S(2)}) collective-permute-start(bf16[128,1024]{1,0:T(8,128)(2,1)S(1)} %get-tuple-element.98), channel_id=1, source_target_pairs={{0,63},{1,0},{2,1},{3,2},{4,3},{5,4},{6,5},{7,6},{8,7},{9,8},{10,9... | collective-permute-start | bytes 786440 | tf_op jit(solution)/shard_map/ppermute | solution.py:337
  71.1 25.5 %conditional.1 = (bf16[128,4096]{1,0:T(8,128)(2,1)}, f32[128,256]{1,0:T(8,128)S(1)}) conditional(s32[]{:T(128)} %bitcast.3, () %tuple.16, (s32[1,1]{1,0:T(1,128)}, f32[128,4096]{1,0:T(8,128)S(1)}, f32[8,4096]{1,0:T(8,128)S(1)}, bf16[640,4096]{1,0:T(8,128)(2,1)S(1)}, bf16[640,512]{1,0:T(8,128)(2,1)S(1)}, /*index=5*/f32[128,1280]{1,0:T(8,128)S(1)}, ...), branch_computations={%region_0.0_spmd, %region_1.0_spmd} | conditional | flops 256 | bytes 1179670 | solution.py:473
  71.1 4.3 %query_back.1 = (bf16[128,4096]{1,0:T(8,128)(2,1)}, f32[8,256]{1,0:T(8,128)S(1)}) custom-call(s32[1,1]{1,0:T(1,128)} %get-tuple-element.16.place_ref, f32[128,4096]{1,0:T(8,128)S(1)} %get-tuple-element.17.unit_ref, f32[8,4096]{1,0:T(8,128)S(1)} %get-tuple-element.18.norm_ref, bf16[640,4096]{1,0:T(8,128)(2,1)S(1)} %get-tuple-element.19.ds_ref, ...), custom_call_target="tpu_custom_call" | custom-call | tf_op jit(solution)/shard_map/cond/branch_1_fun/query_back/pallas_call | solution.py:451
  75.4 1.5 %collective-permute-start = (f32[8,256]{1,0:T(8,128)S(1)}, f32[8,256]{1,0:T(8,128)S(1)}, u32[]{:S(2)}, u32[]{:S(2)}) collective-permute-start(f32[8,256]{1,0:T(8,128)S(1)} %get-tuple-element.25), channel_id=1, source_target_pairs={{0,64},{64,0},{128,192},{192,128},{1,65},{65,1},{129,193},{193,129... | collective-permute-start | bytes 24584 | tf_op jit(solution)/shard_map/cond/branch_1_fun/ppermute | solution.py:333
  77.0 0.8 collective-permute-done
  77.8 0.1 broadcast_in_dim.0
  77.9 18.7 %all_to_all.7 = f32[128,1,256]{2,1,0:T(1,128)S(1)} all-to-all(f32[128,1,256]{2,1,0:T(1,128)S(1)} %broadcast_in_dim.0), channel_id=1, replica_groups={{0,1,2,3,4,5,6,7,8,9,10,11,12,13,14,15,16,17,18,19,20,21,22,23,24,25,26..., dimensions={0} | all-to-all | bytes 262144 | tf_op jit(solution)/shard_map/cond/branch_1_fun/all_to_all | solution.py:466
  96.6 0.0 collective-permute-done.14.rest_0_
  96.6 0.0 collective-permute-done.15.rest_1_
  96.6 0.0 collective-permute-done.16.rest_2_
  96.6 0.0 collective-permute-done.17.rest_3_
  96.7 1.8 %finish.1 = (bf16[128,512]{1,0:T(8,128)(2,1)}, bf16[128,512]{1,0:T(8,128)(2,1)}, f32[1,128]{1,0:T(1,128)}, f32[1,128]{1,0:T(1,128)}) custom-call(s32[1,1]{1,0:T(1,128)} %get-tuple-element.80.place_ref, f32[128,1024]{1,0:T(8,128)S(1)} %get-tuple-element.94.own_ref, bf16[128,1024]{1,0:T(8,128)(2,1)S(1)} %collective-permute-done.14.rest_0_, ...), custom_call_target="tpu_custom_call" | custom-call | tf_op jit(solution)/shard_map/finish/pallas_call | solution.py:476
  (3 shorter events, 0.0 us)
Async XLA Ops:
  0.6 45.2 %copy-start.7 = (f32[128]{0:T(128)S(1)}, f32[128]{0:T(128)}, u32[]{:S(2)}) copy-start(f32[128]{0:T(128)} %param.18) | copy-start | bytes 1540
  0.6 45.2 %copy-start.6 = (f32[128]{0:T(128)S(1)}, f32[128]{0:T(128)}, u32[]{:S(2)}) copy-start(f32[128]{0:T(128)} %param.19) | copy-start | bytes 1540
  2.6 5.5 %collective-permute-start.4 = (bf16[32,1024]{1,0:T(8,128)(2,1)}, bf16[32,1024]{1,0:T(8,128)(2,1)S(1)}, u32[]{:S(2)}, u32[]{:S(2)}) collective-permute-start(bf16[32,1024]{1,0:T(8,128)(2,1)} %get-tuple-element.74), channel_id=1, source_target_pairs={{0,64},{64,0},{128,192},{192,128},{1,65},{65,1},{129,193},{193,129... | collective-permute-start | bytes 196616 | tf_op jit(solution)/shard_map/ppermute | solution.py:333
  5.9 4.0 %collective-permute-start.5 = (bf16[32,1024]{1,0:T(8,128)(2,1)}, bf16[32,1024]{1,0:T(8,128)(2,1)S(1)}, u32[]{:S(2)}, u32[]{:S(2)}) collective-permute-start(bf16[32,1024]{1,0:T(8,128)(2,1)} %get-tuple-element.75), channel_id=1, source_target_pairs={{0,128},{64,192},{128,0},{192,64},{1,129},{65,193},{129,1},{193,65... | collective-permute-start | bytes 196616 | tf_op jit(solution)/shard_map/ppermute | solution.py:333
  5.9 5.4 %collective-permute-start.6 = (bf16[32,1024]{1,0:T(8,128)(2,1)}, bf16[32,1024]{1,0:T(8,128)(2,1)S(1)}, u32[]{:S(2)}, u32[]{:S(2)}) collective-permute-start(bf16[32,1024]{1,0:T(8,128)(2,1)} %get-tuple-element.76), channel_id=1, source_target_pairs={{0,192},{64,128},{128,64},{192,0},{1,193},{65,129},{129,65},{193,1... | collective-permute-start | bytes 196616 | tf_op jit(solution)/shard_map/ppermute | solution.py:333
  11.3 0.8 copy-start.4
  12.2 16.5 %collective-permute-start.7 = (bf16[136,1024]{1,0:T(8,128)(2,1)S(1)}, bf16[136,1024]{1,0:T(8,128)(2,1)S(1)}, u32[]{:S(2)}, u32[]{:S(2)}) collective-permute-start(bf16[136,1024]{1,0:T(8,128)(2,1)S(1)} %kv_join.1.rest_1_.rest_4_), channel_id=1, source_target_pairs={{0,1},{1,2},{2,3},{3,4},{4,5},{5,6},{6,7},{7,8},{8,9},{9,10},{10,1... | collective-permute-start | bytes 835592 | tf_op jit(solution)/shard_map/ppermute | solution.py:337
  13.2 1.2 %copy-start = (bf16[128,4096]{1,0:T(8,128)(2,1)S(1)}, bf16[128,4096]{1,0:T(8,128)(2,1)}, u32[]{:S(2)}) copy-start(bf16[128,4096]{1,0:T(8,128)(2,1)} %array_ref.2) | copy-start | bytes 3145732
  14.5 0.7 copy-start.5
  16.5 5.6 %collective-permute-start.1 = (bf16[32,4096]{1,0:T(8,128)(2,1)S(1)}, bf16[32,4096]{1,0:T(8,128)(2,1)S(1)}, u32[]{:S(2)}, u32[]{:S(2)}) collective-permute-start(bf16[32,4096]{1,0:T(8,128)(2,1)S(1)} %get-tuple-element.69), channel_id=1, source_target_pairs={{0,64},{64,0},{128,192},{192,128},{1,65},{65,1},{129,193},{193,129... | collective-permute-start | bytes 786440 | tf_op jit(solution)/shard_map/ppermute | solution.py:333
  17.1 18.2 %collective-permute-start.10 = (bf16[136,1024]{1,0:T(8,128)(2,1)S(1)}, bf16[136,1024]{1,0:T(8,128)(2,1)S(1)}, u32[]{:S(2)}, u32[]{:S(2)}) collective-permute-start(bf16[136,1024]{1,0:T(8,128)(2,1)S(1)} %kv_join.1.rest_1_.rest_4_), channel_id=1, source_target_pairs={{0,4},{1,5},{2,6},{3,7},{4,8},{5,9},{6,10},{7,11},{8,12},{9,13},{1... | collective-permute-start | bytes 835592 | tf_op jit(solution)/shard_map/ppermute | solution.py:337
  20.1 11.2 %collective-permute-start.2 = (bf16[32,4096]{1,0:T(8,128)(2,1)S(1)}, bf16[32,4096]{1,0:T(8,128)(2,1)S(1)}, u32[]{:S(2)}, u32[]{:S(2)}) collective-permute-start(bf16[32,4096]{1,0:T(8,128)(2,1)S(1)} %get-tuple-element.70), channel_id=1, source_target_pairs={{0,128},{64,192},{128,0},{192,64},{1,129},{65,193},{129,1},{193,65... | collective-permute-start | bytes 786440 | tf_op jit(solution)/shard_map/ppermute | solution.py:333
  20.4 13.6 %collective-permute-start.3 = (bf16[32,4096]{1,0:T(8,128)(2,1)S(1)}, bf16[32,4096]{1,0:T(8,128)(2,1)S(1)}, u32[]{:S(2)}, u32[]{:S(2)}) collective-permute-start(bf16[32,4096]{1,0:T(8,128)(2,1)S(1)} %get-tuple-element.71), channel_id=1, source_target_pairs={{0,192},{64,128},{128,64},{192,0},{1,193},{65,129},{129,65},{193,1... | collective-permute-start | bytes 786440 | tf_op jit(solution)/shard_map/ppermute | solution.py:333
  22.1 18.4 %collective-permute-start.8 = (bf16[136,1024]{1,0:T(8,128)(2,1)S(1)}, bf16[136,1024]{1,0:T(8,128)(2,1)S(1)}, u32[]{:S(2)}, u32[]{:S(2)}) collective-permute-start(bf16[136,1024]{1,0:T(8,128)(2,1)S(1)} %kv_join.1.rest_1_.rest_4_), channel_id=1, source_target_pairs={{0,2},{1,3},{2,4},{3,5},{4,6},{5,7},{6,8},{7,9},{8,10},{9,11},{10,... | collective-permute-start | bytes 835592 | tf_op jit(solution)/shard_map/ppermute | solution.py:337
  28.7 17.1 %collective-permute-start.9 = (bf16[136,1024]{1,0:T(8,128)(2,1)S(1)}, bf16[136,1024]{1,0:T(8,128)(2,1)S(1)}, u32[]{:S(2)}, u32[]{:S(2)}) collective-permute-start(bf16[136,1024]{1,0:T(8,128)(2,1)S(1)} %collective-permute-done.7.rest_2_.rest_5_), channel_id=1, source_target_pairs={{0,2},{1,3},{2,4},{3,5},{4,6},{5,7},{6,8},{7,9},{8,10},{9,11},{10,... | collective-permute-start | bytes 835592 | tf_op jit(solution)/shard_map/ppermute | solution.py:337
  28.7 1.2 %copy-start.1 = (bf16[128,4096]{1,0:T(8,128)(2,1)S(1)}, bf16[128,4096]{1,0:T(8,128)(2,1)}, u32[]{:S(2)}) copy-start(bf16[128,4096]{1,0:T(8,128)(2,1)} %array_ref.3) | copy-start | bytes 3145732
  31.3 25.1 %collective-permute-start.11 = (bf16[32,4096]{1,0:T(8,128)(2,1)S(1)}, bf16[32,4096]{1,0:T(8,128)(2,1)S(1)}, u32[]{:S(2)}, u32[]{:S(2)}) collective-permute-start(bf16[32,4096]{1,0:T(8,128)(2,1)S(1)} %get-tuple-element.83), channel_id=1, source_target_pairs={{0,64},{64,0},{128,192},{192,128},{1,65},{65,1},{129,193},{193,129... | collective-permute-start | bytes 786440 | tf_op jit(solution)/shard_map/ppermute | solution.py:333
  34.0 22.4 %collective-permute-start.12 = (bf16[32,4096]{1,0:T(8,128)(2,1)S(1)}, bf16[32,4096]{1,0:T(8,128)(2,1)S(1)}, u32[]{:S(2)}, u32[]{:S(2)}) collective-permute-start(bf16[32,4096]{1,0:T(8,128)(2,1)S(1)} %get-tuple-element.84), channel_id=1, source_target_pairs={{0,128},{64,192},{128,0},{192,64},{1,129},{65,193},{129,1},{193,65... | collective-permute-start | bytes 786440 | tf_op jit(solution)/shard_map/ppermute | solution.py:333
  35.3 21.1 %collective-permute-start.13 = (bf16[32,4096]{1,0:T(8,128)(2,1)S(1)}, bf16[32,4096]{1,0:T(8,128)(2,1)S(1)}, u32[]{:S(2)}, u32[]{:S(2)}) collective-permute-start(bf16[32,4096]{1,0:T(8,128)(2,1)S(1)} %get-tuple-element.85), channel_id=1, source_target_pairs={{0,192},{64,128},{128,64},{192,0},{1,193},{65,129},{129,65},{193,1... | collective-permute-start | bytes 786440 | tf_op jit(solution)/shard_map/ppermute | solution.py:333
  37.0 1.1 %copy-start.2 = (f32[640,256]{1,0:T(8,128)S(1)}, f32[640,256]{1,0:T(8,128)}, u32[]{:S(2)}) copy-start(f32[640,256]{1,0:T(8,128)} %constant.11.clone.refs_4_) | copy-start | bytes 1966084
  38.1 1.1 %copy-start.3 = (f32[128,1280]{1,0:T(8,128)S(1)}, f32[128,1280]{1,0:T(8,128)}, u32[]{:S(2)}) copy-start(f32[128,1280]{1,0:T(8,128)} %constant.12.clone.refs_5_) | copy-start | bytes 1966084
  63.3 33.3 %collective-permute-start.14 = (bf16[128,1024]{1,0:T(8,128)(2,1)}, bf16[128,1024]{1,0:T(8,128)(2,1)S(1)}, u32[]{:S(2)}, u32[]{:S(2)}) collective-permute-start(bf16[128,1024]{1,0:T(8,128)(2,1)} %get-tuple-element.95), channel_id=1, source_target_pairs={{0,60},{1,61},{2,62},{3,63},{4,0},{5,1},{6,2},{7,3},{8,4},{9,5},{1... | collective-permute-start | bytes 786440 | tf_op jit(solution)/shard_map/ppermute | solution.py:337
  65.2 31.4 %collective-permute-start.15 = (bf16[128,1024]{1,0:T(8,128)(2,1)S(1)}, bf16[128,1024]{1,0:T(8,128)(2,1)S(1)}, u32[]{:S(2)}, u32[]{:S(2)}) collective-permute-start(bf16[128,1024]{1,0:T(8,128)(2,1)S(1)} %get-tuple-element.96), channel_id=1, source_target_pairs={{0,62},{1,63},{2,0},{3,1},{4,2},{5,3},{6,4},{7,5},{8,6},{9,7},{10,... | collective-permute-start | bytes 786440 | tf_op jit(solution)/shard_map/ppermute | solution.py:337
  65.8 30.9 %collective-permute-start.16 = (bf16[128,1024]{1,0:T(8,128)(2,1)S(1)}, bf16[128,1024]{1,0:T(8,128)(2,1)S(1)}, u32[]{:S(2)}, u32[]{:S(2)}) collective-permute-start(bf16[128,1024]{1,0:T(8,128)(2,1)S(1)} %get-tuple-element.97), channel_id=1, source_target_pairs={{0,61},{1,62},{2,63},{3,0},{4,1},{5,2},{6,3},{7,4},{8,5},{9,6},{10... | collective-permute-start | bytes 786440 | tf_op jit(solution)/shard_map/ppermute | solution.py:337
  67.5 29.1 %collective-permute-start.17 = (bf16[128,1024]{1,0:T(8,128)(2,1)S(1)}, bf16[128,1024]{1,0:T(8,128)(2,1)S(1)}, u32[]{:S(2)}, u32[]{:S(2)}) collective-permute-start(bf16[128,1024]{1,0:T(8,128)(2,1)S(1)} %get-tuple-element.98), channel_id=1, source_target_pairs={{0,63},{1,0},{2,1},{3,2},{4,3},{5,4},{6,5},{7,6},{8,7},{9,8},{10,9... | collective-permute-start | bytes 786440 | tf_op jit(solution)/shard_map/ppermute | solution.py:337
  75.4 2.4 %collective-permute-start = (f32[8,256]{1,0:T(8,128)S(1)}, f32[8,256]{1,0:T(8,128)S(1)}, u32[]{:S(2)}, u32[]{:S(2)}) collective-permute-start(f32[8,256]{1,0:T(8,128)S(1)} %get-tuple-element.25), channel_id=1, source_target_pairs={{0,64},{64,0},{128,192},{192,128},{1,65},{65,1},{129,193},{193,129... | collective-permute-start | bytes 24584 | tf_op jit(solution)/shard_map/cond/branch_1_fun/ppermute | solution.py:333
